TPU v7x, 128 devices: a whole 4x4x4 slice. The times are simulated.
128 devices in a mesh: rep: 8 (over y_lo, x), fsdp: 16 (over y_hi, z, core).
Axes of the slice: x: 4, y: 4 (y_hi: 2, y_lo: 2; y = y_hi * 2 + y_lo), z: 4, core: 2. Of those that a mesh axis runs over, the one named last changes fastest.
Arguments:
- inputs: bfloat16 [8, 8192, 8192], P('rep', 'fsdp'), may hold values from -6 to 6
- grad_keys: bfloat16 [8, 8192, 1024], P('rep', 'fsdp'), may hold values from -1.5 to 1.5
- local_weights: bfloat16 [8, 8192, 1024], P('rep', 'fsdp'), may hold values from -6 to 6
- feedback: bfloat16 [8, 8192, 1024], P('rep', 'fsdp'), may hold values from -4 to 4
- base: float32 [8192, 1024], P('fsdp', 'rep'), may hold values from -6 to 6
- momentum: float32 [8192, 1024], P('fsdp', 'rep'), may hold values from -4 to 4
- warm_start: float32 [1024, 64], replicated, may hold values from -6 to 6
Outputs:
- grad_inputs: bfloat16 [8, 8192, 8192], P('rep', 'fsdp')
- feedback_out: float32 [8, 8192, 1024], P('rep', 'fsdp')
- base_out: float32 [8192, 1024], P('fsdp', 'rep')
- momentum_out: float32 [8192, 1024], P('fsdp', 'rep')
- factor_out: float32 [1024, 64], replicated
All inputs are finite; a program needn't handle non-finite values.
Results may differ from a plain program's by a relative error of at most 0.0018.
Values may be sent and summed in bfloat16 or wider, within the bound.
No kernel may reach another device: no remote copies, remote signals or barrier semaphores. Data moves between devices by JAX's collectives and lax.ppermute only.
A program may use at most 128 MiB of HBM per device.

v0:
```python
import math

import jax
import jax.numpy as jnp
from jax import lax
from jax.sharding import PartitionSpec as P

D = 8192
ROUNDS = 2


outer_rate = 0.7
momentum_keep = 0.9
inner_rate = 0.5


def orthonormal_part(matrix, lower_factor):
    return lax.linalg.triangular_solve(
        lower_factor, matrix, left_side=False, lower=True, transpose_a=True
    )


def per_device(inputs, grad_keys, local_weights, feedback, base, momentum, warm_start):
    highest = lax.Precision.HIGHEST
    inv_root = 1.0 / math.sqrt(D)
    tokens_in = inputs[0]
    cotangent = grad_keys[0]
    weights = local_weights[0]
    replicas = lax.axis_size("rep")
    product = lax.dot_general(
        cotangent,
        lax.all_gather(local_weights, "fsdp", axis=1, tiled=True)[0],
        (((1,), (1,)), ((), ())),
        preferred_element_type=jnp.float32,
    )
    grad_inputs = (product * inv_root).astype(jnp.bfloat16)[None]
    product = lax.dot_general(
        tokens_in, cotangent, (((0,), (0,)), ((), ())), preferred_element_type=jnp.float32
    )
    inner_grad = lax.psum_scatter(
        (product * inv_root).astype(jnp.bfloat16), "fsdp", scatter_dimension=0, tiled=True
    ).astype(jnp.float32)
    full_base = lax.all_gather(base, "rep", axis=1, tiled=True)
    pseudo = (
        full_base
        - weights.astype(jnp.float32)
        + inner_rate * inner_grad
        + feedback[0].astype(jnp.float32)
    )
    factor = warm_start
    orthonormal = None
    for repeat in range(ROUNDS):
        left_part = lax.psum(jnp.dot(pseudo, factor, precision=highest), "rep") / replicas
        gram_matrix = lax.psum(jnp.dot(left_part.T, left_part, precision=highest), "fsdp")
        lower_factor = jnp.linalg.cholesky(gram_matrix)
        orthonormal = orthonormal_part(left_part, lower_factor)
        factor = (
            lax.psum(jnp.dot(pseudo.T, orthonormal, precision=highest), ("rep", "fsdp")) / replicas
        )
    approx = jnp.dot(orthonormal, factor.T, precision=highest)
    feedback_out = (pseudo - approx)[None]
    block_width = base.shape[1]
    column_block = lax.dynamic_slice_in_dim(
        approx, lax.axis_index("rep") * block_width, block_width, 1
    )
    momentum_out = momentum_keep * momentum + column_block
    base_out = base - outer_rate * (column_block + momentum_keep * momentum_out)
    return (grad_inputs, feedback_out, base_out, momentum_out, factor)


def solution(mesh):
    return jax.shard_map(
        per_device,
        mesh=mesh,
        in_specs=(
            P("rep", "fsdp", None),
            P("rep", "fsdp", None),
            P("rep", "fsdp", None),
            P("rep", "fsdp", None),
            P("fsdp", "rep"),
            P("fsdp", "rep"),
            P(),
        ),
        out_specs=(
            P("rep", "fsdp", None),
            P("rep", "fsdp", None),
            P("fsdp", "rep"),
            P("fsdp", "rep"),
            P(),
        ),
        check_vma=False,
    )
```

profile of v0, /device:TPU:1, one launch (start us, length us, event | category | flops | bytes accessed | tf_op | source)
XLA Modules:
  0.0 873.1 jit_solution(14288912189052520668)
XLA Ops:
  9.2 15.9 %multiply_convert_fusion = bf16[8192,1024]{1,0:T(8,128)(2,1)} fusion(bf16[1,512,8192]{2,1,0:T(8,128)(2,1)} %param.10, bf16[1,512,1024]{2,1,0:T(8,128)(2,1)S(1)} %copy-done), kind=kOutput, calls=%fused_computation | convolution fusion | flops 8606711808 | bytes 26214400 | tf_op jit(solution)/shard_map/dot_general | solution.py:37
  25.2 29.3 %all-gather.5.cloned.1.call-done = f32[512,1024]{1,0:T(8,128)} async-done(((f32[512,128]{1,0:T(8,128)}), f32[512,1024]{1,0:T(8,128)}) %all-gather.5.cloned.1.call-update) | async-done | bytes 2097168 | tf_op jit(solution)/shard_map/all_gather | solution.py:43
  54.5 119.6 %reduce-scatter.2.cloned.1.call-done = bf16[512,1024]{1,0:T(8,128)(2,1)} async-done(((bf16[8192,1024]{1,0:T(8,128)(2,1)}), bf16[512,1024]{1,0:T(8,128)(2,1)}) %reduce-scatter.2.cloned.1.call-update) | async-done | bytes 1048592 | tf_op jit(solution)/shard_map/reduce_scatter | solution.py:40
  174.2 3.2 convert_add_fusion
  177.4 2.8 fusion.37
  180.3 66.9 %all-reduce.5.cloned.1.call-done = f32[512,64]{0,1:T(8,128)} async-done(((f32[512,64]{0,1:T(8,128)}), f32[512,64]{0,1:T(8,128)}) %all-reduce.5.cloned.1.call-update) | async-done | bytes 131088 | tf_op jit(solution)/shard_map/psum | solution.py:53
  247.2 1.2 fusion.18
  248.5 64.5 %psum.43 = f32[64,64]{0,1:T(8,128)S(1)} all-reduce(f32[64,64]{0,1:T(8,128)S(1)} %fusion.18), channel_id=1, replica_groups=mesh['rep'=8,'fsdp'=16] {'fsdp'}, use_global_device_ids=true, to_apply=%region_2.0 | all-reduce | flops 4096 | bytes 32768 | tf_op jit(solution)/shard_map/psum | solution.py:54
  313.1 5.8 cholesky.44
  320.3 4.9 custom-call.6
  325.2 1.2 convolution_bitcast_fusion.1
  326.4 2.2 fusion.38
  328.8 143.8 %all-reduce.7.cloned.1.call-done = f32[1024,64]{0,1:T(8,128)} async-done(((f32[1024,64]{0,1:T(8,128)}), f32[1024,64]{0,1:T(8,128)}) %all-reduce.7.cloned.1.call-update) | async-done | bytes 262160 | tf_op jit(solution)/shard_map/psum | solution.py:58
  472.6 3.8 fusion.11
  476.4 65.9 %all-reduce.9.cloned.1.call-done = f32[512,64]{0,1:T(8,128)} async-done(((f32[512,64]{0,1:T(8,128)}), f32[512,64]{0,1:T(8,128)}) %all-reduce.9.cloned.1.call-update) | async-done | bytes 131088 | tf_op jit(solution)/shard_map/psum | solution.py:53
  542.4 1.2 fusion.15
  543.6 64.5 %psum.46 = f32[64,64]{0,1:T(8,128)S(1)} all-reduce(f32[64,64]{0,1:T(8,128)S(1)} %fusion.15), channel_id=1, replica_groups=mesh['rep'=8,'fsdp'=16] {'fsdp'}, use_global_device_ids=true, to_apply=%region_7.10 | all-reduce | flops 4096 | bytes 32768 | tf_op jit(solution)/shard_map/psum | solution.py:54
  608.2 5.8 cholesky.55
  615.4 4.9 custom-call.7
  621.5 2.2 fusion.39
  624.3 206.4 %all-reduce.11.cloned.1.call-done = f32[1024,64]{0,1:T(8,128)} async-done(((f32[1024,64]{0,1:T(8,128)}), f32[1024,64]{0,1:T(8,128)}) %all-reduce.11.cloned.1.call-update) | async-done | bytes 262160 | tf_op jit(solution)/shard_map/psum | solution.py:58
  831.7 1.8 fusion.40
  834.5 1.7 subtract_bitcast_fusion
  836.2 29.8 %fusion.4 = bf16[1,512,8192]{2,1,0:T(8,128)(2,1)} fusion(bf16[1,8192,1024]{2,1,0:T(8,128)(2,1)} %all-gather.3.cloned.1.call-done, bf16[1,512,1024]{2,1,0:T(8,128)(2,1)S(1)} %copy-done), kind=kOutput, calls=%fused_computation.4 | convolution fusion | flops 8598323200 | bytes 26214400 | tf_op jit(solution)/shard_map/dot_general | solution.py:30
  (38 shorter events, 8.2 us)
Async XLA Ops:
  8.0 1.2 copy-start
  8.0 46.5 %all-gather.5.cloned.1.call-start = ((), (), s32[]{:S(2)}) async-start(), calls=%async_computation.2 | async-start | bytes 2359296 | tf_op jit(solution)/shard_map/all_gather | solution.py:43
  8.7 165.4 %reduce-scatter.2.cloned.1.call-start = ((), (), s32[]{:S(2)}) async-start(), calls=%async_computation.3 | async-start | bytes 17825792 | tf_op jit(solution)/shard_map/reduce_scatter | solution.py:40
  25.2 152.2 %copy-start.3 = (f32[1024,64]{0,1:T(8,128)S(1)}, f32[1024,64]{0,1:T(8,128)}, u32[]{:S(2)}) copy-start(f32[1024,64]{0,1:T(8,128)} %param.16) | copy-start | bytes 786436
  25.2 222.1 %all-reduce.5.cloned.1.call-start = ((), (), s32[]{:S(2)}) async-start(), calls=%async_computation.4 | async-start | bytes 262144 | tf_op jit(solution)/shard_map/psum | solution.py:53
  180.2 292.4 %all-reduce.7.cloned.1.call-start = ((), (), s32[]{:S(2)}) async-start(), calls=%async_computation.5 | async-start | bytes 524288 | tf_op jit(solution)/shard_map/psum | solution.py:58
  328.6 213.7 %all-reduce.9.cloned.1.call-start = ((), (), s32[]{:S(2)}) async-start(), calls=%async_computation.6 | async-start | bytes 262144 | tf_op jit(solution)/shard_map/psum | solution.py:53
  476.4 354.3 %all-reduce.11.cloned.1.call-start = ((), (), s32[]{:S(2)}) async-start(), calls=%async_computation.7 | async-start | bytes 524288 | tf_op jit(solution)/shard_map/psum | solution.py:58
  623.7 209.9 %copy-start.1 = (f32[512,128]{1,0:T(8,128)S(1)}, f32[512,128]{1,0:T(8,128)}, u32[]{:S(2)}) copy-start(f32[512,128]{1,0:T(8,128)} %param.14) | copy-start | bytes 786436
  623.7 212.5 %all-gather.3.cloned.1.call-start = ((), (), s32[]{:S(2)}) async-start(), calls=%async_computation.1 | async-start | bytes 17825792 | tf_op jit(solution)/shard_map/all_gather | solution.py:32
  830.7 2.9 copy-start.4
  831.7 1.9 copy-start.2
Sparse Core Ops, SparseCore 0:
  10.4 44.0 all-gather.4
  180.4 66.8 all-reduce.4
  328.7 143.8 all-reduce.6
  476.5 65.7 all-reduce.8
  623.9 206.8 all-reduce.10
Sparse Core Ops, SparseCore 1:
  25.3 148.8 reduce-scatter.1
  626.7 111.9 all-gather.2
where the time goes:
time: 874 us; the launch traced here: 873 us
  waiting for transfers between devices  633 us (72%)
  blocking collectives  129 us (15%)
  matrix products  63.4 us (7%)
  other arithmetic  31 us (4%)
  between operations  15.4 us (2%)
    psum x2, waiting for transfers between devices, per_device(): lax.psum(jnp.dot(pseudo.T, orthonormal, precision=highest), ('rep', 'fsdp'))  350 us
    psum x2, waiting for transfers between devices, per_device(): lax.psum(jnp.dot(pseudo, factor, precision=highest), 'rep') / replicas  133 us
    psum x2, blocking collectives, per_device(): lax.psum(jnp.dot(left_part.T, left_part, precision=highest), 'fsdp')  129 us
    reduce_scatter x1, waiting for transfers between devices, per_device(): lax.psum_scatter((product * inv_root).astype(jnp.bfloat16), 'fsdp', scatt...  120 us
    dot_general x1, matrix products, per_device(): lax.dot_general(cotangent, lax.all_gather(local_weights, 'fsdp', axis=1,...  29.8 us
    all_gather x1, waiting for transfers between devices, per_device(): full_base = lax.all_gather(base, 'rep', axis=1, tiled=True)  29.3 us
  transfers between devices with their start and end apart: 7, of which 6 were waited for; matrix products, arithmetic and copies ran while one was open for 2% of the time, Pallas kernels for 0%

commit v1 on v0

v1 whole, which is shorter than its diff:
```python
import math

import jax
import jax.numpy as jnp
from jax import lax
from jax.sharding import Mesh, PartitionSpec as P

D = 8192
ROUNDS = 2

outer_rate = 0.7
momentum_keep = 0.9
inner_rate = 0.5

REP = ("yl", "x")
FSDP = ("yh", "z", "c")
CHIPS = ("yh", "z")
ALL = REP + FSDP
f32 = jnp.float32
bf16 = jnp.bfloat16


def dot(a, b, dims=((1,), (0,))):
    return lax.dot_general(
        a, b, (dims, ((), ())), precision=lax.Precision.HIGHEST, preferred_element_type=f32
    )


def scatter_sum(value, axes, parts):
    got = lax.all_to_all(value, axes, 0, 0, tiled=True)
    return got.reshape(parts, -1, value.shape[1]).astype(f32).sum(0)


def gather_rows(value, axes, parts):
    rows, width = value.shape
    sent = jnp.broadcast_to(value[None], (parts, rows, width)).reshape(parts * rows, width)
    return lax.all_to_all(sent, axes, 0, 0, tiled=True)


def orthonormal_part(matrix, lower_factor):
    return lax.linalg.triangular_solve(
        lower_factor, matrix, left_side=False, lower=True, transpose_a=True
    )


def per_device(inputs, grad_keys, local_weights, feedback, base, momentum, warm_start):
    inv_root = 1.0 / math.sqrt(D)
    tokens_in = inputs[0]
    cotangent = grad_keys[0]
    weights = local_weights[0]
    rep_size, fsdp_size, chip_size = lax.axis_size(REP), lax.axis_size(FSDP), lax.axis_size(CHIPS)
    everyone = rep_size * fsdp_size
    core = lax.axis_index("c")
    rows, width = weights.shape

    product = lax.dot_general(
        tokens_in, cotangent, (((0,), (0,)), ((), ())), preferred_element_type=f32
    )
    term = (product * inv_root).astype(bf16).reshape(chip_size, 2, rows, width)
    away = lax.dynamic_index_in_dim(term, 1 - core, 1, keepdims=False)
    kept = lax.dynamic_index_in_dim(term, core, 1, keepdims=False)
    came = lax.ppermute(away, "c", [(0, 1), (1, 0)])
    pair = (kept.astype(f32) + came.astype(f32)).astype(bf16).reshape(chip_size * rows, width)
    inner_grad = scatter_sum(pair, CHIPS, chip_size)

    full_base = lax.all_gather(base, REP, axis=1, tiled=True)
    drift = feedback[0].astype(f32) - weights.astype(f32)
    part_rows = rows // rep_size
    my_rep = lax.axis_index(REP)
    base_part = lax.dynamic_slice_in_dim(full_base, my_rep * part_rows, part_rows, 0)
    early_mean = base_part + scatter_sum(drift, REP, rep_size) / rep_size
    pseudo_mean = early_mean + (inner_rate / rep_size) * scatter_sum(
        inner_grad.astype(bf16), REP, rep_size
    )
    pseudo = full_base + drift + inner_rate * inner_grad

    factor = warm_start
    rank = factor.shape[1]
    for repeat in range(ROUNDS):
        left_part = dot(pseudo_mean, factor)
        raised = dot(pseudo_mean, left_part, ((0,), (0,)))
        gram_part = dot(left_part, left_part, ((0,), (0,)))
        packed = jnp.concatenate(
            [raised, jnp.tile(gram_part, (raised.shape[0] // rank, 1))], axis=1
        )
        summed = gather_rows(scatter_sum(packed, ALL, everyone), ALL, everyone)
        lower_factor = jnp.linalg.cholesky(summed[:rank, rank:])
        factor = orthonormal_part(summed[:, :rank], lower_factor)
    left = gather_rows(left_part, REP, rep_size)
    orthonormal = orthonormal_part(left, lower_factor)

    approx = dot(orthonormal, factor, ((1,), (1,)))
    feedback_out = (pseudo - approx)[None]
    block_width = base.shape[1]
    column_block = lax.dynamic_slice_in_dim(approx, my_rep * block_width, block_width, 1)
    momentum_out = momentum_keep * momentum + column_block
    base_out = base - outer_rate * (column_block + momentum_keep * momentum_out)

    every_row = lax.all_gather(local_weights, FSDP, axis=1, tiled=True)[0]
    product = lax.dot_general(
        cotangent, every_row, (((1,), (1,)), ((), ())), preferred_element_type=f32
    )
    grad_inputs = (product * inv_root).astype(bf16)[None]
    return (grad_inputs, feedback_out, base_out, momentum_out, factor)


def solution(mesh):
    fine = Mesh(mesh.devices.reshape(2, 4, 2, 4, 2), ALL)
    return jax.shard_map(
        per_device,
        mesh=fine,
        in_specs=(
            P(REP, FSDP, None),
            P(REP, FSDP, None),
            P(REP, FSDP, None),
            P(REP, FSDP, None),
            P(FSDP, REP),
            P(FSDP, REP),
            P(),
        ),
        out_specs=(
            P(REP, FSDP, None),
            P(REP, FSDP, None),
            P(FSDP, REP),
            P(FSDP, REP),
            P(),
        ),
        check_vma=False,
    )
```

time: 874 us -> 417 us (0.48)
  waiting for transfers between devices: 633 us -> 186 us
  blocking collectives: 129 us -> 50.3 us
  starting transfers between devices: 0.47 us -> 35.9 us
  other arithmetic: 31 us -> 61.5 us
  local copies, waits for them, and re-layouts: 0.61 us -> 12 us
    psum x4 -> x0, waiting for transfers between devices: 483 us -> none  [the longest x2 350 us: per_device(): lax.psum(jnp.dot(pseudo.T, orthonormal, precision=highest), ('rep', 'fsdp'))]
    all_to_all x0 -> x6, waiting for transfers between devices: none -> 172 us  [the longest x4 156 us: scatter_sum(): got = lax.all_to_all(value, axes, 0, 0, tiled=True)]
    psum x2 -> x0, blocking collectives: 129 us -> none  [per_device(): lax.psum(jnp.dot(left_part.T, left_part, precision=highest), 'fsdp')]
    reduce_scatter x1 -> x0, waiting for transfers between devices: 120 us -> none  [per_device(): lax.psum_scatter((product * inv_root).astype(jnp.bfloat16), 'fsdp', scatt...]
    all_to_all x0 -> x2, blocking collectives: none -> 50.3 us  [the longest x1 27.9 us: gather_rows(): return lax.all_to_all(sent, axes, 0, 0, tiled=True)]
    all_to_all x0 -> x6, starting transfers between devices: none -> 34.4 us  [the longest x4 24.7 us: scatter_sum(): got = lax.all_to_all(value, axes, 0, 0, tiled=True)]
    all_gather x2, waiting for transfers between devices: 29.3 us -> 0.01 us  [the longest x1 0.01 us: per_device(): full_base = lax.all_gather(base, REP, axis=1, tiled=True)]
    ppermute x0 -> x1, waiting for transfers between devices: none -> 13.1 us  [per_device(): came = lax.ppermute(away, 'c', [(0, 1), (1, 0)])]
  transfers between devices with their start and end apart: 7 -> 9, of which waited for: 6 -> 7; matrix products, arithmetic and copies ran while one was open for 2% -> 24% of each run, Pallas kernels for 0% -> 0%
where the time goes in v1:
time: 417 us; the launch traced here: 416 us
  waiting for transfers between devices  186 us (45%)
  other arithmetic  61.5 us (15%)
  matrix products  55.5 us (13%)
  blocking collectives  50.3 us (12%)
  starting transfers between devices  35.9 us (9%)
  between operations  14.3 us (3%)
  local copies, waits for them, and re-layouts  12 us (3%)
    all_to_all x4, waiting for transfers between devices, scatter_sum(): got = lax.all_to_all(value, axes, 0, 0, tiled=True)  156 us
    dot_general x1, matrix products, per_device(): lax.dot_general(cotangent, every_row, (((1,), (1,)), ((), ())), preferred...  29.8 us
    all_to_all x1, blocking collectives, gather_rows(): return lax.all_to_all(sent, axes, 0, 0, tiled=True)  27.9 us
    all_to_all x4, starting transfers between devices, scatter_sum(): got = lax.all_to_all(value, axes, 0, 0, tiled=True)  24.7 us
    all_to_all x1, blocking collectives, scatter_sum(): got = lax.all_to_all(value, axes, 0, 0, tiled=True)  22.4 us
    all_to_all x2, waiting for transfers between devices, gather_rows(): return lax.all_to_all(sent, axes, 0, 0, tiled=True)  16 us
    dot_general x1, matrix products, per_device(): lax.dot_general(tokens_in, cotangent, (((0,), (0,)), ((), ())), preferred...  15.9 us
    ppermute x1, waiting for transfers between devices, per_device(): came = lax.ppermute(away, 'c', [(0, 1), (1, 0)])  13.1 us
  transfers between devices with their start and end apart: 9, of which 7 were waited for; matrix products, arithmetic and copies ran while one was open for 24% of the time, Pallas kernels for 0%

profile of v1, /device:TPU:1, one launch (start us, length us, event | category | flops | bytes accessed | tf_op | source)
XLA Modules:
  0.0 415.9 jit_solution(4326234299321950177)
XLA Ops:
  8.7 15.9 %multiply_convert_fusion = bf16[8192,1024]{1,0:T(8,128)(2,1)} fusion(bf16[1,512,8192]{2,1,0:T(8,128)(2,1)} %param.10, bf16[1,512,1024]{2,1,0:T(8,128)(2,1)S(1)} %copy-done), kind=kOutput, calls=%fused_computation | convolution fusion | flops 8606711808 | bytes 26214400 | tf_op jit(solution)/shard_map/dot_general | solution.py:56
  24.6 7.8 %dynamic-slice_bitcast_fusion = bf16[8,512,1024]{2,1,0:T(8,128)(2,1)} fusion(bf16[8,2,512,1024]{3,2,1,0:T(8,128)(2,1)} %bitcast.85, s32[]{:T(128)S(6)} %select_n.17), kind=kLoop, calls=%fused_computation.9 | loop fusion | bytes 16777220 | tf_op jit(solution)/shard_map/jit(dynamic_index_in_dim)/squeeze | solution.py:60
  33.8 13.1 %collective-permute-done = bf16[8,512,1024]{2,1,0:T(8,128)(2,1)} collective-permute-done((bf16[8,512,1024]{2,1,0:T(8,128)(2,1)}, bf16[8,512,1024]{2,1,0:T(8,128)(2,1)}, u32[]{:S(2)}, u32[]{:S(2)}) %collective-permute-start) | collective-permute-done | bytes 8388640 | tf_op jit(solution)/shard_map/ppermute | solution.py:62
  46.9 10.7 %fusion = bf16[8,512,1024]{2,1,0:T(8,128)(2,1)} fusion(bf16[8,512,1024]{2,1,0:T(8,128)(2,1)} %collective-permute-done, bf16[8,2,512,1024]{3,2,1,0:T(8,128)(2,1)} %bitcast.86, s32[]{:T(128)S(6)} %select_n.16), kind=kLoop, calls=%fused_computation.2 | loop fusion | flops 16777216 | bytes 25165828 | tf_op jit(solution)/shard_map/convert_element_type | solution.py:63
  57.6 8.0 %all-to-all-start = ((bf16[8,512,1024]{2,1,0:T(8,128)(2,1)}), bf16[8,512,1024]{2,1,0:T(8,128)(2,1)}, u32[]{:S(2)}, u32[]{:S(2)}) async-start(bf16[8,512,1024]{2,1,0:T(8,128)(2,1)} %fusion), calls=%async_computation | async-start | bytes 16777216 | tf_op jit(solution)/shard_map/all_to_all | solution.py:30
  67.3 108.8 %all-to-all-done = bf16[8,512,1024]{2,1,0:T(8,128)(2,1)} async-done(((bf16[8,512,1024]{2,1,0:T(8,128)(2,1)}), bf16[8,512,1024]{2,1,0:T(8,128)(2,1)}, u32[]{:S(2)}, u32[]{:S(2)}) %all-to-all-start) | async-done | bytes 8388640 | tf_op jit(solution)/shard_map/all_to_all | solution.py:30
  176.1 4.4 %all-to-all-start.1 = ((f32[8,64,1024]{2,1,0:T(8,128)}), f32[8,64,1024]{2,1,0:T(8,128)}, u32[]{:S(2)}, u32[]{:S(2)}) async-start(f32[8,64,1024]{2,1,0:T(8,128)} %bitcast.87), calls=%async_computation.1 | async-start | bytes 4194304 | tf_op jit(solution)/shard_map/all_to_all | solution.py:30
  180.5 5.6 %convert_reduce_fusion = f32[512,1024]{1,0:T(8,128)S(1)} fusion(bf16[8,512,1024]{2,1,0:T(8,128)(2,1)} %all-to-all-done), kind=kLoop, calls=%fused_computation.5 | loop fusion | flops 7864320 | bytes 10485760 | tf_op jit(solution)/shard_map/reduce_sum | solution.py:31
  187.2 20.4 %all-to-all-done.1 = f32[8,64,1024]{2,1,0:T(8,128)} async-done(((f32[8,64,1024]{2,1,0:T(8,128)}), f32[8,64,1024]{2,1,0:T(8,128)}, u32[]{:S(2)}, u32[]{:S(2)}) %all-to-all-start.1) | async-done | bytes 2097184 | tf_op jit(solution)/shard_map/all_to_all | solution.py:30
  207.6 7.4 %all-to-all-start.2 = ((bf16[8,64,1024]{2,1,0:T(8,128)(2,1)}), bf16[8,64,1024]{2,1,0:T(8,128)(2,1)}, u32[]{:S(2)}, u32[]{:S(2)}) async-start(bf16[8,64,1024]{2,1,0:T(8,128)(2,1)} %bitcast.88), calls=%async_computation.2 | async-start | bytes 2097152 | tf_op jit(solution)/shard_map/all_to_all | solution.py:30
  217.4 14.1 %all-to-all-done.2 = bf16[8,64,1024]{2,1,0:T(8,128)(2,1)} async-done(((bf16[8,64,1024]{2,1,0:T(8,128)(2,1)}), bf16[8,64,1024]{2,1,0:T(8,128)(2,1)}, u32[]{:S(2)}, u32[]{:S(2)}) %all-to-all-start.2) | async-done | bytes 1048608 | tf_op jit(solution)/shard_map/all_to_all | solution.py:30
  237.7 22.4 %all_to_all.57 = f32[128,8,128]{2,1,0:T(8,128)} all-to-all(f32[128,8,128]{2,1,0:T(8,128)S(1)} %pad_maximum_fusion), channel_id=1, replica_groups=mesh['yl'=2,'x'=4,'yh'=2,'z'=4,'c'=2] {'yl','x','yh','z','c'}, dimensions={0} | all-to-all | bytes 1048576 | tf_op jit(solution)/shard_map/all_to_all | solution.py:30
  261.3 27.9 %all_to_all.58 = f32[128,8,128]{2,1,0:T(8,128)S(1)} all-to-all(f32[128,8,128]{2,1,0:T(8,128)S(1)} %broadcast_in_dim.12), channel_id=1, replica_groups=mesh['yl'=2,'x'=4,'yh'=2,'z'=4,'c'=2] {'yl','x','yh','z','c'}, dimensions={0} | all-to-all | bytes 1048576 | tf_op jit(solution)/shard_map/all_to_all | solution.py:37
  291.0 5.8 %cholesky.44 = f32[64,64]{1,0:T(8,128)S(1)} custom-call(f32[64,64]{1,0:T(8,128)S(1)} %fusion.23), custom_call_target="Cholesky" | custom-call | tf_op jit(solution)/shard_map/jit(cholesky)/cholesky | solution.py:87
  298.2 4.9 %custom-call.10 = f32[1,64,64]{1,2,0:T(8,128)S(1)} custom-call(f32[1,64,64]{2,1,0:T(8,128)S(1)} %fusion.16), custom_call_target="InvertDiagBlocksLowerTriangular" | custom-call | tf_op jit(solution)/shard_map/triangular_solve/custom-call.0 | solution.py:41
  307.5 5.0 %all-to-all-start.6 = ((f32[128,8,128]{2,1,0:T(8,128)}), f32[128,8,128]{2,1,0:T(8,128)}, u32[]{:S(2)}, u32[]{:S(2)}) async-start(f32[128,8,128]{2,1,0:T(8,128)} %pad_maximum_fusion.1), calls=%async_computation.6 | async-start | bytes 1048576 | tf_op jit(solution)/shard_map/all_to_all | solution.py:30
  313.4 12.5 %all-to-all-done.6 = f32[128,8,128]{2,1,0:T(8,128)} async-done(((f32[128,8,128]{2,1,0:T(8,128)}), f32[128,8,128]{2,1,0:T(8,128)}, u32[]{:S(2)}, u32[]{:S(2)}) %all-to-all-start.6) | async-done | bytes 524320 | tf_op jit(solution)/shard_map/all_to_all | solution.py:30
  330.5 4.2 %all-to-all-done.5 = f32[8,1,4096]{2,1,0:T(1,128)S(1)} async-done(((f32[8,1,4096]{2,1,0:T(1,128)}), f32[8,1,4096]{2,1,0:T(1,128)S(1)}, u32[]{:S(2)}, u32[]{:S(2)}) %all-to-all-start.5) | async-done | bytes 131104 | tf_op jit(solution)/shard_map/all_to_all | solution.py:37
  335.5 6.3 %all-to-all-start.7 = ((f32[128,8,128]{2,1,0:T(8,128)}), f32[128,8,128]{2,1,0:T(8,128)}, u32[]{:S(2)}, u32[]{:S(2)}) async-start(f32[128,8,128]{2,1,0:T(8,128)} %broadcast_in_dim.14), calls=%async_computation.7 | async-start | bytes 1048576 | tf_op jit(solution)/shard_map/all_to_all | solution.py:37
  343.4 11.8 %all-to-all-done.7 = f32[128,8,128]{2,1,0:T(8,128)} async-done(((f32[128,8,128]{2,1,0:T(8,128)}), f32[128,8,128]{2,1,0:T(8,128)}, u32[]{:S(2)}, u32[]{:S(2)}) %all-to-all-start.7) | async-done | bytes 524320 | tf_op jit(solution)/shard_map/all_to_all | solution.py:37
  356.9 5.8 %cholesky.55 = f32[64,64]{1,0:T(8,128)S(1)} custom-call(f32[64,64]{1,0:T(8,128)S(1)} %fusion.21), custom_call_target="Cholesky" | custom-call | tf_op jit(solution)/shard_map/jit(cholesky)/cholesky | solution.py:87
  364.1 4.9 %custom-call.8 = f32[1,64,64]{1,2,0:T(8,128)S(1)} custom-call(f32[1,64,64]{2,1,0:T(8,128)S(1)} %fusion.17), custom_call_target="InvertDiagBlocksLowerTriangular" | custom-call | tf_op jit(solution)/shard_map/triangular_solve | solution.py:41
  374.8 4.4 %fusion.11 = f32[1,512,1024]{2,1,0:T(8,128)} fusion(f32[512,1024]{1,0:T(8,128)S(1)} %fusion.28, f32[512,1024]{1,0:T(8,128)} %all-gather.5.cloned.1.call-done, f32[512,1024]{1,0:T(8,128)S(1)} %convert_reduce_fusion, bf16[1,512,1024]{2,1,0:T(8,128)(2,1)} %param.12, bf16[1,512,1024]{2,1,0:T(8,128)(2,1)} %param.13), kind=kLoop, calls=%fused_computation.13 | loop fusion | flops 3670016 | bytes 10485760 | tf_op jit(solution)/shard_map/broadcast_in_dim | solution.py:93
  379.3 29.8 %fusion.5 = bf16[1,512,8192]{2,1,0:T(8,128)(2,1)} fusion(bf16[1,8192,1024]{2,1,0:T(8,128)(2,1)} %all-gather.3.cloned.1.call-done, bf16[1,512,1024]{2,1,0:T(8,128)(2,1)S(1)} %copy-done), kind=kOutput, calls=%fused_computation.7 | convolution fusion | flops 8598323200 | bytes 26214400 | tf_op jit(solution)/shard_map/dot_general | solution.py:100
  (59 shorter events, 39.7 us)
Async XLA Ops:
  7.2 1.5 copy-start
  7.2 226.5 %all-gather.5.cloned.1.call-start = ((), (), s32[]{:S(2)}) async-start(), calls=%async_computation.9 | async-start | bytes 2359296 | tf_op jit(solution)/shard_map/all_gather | solution.py:66
  7.9 371.3 %all-gather.3.cloned.1.call-start = ((), (), s32[]{:S(2)}) async-start(), calls=%async_computation.8 | async-start | bytes 17825792 | tf_op jit(solution)/shard_map/all_gather | solution.py:99
  32.4 14.5 %collective-permute-start = (bf16[8,512,1024]{2,1,0:T(8,128)(2,1)}, bf16[8,512,1024]{2,1,0:T(8,128)(2,1)}, u32[]{:S(2)}, u32[]{:S(2)}) collective-permute-start(bf16[8,512,1024]{2,1,0:T(8,128)(2,1)} %dynamic-slice_bitcast_fusion), channel_id=1, source_target_pairs={{0,1},{1,0},{2,3},{3,2},{4,5},{5,4},{6,7},{7,6},{8,9},{9,8},{10,11... | collective-permute-start | bytes 25165832 | tf_op jit(solution)/shard_map/ppermute | solution.py:62
  57.6 8.0 %copy-start.1 = (bf16[1,512,1024]{2,1,0:T(8,128)(2,1)S(1)}, bf16[1,512,1024]{2,1,0:T(8,128)(2,1)}, u32[]{:S(2)}) copy-start(bf16[1,512,1024]{2,1,0:T(8,128)(2,1)} %param.12) | copy-start | bytes 3145732
  57.6 8.0 %copy-start.2 = (bf16[1,512,1024]{2,1,0:T(8,128)(2,1)S(1)}, bf16[1,512,1024]{2,1,0:T(8,128)(2,1)}, u32[]{:S(2)}) copy-start(bf16[1,512,1024]{2,1,0:T(8,128)(2,1)} %param.13) | copy-start | bytes 3145732
  57.6 118.5 %all-to-all-start = ((bf16[8,512,1024]{2,1,0:T(8,128)(2,1)}), bf16[8,512,1024]{2,1,0:T(8,128)(2,1)}, u32[]{:S(2)}, u32[]{:S(2)}) async-start(bf16[8,512,1024]{2,1,0:T(8,128)(2,1)} %fusion), calls=%async_computation | async-start | bytes 16777216 | tf_op jit(solution)/shard_map/all_to_all | solution.py:30
  176.1 31.5 %all-to-all-start.1 = ((f32[8,64,1024]{2,1,0:T(8,128)}), f32[8,64,1024]{2,1,0:T(8,128)}, u32[]{:S(2)}, u32[]{:S(2)}) async-start(f32[8,64,1024]{2,1,0:T(8,128)} %bitcast.87), calls=%async_computation.1 | async-start | bytes 4194304 | tf_op jit(solution)/shard_map/all_to_all | solution.py:30
  207.6 23.9 %all-to-all-start.2 = ((bf16[8,64,1024]{2,1,0:T(8,128)(2,1)}), bf16[8,64,1024]{2,1,0:T(8,128)(2,1)}, u32[]{:S(2)}, u32[]{:S(2)}) async-start(bf16[8,64,1024]{2,1,0:T(8,128)(2,1)} %bitcast.88), calls=%async_computation.2 | async-start | bytes 2097152 | tf_op jit(solution)/shard_map/all_to_all | solution.py:30
  289.2 0.8 copy-start.3
  307.5 18.4 %all-to-all-start.6 = ((f32[128,8,128]{2,1,0:T(8,128)}), f32[128,8,128]{2,1,0:T(8,128)}, u32[]{:S(2)}, u32[]{:S(2)}) async-start(f32[128,8,128]{2,1,0:T(8,128)} %pad_maximum_fusion.1), calls=%async_computation.6 | async-start | bytes 1048576 | tf_op jit(solution)/shard_map/all_to_all | solution.py:30
  325.9 8.8 %all-to-all-start.5 = ((f32[8,1,4096]{2,1,0:T(1,128)}), f32[8,1,4096]{2,1,0:T(1,128)S(1)}, u32[]{:S(2)}, u32[]{:S(2)}) async-start(f32[8,1,4096]{2,1,0:T(1,128)} %reshape.98), calls=%async_computation.5 | async-start | bytes 262144 | tf_op jit(solution)/shard_map/all_to_all | solution.py:37
  335.5 19.7 %all-to-all-start.7 = ((f32[128,8,128]{2,1,0:T(8,128)}), f32[128,8,128]{2,1,0:T(8,128)}, u32[]{:S(2)}, u32[]{:S(2)}) async-start(f32[128,8,128]{2,1,0:T(8,128)} %broadcast_in_dim.14), calls=%async_computation.7 | async-start | bytes 1048576 | tf_op jit(solution)/shard_map/all_to_all | solution.py:37
  371.1 37.9 %copy-start.4 = (f32[1024,64]{0,1:T(8,128)}, f32[1024,64]{0,1:T(8,128)S(1)}, u32[]{:S(2)}) copy-start(f32[1024,64]{0,1:T(8,128)S(1)} %convolution_bitcast_fusion.2) | copy-start | bytes 786436
Sparse Core Ops, SparseCore 0:
  9.6 44.0 all-gather.4
  56.2 236.4 all-gather.2

commit v2 on v1

v2 whole, which is shorter than its diff:
```python
import functools
import math

import jax
import jax.numpy as jnp
from jax import lax
from jax.experimental import pallas as pl
from jax.experimental.pallas import tpu as pltpu
from jax.sharding import PartitionSpec as P

D = 8192
ROUNDS = 2

outer_rate = 0.7
momentum_keep = 0.9
inner_rate = 0.5
inv_root = 1.0 / math.sqrt(D)

f32 = jnp.float32
bf16 = jnp.bfloat16

NZ = 4
PLACES = [(y, z, c) for y in range(2) for z in range(NZ) for c in range(2)]


def place(y, z, c):
    return ((y % 2) * NZ + z % NZ) * 2 + c % 2


def hop(value, dy=0, dz=0, dc=0):
    pairs = [(place(y, z, c), place(y + dy, z + dz, c + dc)) for y, z, c in PLACES]
    return lax.ppermute(value, "fsdp", pairs)


def dot(a, b, dims=((1,), (0,))):
    return lax.dot_general(
        a, b, (dims, ((), ())), precision=lax.Precision.HIGHEST, preferred_element_type=f32
    )


def scatter_sum(value, axes, parts):
    got = lax.all_to_all(value, axes, 0, 0, tiled=True)
    return got.reshape(parts, -1, value.shape[1]).astype(f32).sum(0)


def gather_rows(value, axes, parts):
    rows, width = value.shape
    sent = jnp.broadcast_to(value[None], (parts, rows, width)).reshape(parts * rows, width)
    return lax.all_to_all(sent, axes, 0, 0, tiled=True)


def orthonormal_part(matrix, lower_factor):
    return lax.linalg.triangular_solve(
        lower_factor, matrix, left_side=False, lower=True, transpose_a=True
    )


def term_kernel(separate, spots, halves, tokens, cotangent, *refs):
    term = inv_root * lax.dot_general(
        tokens[...], cotangent[...], (((0,), (0,)), ((), ())), preferred_element_type=f32
    )
    if not separate:
        refs[0][0] = term.astype(bf16)
        return
    total = (term + refs[0][0].astype(f32)).astype(bf16)
    for index, out in enumerate(refs[1:]):

        @pl.when(pl.program_id(0) == index)
        def _():
            out[...] = total


def term_blocks(tokens_in, cotangent, blocks, core, came=None):
    depth, wide = tokens_in.shape
    rows = wide // len(PLACES)
    half = cotangent.shape[1] // 2
    count = len(blocks)
    me = lax.axis_index("fsdp")
    y, z = me // (2 * NZ), (me // 2) % NZ
    spots = jnp.stack([place(y + dy, z + dz, core) for dy, dz, _ in blocks]).astype(jnp.int32)
    halves = jnp.array([h for _, _, h in blocks], jnp.int32)
    in_specs = [
        pl.BlockSpec((depth, rows), lambda i, spots, halves: (0, spots[i])),
        pl.BlockSpec((depth, half), lambda i, spots, halves: (0, halves[i])),
    ]
    operands = [tokens_in, cotangent]
    if came is None:
        out_specs = pl.BlockSpec((1, rows, half), lambda i, spots, halves: (i, 0, 0))
        out_shape = jax.ShapeDtypeStruct((count, rows, half), bf16)
    else:
        in_specs.append(pl.BlockSpec((1, rows, half), lambda i, spots, halves: (i, 0, 0)))
        operands.append(came)
        out_specs = [pl.BlockSpec((rows, half), lambda i, spots, halves: (0, 0))] * count
        out_shape = [jax.ShapeDtypeStruct((rows, half), bf16)] * count
    return pl.pallas_call(
        functools.partial(term_kernel, came is not None),
        grid_spec=pltpu.PrefetchScalarGridSpec(
            num_scalar_prefetch=2, grid=(count,), in_specs=in_specs, out_specs=out_specs
        ),
        out_shape=out_shape,
        compiler_params=pltpu.CompilerParams(vmem_limit_bytes=40 << 20),
        cost_estimate=pl.CostEstimate(
            flops=2 * count * depth * rows * half,
            bytes_accessed=2 * count * (depth * rows + 2 * rows * half),
            transcendentals=0,
        ),
    )(spots, halves, *operands)


def add(*values):
    total = values[0].astype(f32)
    for value in values[1:]:
        total = total + value.astype(f32)
    return total


def ring_sum(two_up, two_down, up_up, up_down, down_up, down_down, own):
    from_below = hop(two_up, dz=1)
    from_above = hop(two_down, dz=-1)
    plain_below = hop(up_down, dz=1)
    plain_above = hop(down_up, dz=-1)
    merged_below = hop(add(up_up, from_below).astype(bf16), dz=1)
    merged_above = hop(add(down_down, from_above).astype(bf16), dz=-1)
    first = add(own[0], merged_below, plain_above)
    second = add(own[1], plain_below, merged_above)
    return first, second


def reduce_terms(tokens_in, cotangent):
    core = lax.axis_index("fsdp") % 2
    groups = [
        [(1, 2, 1), (1, 1, 1), (1, 3, 1), (1, 0, 1)],
        [(0, 2, 0), (1, 2, 0), (0, 1, 0), (1, 1, 0), (0, 3, 0), (1, 3, 0)],
        [(0, 2, 1), (0, 1, 1), (0, 3, 1), (0, 0, 1), (0, 0, 0), (1, 0, 0)],
    ]
    pair = {}
    for blocks in groups:
        came = hop(term_blocks(tokens_in, cotangent, blocks, 1 - core), dc=1)
        pair.update(zip(blocks, term_blocks(tokens_in, cotangent, blocks, core, came)))
    half_rows = pair[0, 0, 1].shape[0] // 2
    both = {}
    for dz in (2, 1, 3, 0):
        got = hop(pair[1, dz, 1], dy=1)
        mine = pair[0, dz, 1]
        both[dz] = [
            add(mine[:half_rows], got[:half_rows]),
            add(mine[half_rows:], got[half_rows:]),
        ]
    near, far = ring_sum(
        pair[0, 2, 0], pair[1, 2, 0], pair[0, 1, 0], pair[1, 1, 0], pair[0, 3, 0], pair[1, 3, 0],
        (pair[0, 0, 0], pair[1, 0, 0]),
    )
    first_half = add(near, hop(far.astype(bf16), dy=1))
    both = {dz: both[dz] if dz == 0 else [v.astype(bf16) for v in both[dz]] for dz in both}
    second_half = jnp.concatenate(
        ring_sum(both[2][0], both[2][1], both[1][0], both[1][1], both[3][0], both[3][1], both[0])
    )
    return first_half, second_half


def per_device(inputs, grad_keys, local_weights, feedback, base, momentum, warm_start):
    tokens_in = inputs[0]
    cotangent = grad_keys[0]
    weights = local_weights[0]
    rep_size, fsdp_size = lax.axis_size("rep"), lax.axis_size("fsdp")
    everyone = rep_size * fsdp_size
    rows, width = weights.shape
    my_rep = lax.axis_index("rep")

    full_base = lax.all_gather(base, "rep", axis=1, tiled=True)
    drift = feedback[0].astype(f32) - weights.astype(f32)
    part_rows = rows // rep_size
    base_part = lax.dynamic_slice_in_dim(full_base, my_rep * part_rows, part_rows, 0)
    early_mean = base_part + scatter_sum(drift, "rep", rep_size) / rep_size

    halves = reduce_terms(tokens_in, cotangent)
    inner_mean = jnp.concatenate(
        [scatter_sum(half.astype(bf16), "rep", rep_size) for half in halves], axis=1
    )
    pseudo_mean = early_mean + (inner_rate / rep_size) * inner_mean
    pseudo = full_base + drift + inner_rate * jnp.concatenate(halves, axis=1)

    late_weights, pseudo = lax.optimization_barrier((local_weights, pseudo))
    every_row = lax.all_gather(late_weights, "fsdp", axis=1, tiled=True)[0]

    factor = warm_start
    rank = factor.shape[1]
    everything = ("rep", "fsdp")
    for repeat in range(ROUNDS):
        left_part = dot(pseudo_mean, factor)
        raised = dot(pseudo_mean, left_part, ((0,), (0,)))
        gram_part = dot(left_part, left_part, ((0,), (0,)))
        packed = jnp.concatenate(
            [raised, jnp.tile(gram_part, (raised.shape[0] // rank, 1))], axis=1
        )
        summed = gather_rows(scatter_sum(packed, everything, everyone), everything, everyone)
        lower_factor = jnp.linalg.cholesky(summed[:rank, rank:])
        factor = orthonormal_part(summed[:, :rank], lower_factor)
    left = gather_rows(left_part, "rep", rep_size)
    orthonormal = orthonormal_part(left, lower_factor)

    approx = dot(orthonormal, factor, ((1,), (1,)))
    feedback_out = (pseudo - approx)[None]
    block_width = base.shape[1]
    column_block = lax.dynamic_slice_in_dim(approx, my_rep * block_width, block_width, 1)
    momentum_out = momentum_keep * momentum + column_block
    base_out = base - outer_rate * (column_block + momentum_keep * momentum_out)

    product = lax.dot_general(
        cotangent, every_row, (((1,), (1,)), ((), ())), preferred_element_type=f32
    )
    grad_inputs = (product * inv_root).astype(bf16)[None]
    return (grad_inputs, feedback_out, base_out, momentum_out, factor)


def solution(mesh):
    split = P("rep", "fsdp", None)
    shared = P("fsdp", "rep")
    return jax.shard_map(
        per_device,
        mesh=mesh,
        in_specs=(split, split, split, split, shared, shared, P()),
        out_specs=(split, split, shared, shared, P()),
        check_vma=False,
    )
```

time: 417 us -> 397 us (0.952)
  waiting for transfers between devices: 186 us -> 108 us
  blocking collectives: 50.3 us -> 86.2 us
  matrix products: 55.5 us -> 23.8 us
  Pallas kernels: 0 us -> 31.6 us
  local copies, waits for them, and re-layouts: 12 us -> 30.5 us
  starting transfers between devices: 35.9 us -> 52.3 us
  other arithmetic: 61.5 us -> 49 us
    all_to_all x4 -> x3, waiting for transfers between devices: 156 us -> 44.2 us  [scatter_sum(): got = lax.all_to_all(value, axes, 0, 0, tiled=True)]
    ppermute x1 -> x20, waiting for transfers between devices: 13.1 us -> 46.1 us  [hop(): return lax.ppermute(value, 'fsdp', pairs)]
    pallas_call x0 -> x6, Pallas kernels: none -> 31.6 us  [term_blocks(): pl.pallas_call(functools.partial(term_kernel, came is not None), grid_spe...]
    ppermute x1 -> x20, starting transfers between devices: 1.42 us -> 29.3 us  [hop(): return lax.ppermute(value, 'fsdp', pairs)]
    unnamed x14 -> x55, local copies, waits for them, and re-layouts: 1.9 us -> 28.5 us
    all_to_all x1, blocking collectives: 27.9 us -> 49.1 us  [gather_rows(): return lax.all_to_all(sent, axes, 0, 0, tiled=True)]
    dot_general x1 -> x0, matrix products: 15.9 us -> none  [per_device(): lax.dot_general(tokens_in, cotangent, (((0,), (0,)), ((), ())), preferred...]
    all_to_all x1 -> x2, blocking collectives: 22.4 us -> 37.1 us  [scatter_sum(): got = lax.all_to_all(value, axes, 0, 0, tiled=True)]
  transfers between devices with their start and end apart: 9 -> 27, of which waited for: 7 -> 15; matrix products, arithmetic and copies ran while one was open for 24% -> 14% of each run, Pallas kernels for 0% -> 7%
where the time goes in v2:
time: 397 us; the launch traced here: 396 us
  waiting for transfers between devices  108 us (27%)
  blocking collectives  86.2 us (22%)
  starting transfers between devices  52.3 us (13%)
  other arithmetic  49 us (12%)
  Pallas kernels  31.6 us (8%)
  local copies, waits for them, and re-layouts  30.5 us (8%)
  matrix products  23.8 us (6%)
  between operations  14.6 us (4%)
    all_to_all x1, blocking collectives, gather_rows(): return lax.all_to_all(sent, axes, 0, 0, tiled=True)  49.1 us
    ppermute x20, waiting for transfers between devices, hop(): return lax.ppermute(value, 'fsdp', pairs)  46.1 us
    all_to_all x3, waiting for transfers between devices, scatter_sum(): got = lax.all_to_all(value, axes, 0, 0, tiled=True)  44.2 us
    all_to_all x2, blocking collectives, scatter_sum(): got = lax.all_to_all(value, axes, 0, 0, tiled=True)  37.1 us
    pallas_call x6, Pallas kernels, term_blocks(): pl.pallas_call(functools.partial(term_kernel, came is not None), grid_spe...  31.6 us
    ppermute x20, starting transfers between devices, hop(): return lax.ppermute(value, 'fsdp', pairs)  29.3 us
    unnamed x55, local copies, waits for them, and re-layouts  28.5 us
    all_to_all x2, waiting for transfers between devices, gather_rows(): return lax.all_to_all(sent, axes, 0, 0, tiled=True)  17.4 us
  transfers between devices with their start and end apart: 27, of which 15 were waited for; matrix products, arithmetic and copies ran while one was open for 14% of the time, Pallas kernels for 7%

profile of v2, /device:TPU:1, one launch (start us, length us, event | category | flops | bytes accessed | tf_op | source)
XLA Modules:
  0.0 395.7 jit_solution(16961684860097418330)
XLA Ops:
  12.1 5.1 %shard_map.166 = bf16[6,512,512]{2,1,0:T(8,128)(2,1)} custom-call(s32[6]{0:T(128)S(1)} %stack.101.spots, s32[6]{0:T(128)S(1)} %call_exported.1.halves, bf16[512,8192]{1,0:T(8,128)(2,1)S(1)} %bitcast.92, bf16[512,1024]{1,0:T(8,128)(2,1)S(1)} %bitcast.96), custom_call_target="tpu_custom_call" | custom-call | flops 1610612736 | bytes 9437184 | tf_op jit(solution)/shard_map/pallas_call | solution.py:95
  22.1 5.1 %shard_map.164 = bf16[6,512,512]{2,1,0:T(8,128)(2,1)} custom-call(s32[6]{0:T(128)S(1)} %stack.93.spots, s32[6]{0:T(128)S(1)} %copy-done.8, bf16[512,8192]{1,0:T(8,128)(2,1)S(1)} %bitcast.93, bf16[512,1024]{1,0:T(8,128)(2,1)S(1)} %bitcast.97), custom_call_target="tpu_custom_call" | custom-call | flops 1610612736 | bytes 9437184 | tf_op jit(solution)/shard_map/pallas_call | solution.py:95
  48.6 7.4 %shard_map.167 = (bf16[512,512]{1,0:T(8,128)(2,1)S(1)}, bf16[512,512]{1,0:T(8,128)(2,1)}, bf16[512,512]{1,0:T(8,128)(2,1)S(1)}, bf16[512,512]{1,0:T(8,128)(2,1)S...) custom-call(s32[6]{0:T(128)S(1)} %stack.97.spots, s32[6]{0:T(128)S(1)} %call_exported.1.halves, ...), custom_call_target="tpu_custom_call" | custom-call | flops 1610612736 | bytes 9437184 | tf_op jit(solution)/shard_map/pallas_call | solution.py:95
  64.5 6.6 %shard_map.165 = (bf16[512,512]{1,0:T(8,128)(2,1)S(1)}, bf16[512,512]{1,0:T(8,128)(2,1)S(1)}, bf16[512,512]{1,0:T(8,128)(2,1)S(1)}, bf16[512,512]{1,0:T(8,128)(2...) custom-call(s32[6]{0:T(128)S(1)} %stack.87.spots, s32[6]{0:T(128)S(1)} %copy-done.8, ...), custom_call_target="tpu_custom_call" | custom-call | flops 1610612736 | bytes 9437184 | tf_op jit(solution)/shard_map/pallas_call | solution.py:95
  71.1 6.5 %collective-permute-done.12 = bf16[512,512]{1,0:T(8,128)(2,1)} collective-permute-done((bf16[512,512]{1,0:T(8,128)(2,1)}, bf16[512,512]{1,0:T(8,128)(2,1)}, u32[]{:S(2)}, u32[]{:S(2)}) %collective-permute-start.12) | collective-permute-done | bytes 524320 | tf_op jit(solution)/shard_map/ppermute | solution.py:32
  82.7 7.4 %collective-permute-done.11 = bf16[512,512]{1,0:T(8,128)(2,1)S(1)} collective-permute-done((bf16[512,512]{1,0:T(8,128)(2,1)}, bf16[512,512]{1,0:T(8,128)(2,1)S(1)}, u32[]{:S(2)}, u32[]{:S(2)}) %collective-permute-start.11) | collective-permute-done | bytes 524320 | tf_op jit(solution)/shard_map/ppermute | solution.py:32
  93.0 8.4 %collective-permute-done.15 = bf16[512,512]{1,0:T(8,128)(2,1)S(1)} collective-permute-done((bf16[512,512]{1,0:T(8,128)(2,1)S(1)}, bf16[512,512]{1,0:T(8,128)(2,1)S(1)}, u32[]{:S(2)}, u32[]{:S(2)}) %collective-permute-start.15) | collective-permute-done | bytes 524320 | tf_op jit(solution)/shard_map/ppermute | solution.py:32
  111.0 4.9 %collective-permute-done.10 = bf16[512,512]{1,0:T(8,128)(2,1)S(1)} collective-permute-done((bf16[512,512]{1,0:T(8,128)(2,1)S(1)}, bf16[512,512]{1,0:T(8,128)(2,1)S(1)}, u32[]{:S(2)}, u32[]{:S(2)}) %collective-permute-start.10) | collective-permute-done | bytes 524320 | tf_op jit(solution)/shard_map/ppermute | solution.py:32
  125.7 4.9 %collective-permute-done.4 = bf16[512,512]{1,0:T(8,128)(2,1)S(1)} collective-permute-done((bf16[512,512]{1,0:T(8,128)(2,1)S(1)}, bf16[512,512]{1,0:T(8,128)(2,1)S(1)}, u32[]{:S(2)}, u32[]{:S(2)}) %collective-permute-start.4) | collective-permute-done | bytes 524320 | tf_op jit(solution)/shard_map/ppermute | solution.py:32
  143.5 5.1 %all-to-all-start = ((f32[8,64,1024]{2,1,0:T(8,128)}), f32[8,64,1024]{2,1,0:T(8,128)S(1)}, u32[]{:S(2)}, u32[]{:S(2)}) async-start(f32[8,64,1024]{2,1,0:T(8,128)} %bitcast.102), calls=%async_computation | async-start | bytes 4194304 | tf_op jit(solution)/shard_map/all_to_all | solution.py:42
  150.6 25.1 %all-to-all-done = f32[8,64,1024]{2,1,0:T(8,128)S(1)} async-done(((f32[8,64,1024]{2,1,0:T(8,128)}), f32[8,64,1024]{2,1,0:T(8,128)S(1)}, u32[]{:S(2)}, u32[]{:S(2)}) %all-to-all-start) | async-done | bytes 2097184 | tf_op jit(solution)/shard_map/all_to_all | solution.py:42
  175.7 15.8 %all_to_all.60 = bf16[8,64,512]{2,1,0:T(8,128)(2,1)} all-to-all(bf16[8,64,512]{2,1,0:T(8,128)(2,1)} %bitcast.110), channel_id=1, replica_groups=mesh['rep'=8,'fsdp'=16] {'rep'}, dimensions={0} | all-to-all | bytes 1048576 | tf_op jit(solution)/shard_map/all_to_all | solution.py:42
  197.7 6.2 %all-to-all-done.1 = bf16[8,64,512]{2,1,0:T(8,128)(2,1)} async-done(((bf16[8,64,512]{2,1,0:T(8,128)(2,1)}), bf16[8,64,512]{2,1,0:T(8,128)(2,1)}, u32[]{:S(2)}, u32[]{:S(2)}) %all-to-all-start.1) | async-done | bytes 524320 | tf_op jit(solution)/shard_map/all_to_all | solution.py:42
  208.3 21.3 %all_to_all.61 = f32[128,8,128]{2,1,0:T(8,128)S(1)} all-to-all(f32[128,8,128]{2,1,0:T(8,128)S(1)} %pad_maximum_fusion), channel_id=1, replica_groups=mesh['rep'=8,'fsdp'=16] {'rep','fsdp'}, dimensions={0} | all-to-all | bytes 1048576 | tf_op jit(solution)/shard_map/all_to_all | solution.py:42
  229.7 49.1 %all_to_all.62 = f32[128,8,128]{2,1,0:T(8,128)S(1)} all-to-all(f32[128,8,128]{2,1,0:T(8,128)S(1)} %broadcast_in_dim.12), channel_id=1, replica_groups=mesh['rep'=8,'fsdp'=16] {'rep','fsdp'}, dimensions={0} | all-to-all | bytes 1048576 | tf_op jit(solution)/shard_map/all_to_all | solution.py:49
  279.1 5.9 %cholesky.44 = f32[64,64]{1,0:T(8,128)S(1)} custom-call(f32[64,64]{1,0:T(8,128)S(1)} %fusion.18), custom_call_target="Cholesky" | custom-call | tf_op jit(solution)/shard_map/jit(cholesky)/cholesky | solution.py:197
  286.3 4.9 %custom-call.10 = f32[1,64,64]{1,2,0:T(8,128)S(1)} custom-call(f32[1,64,64]{2,1,0:T(8,128)S(1)} %fusion.11), custom_call_target="InvertDiagBlocksLowerTriangular" | custom-call | tf_op jit(solution)/shard_map/triangular_solve/custom-call.0 | solution.py:53
  300.0 12.9 %all-to-all-done.6 = f32[128,8,128]{2,1,0:T(8,128)S(1)} async-done(((f32[128,8,128]{2,1,0:T(8,128)}), f32[128,8,128]{2,1,0:T(8,128)S(1)}, u32[]{:S(2)}, u32[]{:S(2)}) %all-to-all-start.6) | async-done | bytes 524320 | tf_op jit(solution)/shard_map/all_to_all | solution.py:42
  316.4 5.2 %all-to-all-done.5 = f32[8,1,4096]{2,1,0:T(1,128)S(1)} async-done(((f32[8,1,4096]{2,1,0:T(1,128)}), f32[8,1,4096]{2,1,0:T(1,128)S(1)}, u32[]{:S(2)}, u32[]{:S(2)}) %all-to-all-start.5) | async-done | bytes 131104 | tf_op jit(solution)/shard_map/all_to_all | solution.py:49
  322.4 5.8 %all-to-all-start.7 = ((f32[128,8,128]{2,1,0:T(8,128)}), f32[128,8,128]{2,1,0:T(8,128)S(1)}, u32[]{:S(2)}, u32[]{:S(2)}) async-start(f32[128,8,128]{2,1,0:T(8,128)} %broadcast_in_dim.14), calls=%async_computation.7 | async-start | bytes 1048576 | tf_op jit(solution)/shard_map/all_to_all | solution.py:49
  329.9 12.1 %all-to-all-done.7 = f32[128,8,128]{2,1,0:T(8,128)S(1)} async-done(((f32[128,8,128]{2,1,0:T(8,128)}), f32[128,8,128]{2,1,0:T(8,128)S(1)}, u32[]{:S(2)}, u32[]{:S(2)}) %all-to-all-start.7) | async-done | bytes 524320 | tf_op jit(solution)/shard_map/all_to_all | solution.py:49
  342.3 5.9 %cholesky.55 = f32[64,64]{1,0:T(8,128)S(1)} custom-call(f32[64,64]{1,0:T(8,128)S(1)} %fusion.16), custom_call_target="Cholesky" | custom-call | tf_op jit(solution)/shard_map/jit(cholesky)/cholesky | solution.py:197
  359.9 17.0 %fusion.4 = bf16[1,512,8192]{1,2,0:T(8,128)(2,1)} fusion(bf16[1,8192,1024]{2,1,0:T(8,128)(2,1)} %all-gather.5.cloned.1.call-done, bf16[1,512,1024]{2,1,0:T(8,128)(2,1)S(1)} %copy-done.7), kind=kOutput, calls=%fused_computation.3 | convolution fusion | flops 8598323200 | bytes 26214400 | tf_op jit(solution)/shard_map/dot_general | solution.py:209
  376.9 12.0 %copy.29 = bf16[1,512,8192]{2,1,0:T(8,128)(2,1)} copy(bf16[1,512,8192]{1,2,0:T(8,128)(2,1)} %fusion.4) | data formatting | bytes 16777216
  (157 shorter events, 120.6 us)
Async XLA Ops:
  7.2 128.8 %all-gather.3.cloned.1.call-start = ((), (), s32[]{:S(2)}) async-start(), calls=%async_computation.8 | async-start | bytes 2359296 | tf_op jit(solution)/shard_map/all_gather | solution.py:170
  17.2 31.4 %collective-permute-start.1 = (bf16[6,512,512]{2,1,0:T(8,128)(2,1)}, bf16[6,512,512]{2,1,0:T(8,128)(2,1)}, u32[]{:S(2)}, u32[]{:S(2)}) collective-permute-start(bf16[6,512,512]{2,1,0:T(8,128)(2,1)} %shard_map.166), channel_id=1, source_target_pairs={{0,1},{1,0},{2,3},{3,2},{4,5},{5,4},{6,7},{7,6},{8,9},{9,8},{10,11... | collective-permute-start | bytes 9437192 | tf_op jit(solution)/shard_map/ppermute | solution.py:32
  27.1 37.4 %collective-permute-start = (bf16[6,512,512]{2,1,0:T(8,128)(2,1)}, bf16[6,512,512]{2,1,0:T(8,128)(2,1)}, u32[]{:S(2)}, u32[]{:S(2)}) collective-permute-start(bf16[6,512,512]{2,1,0:T(8,128)(2,1)} %shard_map.164), channel_id=1, source_target_pairs={{0,1},{1,0},{2,3},{3,2},{4,5},{5,4},{6,7},{7,6},{8,9},{9,8},{10,11... | collective-permute-start | bytes 9437192 | tf_op jit(solution)/shard_map/ppermute | solution.py:32
  31.5 328.4 %all-gather.5.cloned.1.call-start = ((), (), s32[]{:S(2)}) async-start(), calls=%async_computation.9 | async-start | bytes 17825792 | tf_op jit(solution)/shard_map/all_gather | solution.py:184
  45.5 32.1 %collective-permute-start.12 = (bf16[512,512]{1,0:T(8,128)(2,1)}, bf16[512,512]{1,0:T(8,128)(2,1)}, u32[]{:S(2)}, u32[]{:S(2)}) collective-permute-start(bf16[512,512]{1,0:T(8,128)(2,1)} %get-tuple-element.38), channel_id=1, source_target_pairs={{0,8},{1,9},{2,10},{3,11},{4,12},{5,13},{6,14},{7,15},{8,0},{9,1},... | collective-permute-start | bytes 1572872 | tf_op jit(solution)/shard_map/ppermute | solution.py:32
  57.6 23.9 %collective-permute-start.6 = (bf16[512,512]{1,0:T(8,128)(2,1)}, bf16[512,512]{1,0:T(8,128)(2,1)}, u32[]{:S(2)}, u32[]{:S(2)}) collective-permute-start(bf16[512,512]{1,0:T(8,128)(2,1)} %get-tuple-element.32), channel_id=1, source_target_pairs={{0,6},{1,7},{2,0},{3,1},{4,2},{5,3},{6,4},{7,5},{8,14},{9,15},{10,... | collective-permute-start | bytes 1572872 | tf_op jit(solution)/shard_map/ppermute | solution.py:32
  61.5 28.6 %collective-permute-start.11 = (bf16[512,512]{1,0:T(8,128)(2,1)}, bf16[512,512]{1,0:T(8,128)(2,1)S(1)}, u32[]{:S(2)}, u32[]{:S(2)}) collective-permute-start(bf16[512,512]{1,0:T(8,128)(2,1)} %copy-done.17), channel_id=1, source_target_pairs={{0,8},{1,9},{2,10},{3,11},{4,12},{5,13},{6,14},{7,15},{8,0},{9,1},... | collective-permute-start | bytes 1572872 | tf_op jit(solution)/shard_map/ppermute | solution.py:32
  61.6 39.8 %collective-permute-start.15 = (bf16[512,512]{1,0:T(8,128)(2,1)S(1)}, bf16[512,512]{1,0:T(8,128)(2,1)S(1)}, u32[]{:S(2)}, u32[]{:S(2)}) collective-permute-start(bf16[512,512]{1,0:T(8,128)(2,1)S(1)} %copy-done.14), channel_id=1, source_target_pairs={{0,8},{1,9},{2,10},{3,11},{4,12},{5,13},{6,14},{7,15},{8,0},{9,1},... | collective-permute-start | bytes 1572872 | tf_op jit(solution)/shard_map/ppermute | solution.py:32
  78.8 12.6 %collective-permute-start.13 = (bf16[256,512]{1,0:T(8,128)(2,1)S(1)}, bf16[256,512]{1,0:T(8,128)(2,1)S(1)}, u32[]{:S(2)}, u32[]{:S(2)}) collective-permute-start(bf16[256,512]{1,0:T(8,128)(2,1)S(1)} %get-tuple-element.61), channel_id=1, source_target_pairs={{0,2},{1,3},{2,4},{3,5},{4,6},{5,7},{6,0},{7,1},{8,10},{9,11},{10,... | collective-permute-start | bytes 786440 | tf_op jit(solution)/shard_map/ppermute | solution.py:32
  80.0 23.3 %collective-permute-start.18 = (bf16[256,512]{1,0:T(8,128)(2,1)S(1)}, bf16[256,512]{1,0:T(8,128)(2,1)S(1)}, u32[]{:S(2)}, u32[]{:S(2)}) collective-permute-start(bf16[256,512]{1,0:T(8,128)(2,1)S(1)} %get-tuple-element.62), channel_id=1, source_target_pairs={{0,6},{1,7},{2,0},{3,1},{4,2},{5,3},{6,4},{7,5},{8,14},{9,15},{10,... | collective-permute-start | bytes 786440 | tf_op jit(solution)/shard_map/ppermute | solution.py:32
  81.5 23.5 %collective-permute-start.2 = (bf16[512,512]{1,0:T(8,128)(2,1)S(1)}, bf16[512,512]{1,0:T(8,128)(2,1)S(1)}, u32[]{:S(2)}, u32[]{:S(2)}) collective-permute-start(bf16[512,512]{1,0:T(8,128)(2,1)S(1)} %copy-done.16), channel_id=1, source_target_pairs={{0,2},{1,3},{2,4},{3,5},{4,6},{5,7},{6,0},{7,1},{8,10},{9,11},{10,... | collective-permute-start | bytes 1572872 | tf_op jit(solution)/shard_map/ppermute | solution.py:32
  90.1 19.2 %collective-permute-start.5 = (bf16[512,512]{1,0:T(8,128)(2,1)S(1)}, bf16[512,512]{1,0:T(8,128)(2,1)S(1)}, u32[]{:S(2)}, u32[]{:S(2)}) collective-permute-start(bf16[512,512]{1,0:T(8,128)(2,1)S(1)} %copy-done.12), channel_id=1, source_target_pairs={{0,2},{1,3},{2,4},{3,5},{4,6},{5,7},{6,0},{7,1},{8,10},{9,11},{10,... | collective-permute-start | bytes 1572872 | tf_op jit(solution)/shard_map/ppermute | solution.py:32
  91.3 18.7 %collective-permute-start.7 = (bf16[512,512]{1,0:T(8,128)(2,1)S(1)}, bf16[512,512]{1,0:T(8,128)(2,1)S(1)}, u32[]{:S(2)}, u32[]{:S(2)}) collective-permute-start(bf16[512,512]{1,0:T(8,128)(2,1)S(1)} %add_convert_fusion.1), channel_id=1, source_target_pairs={{0,6},{1,7},{2,0},{3,1},{4,2},{5,3},{6,4},{7,5},{8,14},{9,15},{10,... | collective-permute-start | bytes 1572872 | tf_op jit(solution)/shard_map/ppermute | solution.py:32
  101.4 14.6 %collective-permute-start.10 = (bf16[512,512]{1,0:T(8,128)(2,1)S(1)}, bf16[512,512]{1,0:T(8,128)(2,1)S(1)}, u32[]{:S(2)}, u32[]{:S(2)}) collective-permute-start(bf16[512,512]{1,0:T(8,128)(2,1)S(1)} %copy-done.10), channel_id=1, source_target_pairs={{0,8},{1,9},{2,10},{3,11},{4,12},{5,13},{6,14},{7,15},{8,0},{9,1},... | collective-permute-start | bytes 1572872 | tf_op jit(solution)/shard_map/ppermute | solution.py:32
  103.3 14.5 %collective-permute-start.14 = (bf16[256,512]{1,0:T(8,128)(2,1)S(1)}, bf16[256,512]{1,0:T(8,128)(2,1)S(1)}, u32[]{:S(2)}, u32[]{:S(2)}) collective-permute-start(bf16[256,512]{1,0:T(8,128)(2,1)S(1)} %get-tuple-element.59), channel_id=1, source_target_pairs={{0,2},{1,3},{2,4},{3,5},{4,6},{5,7},{6,0},{7,1},{8,10},{9,11},{10,... | collective-permute-start | bytes 786440 | tf_op jit(solution)/shard_map/ppermute | solution.py:32
  105.0 15.6 %collective-permute-start.17 = (bf16[256,512]{1,0:T(8,128)(2,1)S(1)}, bf16[256,512]{1,0:T(8,128)(2,1)S(1)}, u32[]{:S(2)}, u32[]{:S(2)}) collective-permute-start(bf16[256,512]{1,0:T(8,128)(2,1)S(1)} %get-tuple-element.60), channel_id=1, source_target_pairs={{0,2},{1,3},{2,4},{3,5},{4,6},{5,7},{6,0},{7,1},{8,10},{9,11},{10,... | collective-permute-start | bytes 786440 | tf_op jit(solution)/shard_map/ppermute | solution.py:32
  109.3 15.3 %collective-permute-start.16 = (bf16[256,512]{1,0:T(8,128)(2,1)S(1)}, bf16[256,512]{1,0:T(8,128)(2,1)S(1)}, u32[]{:S(2)}, u32[]{:S(2)}) collective-permute-start(bf16[256,512]{1,0:T(8,128)(2,1)S(1)} %get-tuple-element.63), channel_id=1, source_target_pairs={{0,6},{1,7},{2,0},{3,1},{4,2},{5,3},{6,4},{7,5},{8,14},{9,15},{10,... | collective-permute-start | bytes 786440 | tf_op jit(solution)/shard_map/ppermute | solution.py:32
  110.0 14.6 %collective-permute-start.19 = (bf16[256,512]{1,0:T(8,128)(2,1)S(1)}, bf16[256,512]{1,0:T(8,128)(2,1)S(1)}, u32[]{:S(2)}, u32[]{:S(2)}) collective-permute-start(bf16[256,512]{1,0:T(8,128)(2,1)S(1)} %get-tuple-element.64), channel_id=1, source_target_pairs={{0,6},{1,7},{2,0},{3,1},{4,2},{5,3},{6,4},{7,5},{8,14},{9,15},{10,... | collective-permute-start | bytes 786440 | tf_op jit(solution)/shard_map/ppermute | solution.py:32
  115.9 14.7 %collective-permute-start.4 = (bf16[512,512]{1,0:T(8,128)(2,1)S(1)}, bf16[512,512]{1,0:T(8,128)(2,1)S(1)}, u32[]{:S(2)}, u32[]{:S(2)}) collective-permute-start(bf16[512,512]{1,0:T(8,128)(2,1)S(1)} %get-tuple-element.28), channel_id=1, source_target_pairs={{0,6},{1,7},{2,0},{3,1},{4,2},{5,3},{6,4},{7,5},{8,14},{9,15},{10,... | collective-permute-start | bytes 1572872 | tf_op jit(solution)/shard_map/ppermute | solution.py:32
  117.8 13.3 %collective-permute-start.3 = (bf16[512,512]{1,0:T(8,128)(2,1)S(1)}, bf16[512,512]{1,0:T(8,128)(2,1)S(1)}, u32[]{:S(2)}, u32[]{:S(2)}) collective-permute-start(bf16[512,512]{1,0:T(8,128)(2,1)S(1)} %add_convert_fusion.2), channel_id=1, source_target_pairs={{0,2},{1,3},{2,4},{3,5},{4,6},{5,7},{6,0},{7,1},{8,10},{9,11},{10,... | collective-permute-start | bytes 1572872 | tf_op jit(solution)/shard_map/ppermute | solution.py:32
  120.6 13.9 %collective-permute-start.8 = (bf16[512,512]{1,0:T(8,128)(2,1)S(1)}, bf16[512,512]{1,0:T(8,128)(2,1)S(1)}, u32[]{:S(2)}, u32[]{:S(2)}) collective-permute-start(bf16[512,512]{1,0:T(8,128)(2,1)S(1)} %add_convert_fusion), channel_id=1, source_target_pairs={{0,8},{1,9},{2,10},{3,11},{4,12},{5,13},{6,14},{7,15},{8,0},{9,1},... | collective-permute-start | bytes 1572872 | tf_op jit(solution)/shard_map/ppermute | solution.py:32
  143.5 32.3 %all-to-all-start = ((f32[8,64,1024]{2,1,0:T(8,128)}), f32[8,64,1024]{2,1,0:T(8,128)S(1)}, u32[]{:S(2)}, u32[]{:S(2)}) async-start(f32[8,64,1024]{2,1,0:T(8,128)} %bitcast.102), calls=%async_computation | async-start | bytes 4194304 | tf_op jit(solution)/shard_map/all_to_all | solution.py:42
  294.6 18.3 %all-to-all-start.6 = ((f32[128,8,128]{2,1,0:T(8,128)}), f32[128,8,128]{2,1,0:T(8,128)S(1)}, u32[]{:S(2)}, u32[]{:S(2)}) async-start(f32[128,8,128]{2,1,0:T(8,128)} %pad_maximum_fusion.1), calls=%async_computation.6 | async-start | bytes 1048576 | tf_op jit(solution)/shard_map/all_to_all | solution.py:42
  322.4 19.6 %all-to-all-start.7 = ((f32[128,8,128]{2,1,0:T(8,128)}), f32[128,8,128]{2,1,0:T(8,128)S(1)}, u32[]{:S(2)}, u32[]{:S(2)}) async-start(f32[128,8,128]{2,1,0:T(8,128)} %broadcast_in_dim.14), calls=%async_computation.7 | async-start | bytes 1048576 | tf_op jit(solution)/shard_map/all_to_all | solution.py:49
  (28 other events, 413.2 us)
Sparse Core Ops, SparseCore 0:
  31.6 42.3 all-gather.2
  140.3 141.7 all-gather.4

commit v3 on v2

v3 whole, which is shorter than its diff:
```python
import functools
import math

import jax
import jax.numpy as jnp
from jax import lax
from jax.experimental import pallas as pl
from jax.experimental.pallas import tpu as pltpu
from jax.sharding import PartitionSpec as P

D = 8192
ROUNDS = 2

outer_rate = 0.7
momentum_keep = 0.9
inner_rate = 0.5
inv_root = 1.0 / math.sqrt(D)

f32 = jnp.float32
bf16 = jnp.bfloat16

NZ = 4
FIRST = 384
PLACES = [(y, z, c) for y in range(2) for z in range(NZ) for c in range(2)]


def place(y, z, c):
    return ((y % 2) * NZ + z % NZ) * 2 + c % 2


def hop(value, dy=0, dz=0, dc=0):
    pairs = [(place(y, z, c), place(y + dy, z + dz, c + dc)) for y, z, c in PLACES]
    return lax.ppermute(value, "fsdp", pairs)


def dot(a, b, dims=((1,), (0,))):
    return lax.dot_general(
        a, b, (dims, ((), ())), precision=lax.Precision.HIGHEST, preferred_element_type=f32
    )


def scatter_sum(value, axes, parts):
    got = lax.all_to_all(value, axes, 0, 0, tiled=True)
    return got.reshape(parts, -1, value.shape[1]).astype(f32).sum(0)


def gather_rows(value, axes, parts):
    rows, width = value.shape
    sent = jnp.broadcast_to(value[None], (parts, rows, width)).reshape(parts * rows, width)
    return lax.all_to_all(sent, axes, 0, 0, tiled=True)


def after(value, *others):
    return lax.optimization_barrier((value,) + others)[0]


def all_spots():
    table = [
        [place(y + dy, z + dz, c + dc) for dc in range(2) for dy in range(2) for dz in range(NZ)]
        for y, z, c in PLACES
    ]
    return lax.dynamic_index_in_dim(
        jnp.array(table, jnp.int32), lax.axis_index("fsdp"), 0, keepdims=False
    )


BLOCKS = {
    "up": [(0, 2), (1, 1), (0, 1), (1, 0)],
    "down": [(1, 2), (0, 3), (1, 3), (0, 0)],
}
COUNT = 4


def pick(values, i):
    return sum(value * (i == at).astype(jnp.int32) for at, value in enumerate(values))


def term_of(tokens, cotangent):
    return inv_root * lax.dot_general(
        tokens[...], cotangent[...], (((0,), (0,)), ((), ())), preferred_element_type=f32
    )


def away_kernel(spots, tokens, cotangent, out):
    out[0] = term_of(tokens, cotangent).astype(bf16)


def pair_kernel(crosses, spots, tokens, cotangent, came, sent, kept, last, straight, cross):
    total = (term_of(tokens, cotangent) + came[0].astype(f32)).astype(bf16)
    first, second = total[:FIRST], total[FIRST:]
    step = pl.program_id(0)
    for index in range(COUNT):

        @pl.when(step == index)
        def _():
            if index < 2:
                sent[index] = first
            else:
                (kept, last)[index - 2][...] = first
            (cross if crosses[index] else straight)[sum(c == crosses[index] for c in crosses[:index])] = second


def term_blocks(tokens_in, cotangent, spots, kind, came=None):
    depth, wide = tokens_in.shape
    rows = wide // len(PLACES)
    width = cotangent.shape[1]
    offset = len(PLACES) // 2 if came is None else 0
    blocks = BLOCKS[kind]
    places = [offset + dy * NZ + dz for dy, dz in blocks]
    in_specs = [
        pl.BlockSpec((depth, rows), lambda i, spots: (0, spots[pick(places, i)])),
        pl.BlockSpec((depth, width), lambda i, spots: (0, 0)),
    ]
    operands = [tokens_in, cotangent]
    whole = pl.BlockSpec((1, rows, width), lambda i, spots: (i, 0, 0))
    if came is None:
        kernel = away_kernel
        out_specs = whole
        out_shape = jax.ShapeDtypeStruct((COUNT, rows, width), bf16)
    else:
        kernel = functools.partial(pair_kernel, [dy for dy, _ in blocks])
        in_specs.append(whole)
        operands.append(came)
        rest = rows - FIRST
        shapes = [(2, FIRST, width)] + [(FIRST, width)] * 2 + [(2, rest, width)] * 2
        out_specs = [
            pl.BlockSpec(shape, lambda i, spots, zeros=(0,) * len(shape): zeros) for shape in shapes
        ]
        out_shape = [jax.ShapeDtypeStruct(shape, bf16) for shape in shapes]
    return pl.pallas_call(
        kernel,
        grid_spec=pltpu.PrefetchScalarGridSpec(
            num_scalar_prefetch=1, grid=(COUNT,), in_specs=in_specs, out_specs=out_specs
        ),
        out_shape=out_shape,
        compiler_params=pltpu.CompilerParams(vmem_limit_bytes=56 << 20),
        cost_estimate=pl.CostEstimate(
            flops=2 * COUNT * depth * rows * width,
            bytes_accessed=2 * COUNT * (depth * rows + 2 * rows * width),
            transcendentals=0,
        ),
    )(spots, *operands)


def grad_kernel(cotangent, block, out):
    product = lax.dot_general(
        cotangent[...], block[...], (((1,), (1,)), ((), ())), preferred_element_type=f32
    )
    out[...] = (inv_root * product).astype(bf16)


def grad_of_inputs(cotangent, every_row):
    tokens, depth = cotangent.shape
    wide = every_row.shape[0]
    rows = 1024
    return pl.pallas_call(
        grad_kernel,
        grid=(wide // rows,),
        in_specs=[
            pl.BlockSpec((tokens, depth), lambda i: (0, 0)),
            pl.BlockSpec((rows, depth), lambda i: (i, 0)),
        ],
        out_specs=pl.BlockSpec((tokens, rows), lambda i: (0, i)),
        out_shape=jax.ShapeDtypeStruct((tokens, wide), bf16),
        compiler_params=pltpu.CompilerParams(vmem_limit_bytes=56 << 20),
        cost_estimate=pl.CostEstimate(
            flops=2 * tokens * depth * wide,
            bytes_accessed=2 * wide * (depth + tokens),
            transcendentals=0,
        ),
    )(cotangent, every_row)


def inverse_of_lower_factor(gram):
    rank = gram.shape[0]
    row = lax.broadcasted_iota(jnp.int32, (rank, rank), 0)
    lane = lax.broadcasted_iota(jnp.int32, (rank, rank), 1)
    work = jnp.concatenate([gram, (row == lane).astype(f32)], axis=1)
    tall = lax.broadcasted_iota(jnp.int32, (rank, 1), 0)
    scales = jnp.zeros((rank, 1), f32)
    for step in range(rank):
        column = work[:, step : step + 1]
        pivot = work[step : step + 1, step : step + 1]
        scales = jnp.where(tall == step, lax.rsqrt(pivot), scales)
        ratio = jnp.where(tall > step, column / pivot, 0.0)
        work = work - ratio * work[step : step + 1, :]
    return work[:, rank:] * scales


def round_kernel(last, summed, mean, *outs):
    rank = summed.shape[1] // 2
    inverse = inverse_of_lower_factor(summed[:rank, rank:])
    factor = dot(summed[:, :rank], inverse, ((1,), (1,)))
    if last:
        outs[0][...] = factor
        outs[1][...] = inverse
        return
    product_kernel_body(mean[...], factor, *outs)


def product_kernel_body(mean, factor, packed, left):
    rank = factor.shape[1]
    left_part = dot(mean, factor)
    left[...] = left_part
    gram = dot(left_part, left_part, ((0,), (0,)))
    raised = dot(mean, left_part, ((0,), (0,)))
    packed[:, :rank] = raised
    packed[:, rank:] = jnp.tile(gram, (raised.shape[0] // rank, 1))


def first_kernel(mean, factor, packed, left):
    product_kernel_body(mean[...], factor[...], packed, left)


def small_call(kernel, out_shapes, *operands):
    return pl.pallas_call(
        kernel,
        out_shape=[jax.ShapeDtypeStruct(shape, f32) for shape in out_shapes],
        compiler_params=pltpu.CompilerParams(vmem_limit_bytes=32 << 20),
        cost_estimate=pl.CostEstimate(
            flops=10**9, bytes_accessed=2 << 20, transcendentals=0
        ),
    )(*operands)


def add(*values):
    total = values[0].astype(f32)
    for value in values[1:]:
        total = total + value.astype(f32)
    return total


def reduce_terms(tokens_in, cotangent, spots):
    blocks = functools.partial(term_blocks, tokens_in)
    away_up = blocks(cotangent, spots, "up")
    came_up = hop(away_up, dc=1)
    away_down = blocks(after(cotangent, away_up), spots, "down")
    came_down = hop(after(away_down, came_up), dc=1)
    sent_up, up_y0, own_y1, up_straight, up_cross = blocks(
        after(cotangent, away_down), spots, "up", came_up
    )
    below = hop(sent_up, dz=1)
    up_crossed = hop(up_cross, dy=1)
    sent_down, down_y1, own_y0, down_straight, down_cross = blocks(
        after(cotangent, up_y0), spots, "down", came_down
    )
    above = hop(sent_down, dz=-1)
    down_crossed = hop(down_cross, dy=1)

    below, above, up_crossed, down_crossed = lax.optimization_barrier(
        (below, above, up_crossed, down_crossed)
    )
    half = up_straight.shape[1] // 2

    def both(straight, crossed):
        total = add(straight, crossed)
        return total[:half], total[half:]

    two_up, two_down = both(up_straight[0], down_crossed[0])
    up_up, up_down = both(up_straight[1], up_crossed[0])
    down_up, down_down = both(down_straight[0], down_crossed[1])
    sent_up = jnp.concatenate([add(up_y0, below[0]), two_up, up_down]).astype(bf16)
    sent_down = jnp.concatenate([add(down_y1, above[0]), two_down, down_up]).astype(bf16)
    below_again, above_again = hop(sent_up, dz=1), hop(sent_down, dz=-1)
    own_second = add(down_straight[1], up_crossed[1])

    below_again, above_again, own_second = lax.optimization_barrier(
        (below_again, above_again, own_second)
    )
    sent = add(own_y1, below[1], above_again[:FIRST]).astype(bf16)
    second_up = add(up_up, below_again[FIRST : FIRST + half]).astype(bf16)
    second_down = add(down_down, above_again[FIRST : FIRST + half]).astype(bf16)
    crossed = hop(sent, dy=1)
    last_below, last_above = hop(second_up, dz=1), hop(second_down, dz=-1)

    second_sum = own_second + jnp.concatenate(
        [add(last_below, above_again[FIRST + half :]), add(below_again[FIRST + half :], last_above)]
    )
    first_sum = add(own_y0, below_again[:FIRST], above[1], crossed)
    return first_sum, second_sum, sent


def per_device(inputs, grad_keys, local_weights, feedback, base, momentum, warm_start):
    tokens_in = inputs[0]
    cotangent = grad_keys[0]
    weights = local_weights[0]
    wide = tokens_in.shape[1]
    rep_size, fsdp_size = lax.axis_size("rep"), lax.axis_size("fsdp")
    everyone = rep_size * fsdp_size
    rows, width = weights.shape
    rank = warm_start.shape[1]
    my_rep = lax.axis_index("rep")
    block_width = base.shape[1]
    everything = ("rep", "fsdp")
    spots = all_spots()

    first_sum, second_sum, sent = reduce_terms(tokens_in, cotangent, spots)

    lane = lax.broadcasted_iota(jnp.int32, (1, width), 1)
    mine = lane // block_width == my_rep
    drift = feedback[0].astype(f32) - weights.astype(f32)
    own_base = jnp.where(mine, jnp.tile(rep_size * base, (1, width // block_width)), 0.0)
    moved = drift + inner_rate * jnp.concatenate([first_sum, second_sum])
    mean = scatter_sum(moved + own_base, "rep", rep_size) / rep_size

    def product_shapes():
        return (width, 2 * rank), (rows // rep_size, rank)

    packed, left_part = small_call(first_kernel, product_shapes(), mean, warm_start)
    full_base = lax.all_gather(after(base, mean), "rep", axis=1, tiled=True)
    every_row = lax.all_gather(local_weights, "fsdp", axis=1, tiled=True)[0]
    grad = grad_of_inputs(after(cotangent, packed), every_row)
    for repeat in range(ROUNDS - 1):
        share = scatter_sum(packed, everything, everyone)
        summed = gather_rows(share, everything, everyone)
        summed, grad = lax.optimization_barrier((summed, grad))
        packed, left_part = small_call(
            functools.partial(round_kernel, False), product_shapes(), summed, mean
        )
    share = scatter_sum(packed, everything, everyone)
    summed = gather_rows(share, everything, everyone)
    left = gather_rows(after(left_part, share), "rep", rep_size)
    factor, inverse = small_call(
        functools.partial(round_kernel, True), ((width, rank), (rank, rank)), summed, mean
    )
    orthonormal = dot(left, inverse, ((1,), (1,)))
    approx = dot(orthonormal, factor, ((1,), (1,)))
    feedback_out = (full_base + moved - approx)[None]
    column_block = lax.dynamic_slice_in_dim(approx, my_rep * block_width, block_width, 1)
    momentum_out = momentum_keep * momentum + column_block
    base_out = base - outer_rate * (column_block + momentum_keep * momentum_out)
    return (grad[None], feedback_out, base_out, momentum_out, factor)


def solution(mesh):
    split = P("rep", "fsdp", None)
    shared = P("fsdp", "rep")
    return jax.shard_map(
        per_device,
        mesh=mesh,
        in_specs=(split, split, split, split, shared, shared, P()),
        out_specs=(split, split, shared, shared, P()),
        check_vma=False,
    )
```

time: 397 us -> 338 us (0.85)
  Pallas kernels: 31.6 us -> 62.9 us
  other arithmetic: 49 us -> 19.7 us
  blocking collectives: 86.2 us -> 58.9 us
  waiting for transfers between devices: 108 us -> 131 us
  matrix products: 23.8 us -> 3.11 us
  starting transfers between devices: 52.3 us -> 32.8 us
  local copies, waits for them, and re-layouts: 30.5 us -> 13.5 us
    ppermute x20 -> x11, waiting for transfers between devices: 46.1 us -> 103 us  [hop(): return lax.ppermute(value, 'fsdp', pairs)]
    all_to_all x1, blocking collectives: 49.1 us -> 7.83 us  [gather_rows(): return lax.all_to_all(sent, axes, 0, 0, tiled=True)]
    pallas_call x6 -> x8, Pallas kernels: 31.6 us -> 62.9 us  [the longest x4 30.9 us: term_blocks(): pl.pallas_call(kernel, grid_spec=pltpu.PrefetchScalarGridSpec(num_scalar_...]
    all_to_all x3 -> x1, waiting for transfers between devices: 44.2 us -> 16 us  [scatter_sum(): got = lax.all_to_all(value, axes, 0, 0, tiled=True)]
    another operation x12 -> x2, other arithmetic: 24.3 us -> 0.61 us  [the longest x6 13.1 us: per_device(): lower_factor = jnp.linalg.cholesky(summed[:rank, rank:])]
    unnamed x55 -> x40, local copies, waits for them, and re-layouts: 28.5 us -> 8.4 us
    dot_general x1 -> x0, matrix products: 17 us -> none  [per_device(): lax.dot_general(cotangent, every_row, (((1,), (1,)), ((), ())), preferred...]
    ppermute x20 -> x11, starting transfers between devices: 29.3 us -> 12.6 us  [hop(): return lax.ppermute(value, 'fsdp', pairs)]
  transfers between devices with their start and end apart: 27 -> 16, of which waited for: 15 -> 12; matrix products, arithmetic and copies ran while one was open for 14% -> 7% of each run, Pallas kernels for 7% -> 19%
where the time goes in v3:
time: 338 us; the launch traced here: 337 us
  waiting for transfers between devices  131 us (39%)
  Pallas kernels  62.9 us (19%)
  blocking collectives  58.9 us (17%)
  starting transfers between devices  32.8 us (10%)
  other arithmetic  19.7 us (6%)
  between operations  14.4 us (4%)
  local copies, waits for them, and re-layouts  13.5 us (4%)
    ppermute x11, waiting for transfers between devices, hop(): return lax.ppermute(value, 'fsdp', pairs)  103 us
    all_to_all x2, blocking collectives, scatter_sum(): got = lax.all_to_all(value, axes, 0, 0, tiled=True)  51.1 us
    pallas_call x4, Pallas kernels, term_blocks(): pl.pallas_call(kernel, grid_spec=pltpu.PrefetchScalarGridSpec(num_scalar_...  30.9 us
    pallas_call x3, Pallas kernels, small_call(): pl.pallas_call(kernel, out_shape=[jax.ShapeDtypeStruct(shape, f32) for sh...  16.3 us
    all_to_all x1, waiting for transfers between devices, scatter_sum(): got = lax.all_to_all(value, axes, 0, 0, tiled=True)  16 us
    pallas_call x1, Pallas kernels, grad_of_inputs(): pl.pallas_call(grad_kernel, grid=(wide // rows,), in_specs=[pl.BlockSpec(...  15.7 us
    ppermute x11, starting transfers between devices, hop(): return lax.ppermute(value, 'fsdp', pairs)  12.6 us
    all_to_all x2, starting transfers between devices, gather_rows(): return lax.all_to_all(sent, axes, 0, 0, tiled=True)  12.3 us
  transfers between devices with their start and end apart: 16, of which 12 were waited for; matrix products, arithmetic and copies ran while one was open for 7% of the time, Pallas kernels for 19%

profile of v3, /device:TPU:1, one launch (start us, length us, event | category | flops | bytes accessed | tf_op | source)
XLA Modules:
  0.0 336.6 jit_solution(5833273854223627453)
XLA Ops:
  9.2 6.8 %shard_map.119 = bf16[4,512,1024]{2,1,0:T(8,128)(2,1)} custom-call(s32[16]{0:T(128)} %dynamic-slice_bitcast_fusion.spots, bf16[512,8192]{1,0:T(8,128)(2,1)} %bitcast.64, bf16[512,1024]{1,0:T(8,128)(2,1)} %bitcast.68), custom_call_target="tpu_custom_call" | custom-call | flops 2147483648 | bytes 10485760 | tf_op jit(solution)/shard_map/pallas_call | solution.py:130
  17.4 6.9 %shard_map.120 = bf16[4,512,1024]{2,1,0:T(8,128)(2,1)} custom-call(s32[16]{0:T(128)} %dynamic-slice_bitcast_fusion.spots, bf16[512,8192]{1,0:T(8,128)(2,1)} %bitcast.65, bf16[512,1024]{1,0:T(8,128)(2,1)} %bitcast.69), custom_call_target="tpu_custom_call" | custom-call | flops 2147483648 | bytes 10485760 | tf_op jit(solution)/shard_map/pallas_call | solution.py:130
  24.9 8.7 %shard_map.121 = (bf16[2,384,1024]{2,1,0:T(8,128)(2,1)}, bf16[384,1024]{1,0:T(8,128)(2,1)}, bf16[384,1024]{1,0:T(8,128)(2,1)}, bf16[2,128,1024]{2,1,0:T(8,128)(2,1)}, bf16[2,128,1024]{2,1,0:T(8,128)(2,1)}) custom-call(s32[16]{0:T(128)} %dynamic-slice_bitcast_fusion.spots, bf16[512,8192]{1,0:T(8,128)(2,1)} %bitcast.66, bf16[512,1024]{1,0:T(8,128)(2,1)} %bitcast.70, ...), custom_call_target="tpu_custom_call" | custom-call | flops 2147483648 | bytes 10485760 | tf_op jit(solution)/shard_map/pallas_call | solution.py:130
  37.3 8.5 %shard_map.122 = (bf16[2,384,1024]{2,1,0:T(8,128)(2,1)}, bf16[384,1024]{1,0:T(8,128)(2,1)}, bf16[384,1024]{1,0:T(8,128)(2,1)}, bf16[2,128,1024]{2,1,0:T(8,128)(2,1)}, bf16[2,128,1024]{2,1,0:T(8,128)(2,1)}) custom-call(s32[16]{0:T(128)} %dynamic-slice_bitcast_fusion.spots, bf16[512,8192]{1,0:T(8,128)(2,1)} %bitcast.67, bf16[512,1024]{1,0:T(8,128)(2,1)} %bitcast.71, ...), custom_call_target="tpu_custom_call" | custom-call | flops 2147483648 | bytes 10485760 | tf_op jit(solution)/shard_map/pallas_call | solution.py:130
  51.0 11.6 %collective-permute-done.4 = bf16[2,128,1024]{2,1,0:T(8,128)(2,1)S(1)} collective-permute-done((bf16[2,128,1024]{2,1,0:T(8,128)(2,1)S(1)}, bf16[2,128,1024]{2,1,0:T(8,128)(2,1)S(1)}, u32[]{:S(2)}, u32[]{:S(2)}) %collective-permute-start.4) | collective-permute-done | bytes 524320 | tf_op jit(solution)/shard_map/ppermute | solution.py:33
  62.5 33.7 %collective-permute-done.2 = bf16[2,384,1024]{2,1,0:T(8,128)(2,1)S(1)} collective-permute-done((bf16[2,384,1024]{2,1,0:T(8,128)(2,1)}, bf16[2,384,1024]{2,1,0:T(8,128)(2,1)S(1)}, u32[]{:S(2)}, u32[]{:S(2)}) %collective-permute-start.2) | collective-permute-done | bytes 1572896 | tf_op jit(solution)/shard_map/ppermute | solution.py:33
  96.3 4.4 %collective-permute-done.3 = bf16[2,384,1024]{2,1,0:T(8,128)(2,1)S(1)} collective-permute-done((bf16[2,384,1024]{2,1,0:T(8,128)(2,1)}, bf16[2,384,1024]{2,1,0:T(8,128)(2,1)S(1)}, u32[]{:S(2)}, u32[]{:S(2)}) %collective-permute-start.3) | collective-permute-done | bytes 1572896 | tf_op jit(solution)/shard_map/ppermute | solution.py:33
  103.0 3.5 %collective-permute-start.7 = (bf16[512,1024]{1,0:T(8,128)(2,1)S(1)}, bf16[512,1024]{1,0:T(8,128)(2,1)S(1)}, u32[]{:S(2)}, u32[]{:S(2)}) collective-permute-start(bf16[512,1024]{1,0:T(8,128)(2,1)S(1)} %pad_maximum_fusion.1), channel_id=1, source_target_pairs={{0,6},{1,7},{2,0},{3,1},{4,2},{5,3},{6,4},{7,5},{8,14},{9,15},{10,... | collective-permute-start | bytes 3145736 | tf_op jit(solution)/shard_map/ppermute | solution.py:33
  109.8 30.7 %collective-permute-done.7 = bf16[512,1024]{1,0:T(8,128)(2,1)S(1)} collective-permute-done((bf16[512,1024]{1,0:T(8,128)(2,1)S(1)}, bf16[512,1024]{1,0:T(8,128)(2,1)S(1)}, u32[]{:S(2)}, u32[]{:S(2)}) %collective-permute-start.7) | collective-permute-done | bytes 1048608 | tf_op jit(solution)/shard_map/ppermute | solution.py:33
  140.5 6.1 %collective-permute-done.6 = bf16[512,1024]{1,0:T(8,128)(2,1)S(1)} collective-permute-done((bf16[512,1024]{1,0:T(8,128)(2,1)S(1)}, bf16[512,1024]{1,0:T(8,128)(2,1)S(1)}, u32[]{:S(2)}, u32[]{:S(2)}) %collective-permute-start.6) | collective-permute-done | bytes 1048608 | tf_op jit(solution)/shard_map/ppermute | solution.py:33
  148.5 3.3 collective-permute-done.9
  157.9 9.8 %collective-permute-done.8 = bf16[384,1024]{1,0:T(8,128)(2,1)} collective-permute-done((bf16[384,1024]{1,0:T(8,128)(2,1)}, bf16[384,1024]{1,0:T(8,128)(2,1)}, u32[]{:S(2)}, u32[]{:S(2)}) %collective-permute-start.8) | collective-permute-done | bytes 786464 | tf_op jit(solution)/shard_map/ppermute | solution.py:33
  173.1 28.1 %all_to_all.50 = f32[8,64,1024]{2,1,0:T(8,128)} all-to-all(f32[8,64,1024]{2,1,0:T(8,128)S(1)} %select_add_fusion), channel_id=1, replica_groups=mesh['rep'=8,'fsdp'=16] {'rep'}, dimensions={0} | all-to-all | bytes 4194304 | tf_op jit(solution)/shard_map/all_to_all | solution.py:43
  205.1 7.8 %all-to-all-start.1 = ((f32[128,8,128]{2,1,0:T(8,128)}), f32[128,8,128]{2,1,0:T(8,128)S(1)}, u32[]{:S(2)}, u32[]{:S(2)}) async-start(f32[128,8,128]{2,1,0:T(8,128)} %bitcast.16), calls=%async_computation.1 | async-start | bytes 1048576 | tf_op jit(solution)/shard_map/all_to_all | solution.py:43
  212.9 16.0 %all-to-all-done.1 = f32[128,8,128]{2,1,0:T(8,128)S(1)} async-done(((f32[128,8,128]{2,1,0:T(8,128)}), f32[128,8,128]{2,1,0:T(8,128)S(1)}, u32[]{:S(2)}, u32[]{:S(2)}) %all-to-all-start.1) | async-done | bytes 524320 | tf_op jit(solution)/shard_map/all_to_all | solution.py:43
  229.9 5.8 %all-to-all-start.2 = ((f32[128,8,128]{2,1,0:T(8,128)}), f32[128,8,128]{2,1,0:T(8,128)S(1)}, u32[]{:S(2)}, u32[]{:S(2)}) async-start(f32[128,8,128]{2,1,0:T(8,128)} %broadcast_in_dim.38), calls=%async_computation.2 | async-start | bytes 1048576 | tf_op jit(solution)/shard_map/all_to_all | solution.py:50
  235.8 15.7 %shard_map.124 = bf16[512,8192]{1,0:T(8,128)(2,1)} custom-call(bf16[512,1024]{1,0:T(8,128)(2,1)} %bitcast.72, bf16[8192,1024]{1,0:T(8,128)(2,1)} %bitcast.76), custom_call_target="tpu_custom_call" | custom-call | flops 8589934592 | bytes 25165824 | tf_op jit(solution)/shard_map/pallas_call | solution.py:156
  251.8 8.1 %shard_map.125 = (f32[1024,128]{1,0:T(8,128)S(1)}, f32[64,64]{1,0:T(8,128)S(1)}) custom-call(f32[1024,128]{1,0:T(8,128)S(1)} %bitcast.62, f32[64,1024]{1,0:T(8,128)S(1)} %broadcast_multiply_fusion.mean), custom_call_target="tpu_custom_call" | custom-call | flops 1000000000 | bytes 2097152 | tf_op jit(solution)/shard_map/pallas_call | solution.py:216
  259.9 23.0 %all_to_all.51 = f32[128,8,128]{2,1,0:T(8,128)S(1)} all-to-all(f32[128,8,128]{2,1,0:T(8,128)S(1)} %bitcast.63), channel_id=1, replica_groups=mesh['rep'=8,'fsdp'=16] {'rep','fsdp'}, dimensions={0} | all-to-all | bytes 1048576 | tf_op jit(solution)/shard_map/all_to_all | solution.py:43
  283.2 7.8 %all_to_all.52 = f32[8,1,4096]{2,1,0:T(1,128)S(1)} all-to-all(f32[8,1,4096]{2,1,0:T(1,128)S(1)} %reshape.131), channel_id=1, replica_groups=mesh['rep'=8,'fsdp'=16] {'rep'}, dimensions={0} | all-to-all | bytes 262144 | tf_op jit(solution)/shard_map/all_to_all | solution.py:50
  291.8 6.6 %all-to-all-start.5 = ((f32[128,8,128]{2,1,0:T(8,128)}), f32[128,8,128]{2,1,0:T(8,128)S(1)}, u32[]{:S(2)}, u32[]{:S(2)}) async-start(f32[128,8,128]{2,1,0:T(8,128)} %broadcast_in_dim.41), calls=%async_computation.5 | async-start | bytes 1048576 | tf_op jit(solution)/shard_map/all_to_all | solution.py:50
  300.7 11.4 %all-to-all-done.5 = f32[128,8,128]{2,1,0:T(8,128)S(1)} async-done(((f32[128,8,128]{2,1,0:T(8,128)}), f32[128,8,128]{2,1,0:T(8,128)S(1)}, u32[]{:S(2)}, u32[]{:S(2)}) %all-to-all-start.5) | async-done | bytes 524320 | tf_op jit(solution)/shard_map/all_to_all | solution.py:50
  312.1 6.4 %shard_map.126 = (f32[1024,64]{1,0:T(8,128)S(1)}, f32[64,64]{1,0:T(8,128)S(1)}) custom-call(f32[1024,128]{1,0:T(8,128)S(1)} %bitcast.61, f32[64,1024]{1,0:T(8,128)S(1)} %broadcast_multiply_fusion.mean), custom_call_target="tpu_custom_call" | custom-call | flops 1000000000 | bytes 2097152 | tf_op jit(solution)/shard_map/pallas_call | solution.py:216
  324.8 5.0 %fusion.2 = f32[1,512,1024]{2,1,0:T(8,128)} fusion(f32[512,1024]{1,0:T(8,128)} %copy-done, f32[512,1024]{1,0:T(8,128)} %all-gather.5.cloned.1.call-done, bf16[1,512,1024]{2,1,0:T(8,128)(2,1)} %param.10, bf16[1,512,1024]{2,1,0:T(8,128)(2,1)} %param.11, f32[128,1024]{1,0:T(8,128)S(1)} %maximum_add_fusion, f32[384,1024]{1,0:T(8,128)S(1)} %fusion.5), kind=kLoop, calls=%fused_computation.4 | loop fusion | flops 4194304 | bytes 10485760 | tf_op jit(solution)/shard_map/broadcast_in_dim | solution.py:328
  (96 shorter events, 46.3 us)
Async XLA Ops:
  7.2 228.6 %all-gather.3.cloned.1.call-start = ((), (), s32[]{:S(2)}) async-start(), calls=%async_computation.6 | async-start | bytes 17825792 | tf_op jit(solution)/shard_map/all_gather | solution.py:311
  7.9 316.9 %all-gather.5.cloned.1.call-start = ((), (), s32[]{:S(2)}) async-start(), calls=%async_computation.7 | async-start | bytes 2359296 | tf_op jit(solution)/shard_map/all_gather | solution.py:310
  15.9 8.5 %collective-permute-start = (bf16[4,512,1024]{2,1,0:T(8,128)(2,1)}, bf16[4,512,1024]{2,1,0:T(8,128)(2,1)}, u32[]{:S(2)}, u32[]{:S(2)}) collective-permute-start(bf16[4,512,1024]{2,1,0:T(8,128)(2,1)} %shard_map.119), channel_id=1, source_target_pairs={{0,1},{1,0},{2,3},{3,2},{4,5},{5,4},{6,7},{7,6},{8,9},{9,8},{10,11... | collective-permute-start | bytes 12582920 | tf_op jit(solution)/shard_map/ppermute | solution.py:33
  24.5 10.8 %collective-permute-start.1 = (bf16[4,512,1024]{2,1,0:T(8,128)(2,1)}, bf16[4,512,1024]{2,1,0:T(8,128)(2,1)S(1)}, u32[]{:S(2)}, u32[]{:S(2)}) collective-permute-start(bf16[4,512,1024]{2,1,0:T(8,128)(2,1)} %shard_map.120), channel_id=1, source_target_pairs={{0,1},{1,0},{2,3},{3,2},{4,5},{5,4},{6,7},{7,6},{8,9},{9,8},{10,11... | collective-permute-start | bytes 12582920 | tf_op jit(solution)/shard_map/ppermute | solution.py:33
  33.6 14.3 %copy-start.17 = (bf16[2,128,1024]{2,1,0:T(8,128)(2,1)S(1)}, bf16[2,128,1024]{2,1,0:T(8,128)(2,1)}, u32[]{:S(2)}) copy-start(bf16[2,128,1024]{2,1,0:T(8,128)(2,1)} %get-tuple-element.44) | copy-start | bytes 1572868
  33.6 67.1 %copy-start.14 = (bf16[2,128,1024]{2,1,0:T(8,128)(2,1)S(1)}, bf16[2,128,1024]{2,1,0:T(8,128)(2,1)}, u32[]{:S(2)}) copy-start(bf16[2,128,1024]{2,1,0:T(8,128)(2,1)} %get-tuple-element.47) | copy-start | bytes 1572868
  33.6 62.7 %collective-permute-start.2 = (bf16[2,384,1024]{2,1,0:T(8,128)(2,1)}, bf16[2,384,1024]{2,1,0:T(8,128)(2,1)S(1)}, u32[]{:S(2)}, u32[]{:S(2)}) collective-permute-start(bf16[2,384,1024]{2,1,0:T(8,128)(2,1)} %get-tuple-element.42), channel_id=1, source_target_pairs={{0,2},{1,3},{2,4},{3,5},{4,6},{5,7},{6,0},{7,1},{8,10},{9,11},{10,... | collective-permute-start | bytes 4718600 | tf_op jit(solution)/shard_map/ppermute | solution.py:33
  45.8 54.9 %collective-permute-start.3 = (bf16[2,384,1024]{2,1,0:T(8,128)(2,1)}, bf16[2,384,1024]{2,1,0:T(8,128)(2,1)S(1)}, u32[]{:S(2)}, u32[]{:S(2)}) collective-permute-start(bf16[2,384,1024]{2,1,0:T(8,128)(2,1)} %get-tuple-element.43), channel_id=1, source_target_pairs={{0,6},{1,7},{2,0},{3,1},{4,2},{5,3},{6,4},{7,5},{8,14},{9,15},{10,... | collective-permute-start | bytes 4718600 | tf_op jit(solution)/shard_map/ppermute | solution.py:33
  47.9 14.7 %collective-permute-start.4 = (bf16[2,128,1024]{2,1,0:T(8,128)(2,1)S(1)}, bf16[2,128,1024]{2,1,0:T(8,128)(2,1)S(1)}, u32[]{:S(2)}, u32[]{:S(2)}) collective-permute-start(bf16[2,128,1024]{2,1,0:T(8,128)(2,1)S(1)} %copy-done.17), channel_id=1, source_target_pairs={{0,8},{1,9},{2,10},{3,11},{4,12},{5,13},{6,14},{7,15},{8,0},{9,1},... | collective-permute-start | bytes 1572872 | tf_op jit(solution)/shard_map/ppermute | solution.py:33
  50.9 45.4 %collective-permute-start.5 = (bf16[2,128,1024]{2,1,0:T(8,128)(2,1)}, bf16[2,128,1024]{2,1,0:T(8,128)(2,1)S(1)}, u32[]{:S(2)}, u32[]{:S(2)}) collective-permute-start(bf16[2,128,1024]{2,1,0:T(8,128)(2,1)} %get-tuple-element.45), channel_id=1, source_target_pairs={{0,8},{1,9},{2,10},{3,11},{4,12},{5,13},{6,14},{7,15},{8,0},{9,1},... | collective-permute-start | bytes 1572872 | tf_op jit(solution)/shard_map/ppermute | solution.py:33
  103.0 37.5 %collective-permute-start.7 = (bf16[512,1024]{1,0:T(8,128)(2,1)S(1)}, bf16[512,1024]{1,0:T(8,128)(2,1)S(1)}, u32[]{:S(2)}, u32[]{:S(2)}) collective-permute-start(bf16[512,1024]{1,0:T(8,128)(2,1)S(1)} %pad_maximum_fusion.1), channel_id=1, source_target_pairs={{0,6},{1,7},{2,0},{3,1},{4,2},{5,3},{6,4},{7,5},{8,14},{9,15},{10,... | collective-permute-start | bytes 3145736 | tf_op jit(solution)/shard_map/ppermute | solution.py:33
  106.9 39.8 %copy-start.11 = (bf16[384,1024]{1,0:T(8,128)(2,1)S(1)}, bf16[384,1024]{1,0:T(8,128)(2,1)}, u32[]{:S(2)}) copy-start(bf16[384,1024]{1,0:T(8,128)(2,1)} %get-tuple-element.54) | copy-start | bytes 2359300
  107.0 39.7 %collective-permute-start.6 = (bf16[512,1024]{1,0:T(8,128)(2,1)S(1)}, bf16[512,1024]{1,0:T(8,128)(2,1)S(1)}, u32[]{:S(2)}, u32[]{:S(2)}) collective-permute-start(bf16[512,1024]{1,0:T(8,128)(2,1)S(1)} %pad_maximum_fusion), channel_id=1, source_target_pairs={{0,2},{1,3},{2,4},{3,5},{4,6},{5,7},{6,0},{7,1},{8,10},{9,11},{10,... | collective-permute-start | bytes 3145736 | tf_op jit(solution)/shard_map/ppermute | solution.py:33
  146.6 5.9 %copy-start.10 = (bf16[512,1024]{1,0:T(8,128)(2,1)}, bf16[512,1024]{1,0:T(8,128)(2,1)S(1)}, u32[]{:S(2)}) copy-start(bf16[512,1024]{1,0:T(8,128)(2,1)S(1)} %collective-permute-done.6) | copy-start | bytes 3145732
  146.7 5.1 %collective-permute-start.9 = (bf16[64,1024]{1,0:T(8,128)(2,1)S(1)}, bf16[64,1024]{1,0:T(8,128)(2,1)S(1)}, u32[]{:S(2)}, u32[]{:S(2)}) collective-permute-start(bf16[64,1024]{1,0:T(8,128)(2,1)S(1)} %fusion.11), channel_id=1, source_target_pairs={{0,2},{1,3},{2,4},{3,5},{4,6},{5,7},{6,0},{7,1},{8,10},{9,11},{10,... | collective-permute-start | bytes 393224 | tf_op jit(solution)/shard_map/ppermute | solution.py:33
  146.8 5.7 %copy-start.6 = (f32[512,128]{1,0:T(8,128)S(1)}, f32[512,128]{1,0:T(8,128)}, u32[]{:S(2)}) copy-start(f32[512,128]{1,0:T(8,128)} %param.12) | copy-start | bytes 786436
  148.1 19.6 %collective-permute-start.8 = (bf16[384,1024]{1,0:T(8,128)(2,1)}, bf16[384,1024]{1,0:T(8,128)(2,1)}, u32[]{:S(2)}, u32[]{:S(2)}) collective-permute-start(bf16[384,1024]{1,0:T(8,128)(2,1)} %fusion.4), channel_id=1, source_target_pairs={{0,8},{1,9},{2,10},{3,11},{4,12},{5,13},{6,14},{7,15},{8,0},{9,1},... | collective-permute-start | bytes 2359304 | tf_op jit(solution)/shard_map/ppermute | solution.py:33
  152.5 4.4 %collective-permute-start.10 = (bf16[64,1024]{1,0:T(8,128)(2,1)}, bf16[64,1024]{1,0:T(8,128)(2,1)S(1)}, u32[]{:S(2)}, u32[]{:S(2)}) collective-permute-start(bf16[64,1024]{1,0:T(8,128)(2,1)} %get-tuple-element.75), channel_id=1, source_target_pairs={{0,6},{1,7},{2,0},{3,1},{4,2},{5,3},{6,4},{7,5},{8,14},{9,15},{10,... | collective-permute-start | bytes 393224 | tf_op jit(solution)/shard_map/ppermute | solution.py:33
  154.2 13.6 %copy-start.9 = (bf16[2,384,1024]{2,1,0:T(8,128)(2,1)S(1)}, bf16[2,384,1024]{2,1,0:T(8,128)(2,1)}, u32[]{:S(2)}) copy-start(bf16[2,384,1024]{2,1,0:T(8,128)(2,1)} %copy-done.8) | copy-start | bytes 4718596
  205.1 23.9 %all-to-all-start.1 = ((f32[128,8,128]{2,1,0:T(8,128)}), f32[128,8,128]{2,1,0:T(8,128)S(1)}, u32[]{:S(2)}, u32[]{:S(2)}) async-start(f32[128,8,128]{2,1,0:T(8,128)} %bitcast.16), calls=%async_computation.1 | async-start | bytes 1048576 | tf_op jit(solution)/shard_map/all_to_all | solution.py:43
  229.9 21.9 %all-to-all-start.2 = ((f32[128,8,128]{2,1,0:T(8,128)}), f32[128,8,128]{2,1,0:T(8,128)S(1)}, u32[]{:S(2)}, u32[]{:S(2)}) async-start(f32[128,8,128]{2,1,0:T(8,128)} %broadcast_in_dim.38), calls=%async_computation.2 | async-start | bytes 1048576 | tf_op jit(solution)/shard_map/all_to_all | solution.py:50
  291.8 20.3 %all-to-all-start.5 = ((f32[128,8,128]{2,1,0:T(8,128)}), f32[128,8,128]{2,1,0:T(8,128)S(1)}, u32[]{:S(2)}, u32[]{:S(2)}) async-start(f32[128,8,128]{2,1,0:T(8,128)} %broadcast_in_dim.41), calls=%async_computation.5 | async-start | bytes 1048576 | tf_op jit(solution)/shard_map/all_to_all | solution.py:50
  318.5 5.4 %copy-start.7 = (f32[512,128]{1,0:T(8,128)S(1)}, f32[512,128]{1,0:T(8,128)}, u32[]{:S(2)}) copy-start(f32[512,128]{1,0:T(8,128)} %param.12) | copy-start | bytes 786436
  318.5 5.4 %copy-start.16 = (f32[512,128]{1,0:T(8,128)S(1)}, f32[512,128]{1,0:T(8,128)}, u32[]{:S(2)}) copy-start(f32[512,128]{1,0:T(8,128)} %param.13) | copy-start | bytes 786436
  (10 other events, 19.4 us)
Sparse Core Ops, SparseCore 0:
  10.5 137.4 all-gather.2
  203.2 50.7 all-gather.4

commit v4 on v3

--- a/solution.py
+++ b/solution.py
@@ -20,7 +20,7 @@
 bf16 = jnp.bfloat16
 
 NZ = 4
-FIRST = 384
+FIRST = 320
 PLACES = [(y, z, c) for y in range(2) for z in range(NZ) for c in range(2)]
 
 
@@ -142,33 +142,83 @@
     )(spots, *operands)
 
 
-def grad_kernel(cotangent, block, out):
+def grad_kernel(cotangent, block, *refs):
     product = lax.dot_general(
         cotangent[...], block[...], (((1,), (1,)), ((), ())), preferred_element_type=f32
     )
-    out[...] = (inv_root * product).astype(bf16)
-
-
-def grad_of_inputs(cotangent, every_row):
+    refs[-1][...] = (inv_root * product).astype(bf16)
+
+
+def half_of_grad(cotangent, every_row, which, before=None):
     tokens, depth = cotangent.shape
     wide = every_row.shape[0]
     rows = 1024
+    steps = wide // rows // 2
+    in_specs = [
+        pl.BlockSpec((tokens, depth), lambda i: (0, 0)),
+        pl.BlockSpec((rows, depth), lambda i: (i + which * steps, 0)),
+    ]
+    operands = [cotangent, every_row]
+    aliases = {}
+    if before is not None:
+        in_specs.append(pl.BlockSpec(memory_space=pl.ANY))
+        aliases = {len(operands): 0}
+        operands.append(before)
     return pl.pallas_call(
         grad_kernel,
-        grid=(wide // rows,),
-        in_specs=[
-            pl.BlockSpec((tokens, depth), lambda i: (0, 0)),
-            pl.BlockSpec((rows, depth), lambda i: (i, 0)),
-        ],
-        out_specs=pl.BlockSpec((tokens, rows), lambda i: (0, i)),
+        grid=(steps,),
+        in_specs=in_specs,
+        out_specs=pl.BlockSpec((tokens, rows), lambda i: (0, i + which * steps)),
         out_shape=jax.ShapeDtypeStruct((tokens, wide), bf16),
+        input_output_aliases=aliases,
         compiler_params=pltpu.CompilerParams(vmem_limit_bytes=56 << 20),
         cost_estimate=pl.CostEstimate(
-            flops=2 * tokens * depth * wide,
-            bytes_accessed=2 * wide * (depth + tokens),
+            flops=tokens * depth * wide,
+            bytes_accessed=wide * (depth + tokens),
             transcendentals=0,
         ),
-    )(cotangent, every_row)
+    )(*operands)
+
+
+def final_kernel(
+    my_rep, left, inverse, factor, moved, full_base, base, momentum, feedback_out, base_out, momentum_out
+):
+    orthonormal = dot(left[:, : inverse.shape[0]], inverse[...], ((1,), (1,)))
+    approx = dot(orthonormal, factor[...], ((1,), (1,)))
+    feedback_out[...] = full_base[...] + moved[...] - approx
+    width = base.shape[1]
+    columns = factor[pl.ds(pl.multiple_of(my_rep[0] * width, width), width), :]
+    approx = dot(orthonormal, columns, ((1,), (1,)))
+    moment = momentum_keep * momentum[...] + approx
+    momentum_out[...] = moment
+    base_out[...] = base[...] - outer_rate * (approx + momentum_keep * moment)
+
+
+def final_outputs(my_rep, left, inverse, factor, moved, full_base, base, momentum):
+    rows, width = moved.shape
+    step = 128
+
+    def by_rows(array):
+        return pl.BlockSpec((step, array.shape[1]), lambda i, my_rep: (i, 0))
+
+    def whole(array):
+        return pl.BlockSpec(array.shape, lambda i, my_rep: (0, 0))
+
+    return pl.pallas_call(
+        final_kernel,
+        grid_spec=pltpu.PrefetchScalarGridSpec(
+            num_scalar_prefetch=1,
+            grid=(rows // step,),
+            in_specs=[
+                by_rows(left), whole(inverse), whole(factor), by_rows(moved), by_rows(full_base),
+                by_rows(base), by_rows(momentum),
+            ],
+            out_specs=[by_rows(moved), by_rows(base), by_rows(momentum)],
+        ),
+        out_shape=[jax.ShapeDtypeStruct(array.shape, f32) for array in (moved, base, momentum)],
+        compiler_params=pltpu.CompilerParams(vmem_limit_bytes=32 << 20),
+        cost_estimate=pl.CostEstimate(flops=10**9, bytes_accessed=8 << 20, transcendentals=0),
+    )(my_rep.reshape(1).astype(jnp.int32), left, inverse, factor, moved, full_base, base, momentum)
 
 
 def inverse_of_lower_factor(gram):
@@ -201,7 +251,7 @@
 def product_kernel_body(mean, factor, packed, left):
     rank = factor.shape[1]
     left_part = dot(mean, factor)
-    left[...] = left_part
+    left[...] = jnp.concatenate([left_part, left_part], axis=1)
     gram = dot(left_part, left_part, ((0,), (0,)))
     raised = dot(mean, left_part, ((0,), (0,)))
     packed[:, :rank] = raised
@@ -230,7 +280,7 @@
     return total
 
 
-def reduce_terms(tokens_in, cotangent, spots):
+def reduce_terms(tokens_in, cotangent, spots, early_of):
     blocks = functools.partial(term_blocks, tokens_in)
     away_up = blocks(cotangent, spots, "up")
     came_up = hop(away_up, dc=1)
@@ -264,8 +314,8 @@
     below_again, above_again = hop(sent_up, dz=1), hop(sent_down, dz=-1)
     own_second = add(down_straight[1], up_crossed[1])
 
-    below_again, above_again, own_second = lax.optimization_barrier(
-        (below_again, above_again, own_second)
+    early, below_again, above_again, own_second = lax.optimization_barrier(
+        (early_of(sent_up, sent_down), below_again, above_again, own_second)
     )
     sent = add(own_y1, below[1], above_again[:FIRST]).astype(bf16)
     second_up = add(up_up, below_again[FIRST : FIRST + half]).astype(bf16)
@@ -277,7 +327,7 @@
         [add(last_below, above_again[FIRST + half :]), add(below_again[FIRST + half :], last_above)]
     )
     first_sum = add(own_y0, below_again[:FIRST], above[1], crossed)
-    return first_sum, second_sum, sent
+    return first_sum, second_sum, early
 
 
 def per_device(inputs, grad_keys, local_weights, feedback, base, momentum, warm_start):
@@ -294,42 +344,45 @@
     everything = ("rep", "fsdp")
     spots = all_spots()
 
-    first_sum, second_sum, sent = reduce_terms(tokens_in, cotangent, spots)
-
     lane = lax.broadcasted_iota(jnp.int32, (1, width), 1)
     mine = lane // block_width == my_rep
     drift = feedback[0].astype(f32) - weights.astype(f32)
-    own_base = jnp.where(mine, jnp.tile(rep_size * base, (1, width // block_width)), 0.0)
-    moved = drift + inner_rate * jnp.concatenate([first_sum, second_sum])
-    mean = scatter_sum(moved + own_base, "rep", rep_size) / rep_size
+
+    def early_of(*behind):
+        own_base = jnp.where(mine, jnp.tile(rep_size * base, (1, width // block_width)), 0.0)
+        return scatter_sum(after(drift + own_base, *behind), "rep", rep_size)
+
+    first_sum, second_sum, early = reduce_terms(tokens_in, cotangent, spots, early_of)
+    inner_grad = jnp.concatenate([first_sum, second_sum])
+    mean = (
+        early + inner_rate * scatter_sum(inner_grad.astype(bf16), "rep", rep_size)
+    ) / rep_size
+    moved = drift + inner_rate * inner_grad
 
     def product_shapes():
-        return (width, 2 * rank), (rows // rep_size, rank)
+        return (width, 2 * rank), (rows // rep_size, 2 * rank)
 
     packed, left_part = small_call(first_kernel, product_shapes(), mean, warm_start)
     full_base = lax.all_gather(after(base, mean), "rep", axis=1, tiled=True)
     every_row = lax.all_gather(local_weights, "fsdp", axis=1, tiled=True)[0]
-    grad = grad_of_inputs(after(cotangent, packed), every_row)
-    for repeat in range(ROUNDS - 1):
-        share = scatter_sum(packed, everything, everyone)
-        summed = gather_rows(share, everything, everyone)
+    grad = None
+    for repeat in range(ROUNDS):
+        if repeat < 2:
+            grad = half_of_grad(after(cotangent, packed), every_row, repeat, grad)
+        summed = gather_rows(scatter_sum(packed, everything, everyone), everything, everyone)
         summed, grad = lax.optimization_barrier((summed, grad))
-        packed, left_part = small_call(
-            functools.partial(round_kernel, False), product_shapes(), summed, mean
-        )
-    share = scatter_sum(packed, everything, everyone)
-    summed = gather_rows(share, everything, everyone)
-    left = gather_rows(after(left_part, share), "rep", rep_size)
+        if repeat < ROUNDS - 1:
+            packed, left_part = small_call(
+                functools.partial(round_kernel, False), product_shapes(), summed, mean
+            )
+    left = gather_rows(after(left_part, summed), "rep", rep_size)
     factor, inverse = small_call(
         functools.partial(round_kernel, True), ((width, rank), (rank, rank)), summed, mean
     )
-    orthonormal = dot(left, inverse, ((1,), (1,)))
-    approx = dot(orthonormal, factor, ((1,), (1,)))
-    feedback_out = (full_base + moved - approx)[None]
-    column_block = lax.dynamic_slice_in_dim(approx, my_rep * block_width, block_width, 1)
-    momentum_out = momentum_keep * momentum + column_block
-    base_out = base - outer_rate * (column_block + momentum_keep * momentum_out)
-    return (grad[None], feedback_out, base_out, momentum_out, factor)
+    feedback_out, base_out, momentum_out = final_outputs(
+        my_rep, left, inverse, factor, moved, full_base, base, momentum
+    )
+    return (grad[None], feedback_out[None], base_out, momentum_out, factor)
 
 
 def solution(mesh):

time: 338 us -> 319 us (0.944)
  waiting for transfers between devices: 131 us -> 106 us
  blocking collectives: 58.9 us -> 68.6 us
  Pallas kernels: 62.9 us -> 68.7 us
  local copies, waits for them, and re-layouts: 13.5 us -> 8.73 us
    ppermute x11, waiting for transfers between devices: 103 us -> 65.2 us  [hop(): return lax.ppermute(value, 'fsdp', pairs)]
    all_to_all x2 -> x3, blocking collectives: 51.1 us -> 68.6 us  [scatter_sum(): got = lax.all_to_all(value, axes, 0, 0, tiled=True)]
    all_to_all x1, waiting for transfers between devices: 16 us -> 28.4 us  [scatter_sum(): got = lax.all_to_all(value, axes, 0, 0, tiled=True)]
    all_to_all x1 -> x0, blocking collectives: 7.83 us -> none  [gather_rows(): return lax.all_to_all(sent, axes, 0, 0, tiled=True)]
    pallas_call x1 -> x3, Pallas kernels: 15.7 us -> 22.2 us  [the longest x2 17.7 us: half_of_grad(): pl.pallas_call(grad_kernel, grid=(steps,), in_specs=in_specs, out_specs=p...]
    broadcast_in_dim x1 -> x0, other arithmetic: 5.02 us -> none  [per_device(): feedback_out = (full_base + moved - approx)[None]]
    all_to_all x1, starting transfers between devices: 7.82 us -> 3.95 us  [scatter_sum(): got = lax.all_to_all(value, axes, 0, 0, tiled=True)]
    add x1 -> x2, other arithmetic: 0.91 us -> 4.58 us  [the longest x1 2.41 us: per_device(): moved = drift + inner_rate * inner_grad]
  transfers between devices with their start and end apart: 16 -> 17, of which waited for: 12 -> 10; matrix products, arithmetic and copies ran while one was open for 7% -> 8% of each run, Pallas kernels for 19% -> 20%
where the time goes in v4:
time: 319 us; the launch traced here: 317 us
  waiting for transfers between devices  106 us (33%)
  Pallas kernels  68.7 us (22%)
  blocking collectives  68.6 us (22%)
  starting transfers between devices  30.6 us (10%)
  other arithmetic  20.3 us (6%)
  between operations  14.5 us (5%)
  local copies, waits for them, and re-layouts  8.73 us (3%)
    all_to_all x3, blocking collectives, scatter_sum(): got = lax.all_to_all(value, axes, 0, 0, tiled=True)  68.6 us
    ppermute x11, waiting for transfers between devices, hop(): return lax.ppermute(value, 'fsdp', pairs)  65.2 us
    pallas_call x4, Pallas kernels, term_blocks(): pl.pallas_call(kernel, grid_spec=pltpu.PrefetchScalarGridSpec(num_scalar_...  30.8 us
    all_to_all x1, waiting for transfers between devices, scatter_sum(): got = lax.all_to_all(value, axes, 0, 0, tiled=True)  28.4 us
    pallas_call x2, Pallas kernels, half_of_grad(): pl.pallas_call(grad_kernel, grid=(steps,), in_specs=in_specs, out_specs=p...  17.7 us
    pallas_call x3, Pallas kernels, small_call(): pl.pallas_call(kernel, out_shape=[jax.ShapeDtypeStruct(shape, f32) for sh...  15.7 us
    ppermute x11, starting transfers between devices, hop(): return lax.ppermute(value, 'fsdp', pairs)  13.8 us
    all_to_all x3, starting transfers between devices, gather_rows(): return lax.all_to_all(sent, axes, 0, 0, tiled=True)  12.8 us
  transfers between devices with their start and end apart: 17, of which 10 were waited for; matrix products, arithmetic and copies ran while one was open for 8% of the time, Pallas kernels for 20%

profile of v4, /device:TPU:1, one launch (start us, length us, event | category | flops | bytes accessed | tf_op | source)
XLA Modules:
  0.0 317.4 jit_solution(11490600215265081744)
XLA Ops:
  9.1 6.8 %shard_map.119 = bf16[4,512,1024]{2,1,0:T(8,128)(2,1)} custom-call(s32[16]{0:T(128)} %dynamic-slice_bitcast_fusion.spots, bf16[512,8192]{1,0:T(8,128)(2,1)} %bitcast.62, bf16[512,1024]{1,0:T(8,128)(2,1)} %bitcast.68), custom_call_target="tpu_custom_call" | custom-call | flops 2147483648 | bytes 10485760 | tf_op jit(solution)/shard_map/pallas_call | solution.py:130
  17.3 6.8 %shard_map.120 = bf16[4,512,1024]{2,1,0:T(8,128)(2,1)} custom-call(s32[16]{0:T(128)} %dynamic-slice_bitcast_fusion.spots, bf16[512,8192]{1,0:T(8,128)(2,1)} %bitcast.63, bf16[512,1024]{1,0:T(8,128)(2,1)} %bitcast.69), custom_call_target="tpu_custom_call" | custom-call | flops 2147483648 | bytes 10485760 | tf_op jit(solution)/shard_map/pallas_call | solution.py:130
  24.8 8.7 %shard_map.121 = (bf16[2,320,1024]{2,1,0:T(8,128)(2,1)}, bf16[320,1024]{1,0:T(8,128)(2,1)}, bf16[320,1024]{1,0:T(8,128)(2,1)}, bf16[2,192,1024]{2,1,0:T(8,128)(2,1)}, bf16[2,192,1024]{2,1,0:T(8,128)(2,1)}) custom-call(s32[16]{0:T(128)} %dynamic-slice_bitcast_fusion.spots, bf16[512,8192]{1,0:T(8,128)(2,1)} %bitcast.64, bf16[512,1024]{1,0:T(8,128)(2,1)} %bitcast.70, ...), custom_call_target="tpu_custom_call" | custom-call | flops 2147483648 | bytes 10485760 | tf_op jit(solution)/shard_map/pallas_call | solution.py:130
  37.2 8.5 %shard_map.122 = (bf16[2,320,1024]{2,1,0:T(8,128)(2,1)}, bf16[320,1024]{1,0:T(8,128)(2,1)}, bf16[320,1024]{1,0:T(8,128)(2,1)}, bf16[2,192,1024]{2,1,0:T(8,128)(2,1)}, bf16[2,192,1024]{2,1,0:T(8,128)(2,1)}) custom-call(s32[16]{0:T(128)} %dynamic-slice_bitcast_fusion.spots, bf16[512,8192]{1,0:T(8,128)(2,1)} %bitcast.65, bf16[512,1024]{1,0:T(8,128)(2,1)} %bitcast.71, ...), custom_call_target="tpu_custom_call" | custom-call | flops 2147483648 | bytes 10485760 | tf_op jit(solution)/shard_map/pallas_call | solution.py:130
  53.2 18.5 %collective-permute-done.4 = bf16[2,192,1024]{2,1,0:T(8,128)(2,1)S(1)} collective-permute-done((bf16[2,192,1024]{2,1,0:T(8,128)(2,1)}, bf16[2,192,1024]{2,1,0:T(8,128)(2,1)S(1)}, u32[]{:S(2)}, u32[]{:S(2)}) %collective-permute-start.4) | collective-permute-done | bytes 786464 | tf_op jit(solution)/shard_map/ppermute | solution.py:33
  71.7 13.3 %collective-permute-done.1 = bf16[2,320,1024]{2,1,0:T(8,128)(2,1)} collective-permute-done((bf16[2,320,1024]{2,1,0:T(8,128)(2,1)}, bf16[2,320,1024]{2,1,0:T(8,128)(2,1)}, u32[]{:S(2)}, u32[]{:S(2)}) %collective-permute-start.1) | collective-permute-done | bytes 1310752 | tf_op jit(solution)/shard_map/ppermute | solution.py:33
  85.0 20.4 %collective-permute-done.5 = bf16[2,192,1024]{2,1,0:T(8,128)(2,1)} collective-permute-done((bf16[2,192,1024]{2,1,0:T(8,128)(2,1)}, bf16[2,192,1024]{2,1,0:T(8,128)(2,1)}, u32[]{:S(2)}, u32[]{:S(2)}) %collective-permute-start.5) | collective-permute-done | bytes 786464 | tf_op jit(solution)/shard_map/ppermute | solution.py:33
  113.5 4.0 %all-to-all-start = ((f32[8,64,1024]{2,1,0:T(8,128)}), f32[8,64,1024]{2,1,0:T(8,128)S(1)}, u32[]{:S(2)}, u32[]{:S(2)}) async-start(f32[8,64,1024]{2,1,0:T(8,128)} %bitcast.75), calls=%async_computation | async-start | bytes 4194304 | tf_op jit(solution)/shard_map/all_to_all | solution.py:43
  119.1 28.4 %all-to-all-done = f32[8,64,1024]{2,1,0:T(8,128)S(1)} async-done(((f32[8,64,1024]{2,1,0:T(8,128)}), f32[8,64,1024]{2,1,0:T(8,128)S(1)}, u32[]{:S(2)}, u32[]{:S(2)}) %all-to-all-start) | async-done | bytes 2097184 | tf_op jit(solution)/shard_map/all_to_all | solution.py:43
  148.9 5.7 %collective-permute-done.9 = bf16[96,1024]{1,0:T(8,128)(2,1)S(1)} collective-permute-done((bf16[96,1024]{1,0:T(8,128)(2,1)S(1)}, bf16[96,1024]{1,0:T(8,128)(2,1)S(1)}, u32[]{:S(2)}, u32[]{:S(2)}) %collective-permute-start.9) | collective-permute-done | bytes 196640 | tf_op jit(solution)/shard_map/ppermute | solution.py:33
  161.4 3.8 %collective-permute-done.10 = bf16[96,1024]{1,0:T(8,128)(2,1)S(1)} collective-permute-done((bf16[96,1024]{1,0:T(8,128)(2,1)S(1)}, bf16[96,1024]{1,0:T(8,128)(2,1)S(1)}, u32[]{:S(2)}, u32[]{:S(2)}) %collective-permute-start.10) | collective-permute-done | bytes 196640 | tf_op jit(solution)/shard_map/ppermute | solution.py:33
  171.3 21.8 %all_to_all.59 = bf16[8,64,1024]{2,1,0:T(8,128)(2,1)S(1)} all-to-all(bf16[8,64,1024]{2,1,0:T(8,128)(2,1)S(1)} %bitcast.77), channel_id=1, replica_groups=mesh['rep'=8,'fsdp'=16] {'rep'}, dimensions={0} | all-to-all | bytes 2097152 | tf_op jit(solution)/shard_map/all_to_all | solution.py:43
  194.8 27.5 %all_to_all.60 = f32[128,8,128]{2,1,0:T(8,128)S(1)} all-to-all(f32[128,8,128]{2,1,0:T(8,128)S(1)} %bitcast.60), channel_id=1, replica_groups=mesh['rep'=8,'fsdp'=16] {'rep','fsdp'}, dimensions={0} | all-to-all | bytes 1048576 | tf_op jit(solution)/shard_map/all_to_all | solution.py:43
  223.4 4.6 %all-to-all-start.3 = ((f32[128,8,128]{2,1,0:T(8,128)}), f32[128,8,128]{2,1,0:T(8,128)S(1)}, u32[]{:S(2)}, u32[]{:S(2)}) async-start(f32[128,8,128]{2,1,0:T(8,128)} %broadcast_in_dim.38), calls=%async_computation.3 | async-start | bytes 1048576 | tf_op jit(solution)/shard_map/all_to_all | solution.py:50
  228.0 8.9 %shard_map.124.refs_0_ = bf16[512,8192]{1,0:T(8,128)(2,1)} custom-call(bf16[512,1024]{1,0:T(8,128)(2,1)} %bitcast.72, bf16[8192,1024]{1,0:T(8,128)(2,1)} %bitcast.66), custom_call_target="tpu_custom_call" | custom-call | flops 4294967296 | bytes 12582912 | tf_op jit(solution)/shard_map/pallas_call | solution.py:167
  236.9 6.8 %all-to-all-done.3 = f32[128,8,128]{2,1,0:T(8,128)S(1)} async-done(((f32[128,8,128]{2,1,0:T(8,128)}), f32[128,8,128]{2,1,0:T(8,128)S(1)}, u32[]{:S(2)}, u32[]{:S(2)}) %all-to-all-start.3) | async-done | bytes 524320 | tf_op jit(solution)/shard_map/all_to_all | solution.py:50
  243.6 8.1 %shard_map.125 = (f32[1024,128]{1,0:T(8,128)S(1)}, f32[64,128]{1,0:T(8,128)S(1)}) custom-call(f32[1024,128]{1,0:T(8,128)S(1)} %bitcast.59, f32[64,1024]{1,0:T(8,128)S(1)} %add_multiply_fusion.mean), custom_call_target="tpu_custom_call" | custom-call | flops 1000000000 | bytes 2097152 | tf_op jit(solution)/shard_map/pallas_call | solution.py:266
  251.7 19.3 %all_to_all.61 = f32[128,8,128]{2,1,0:T(8,128)S(1)} all-to-all(f32[128,8,128]{2,1,0:T(8,128)S(1)} %bitcast.61), channel_id=1, replica_groups=mesh['rep'=8,'fsdp'=16] {'rep','fsdp'}, dimensions={0} | all-to-all | bytes 1048576 | tf_op jit(solution)/shard_map/all_to_all | solution.py:43
  271.9 4.5 %all-to-all-start.5 = ((f32[128,8,128]{2,1,0:T(8,128)}), f32[128,8,128]{2,1,0:T(8,128)S(1)}, u32[]{:S(2)}, u32[]{:S(2)}) async-start(f32[128,8,128]{2,1,0:T(8,128)} %broadcast_in_dim.39), calls=%async_computation.5 | async-start | bytes 1048576 | tf_op jit(solution)/shard_map/all_to_all | solution.py:50
  276.5 8.9 %shard_map.126 = bf16[512,8192]{1,0:T(8,128)(2,1)} custom-call(bf16[512,1024]{1,0:T(8,128)(2,1)} %bitcast.73, bf16[8192,1024]{1,0:T(8,128)(2,1)} %bitcast.67, bf16[512,8192]{1,0:T(8,128)(2,1)} %shard_map.124.refs_0_), custom_call_target="tpu_custom_call", output_to_operand_aliasing={{}: (2, {})} | custom-call | flops 4294967296 | bytes 12582912 | tf_op jit(solution)/shard_map/pallas_call | solution.py:167
  285.3 4.9 %all-to-all-done.5 = f32[128,8,128]{2,1,0:T(8,128)S(1)} async-done(((f32[128,8,128]{2,1,0:T(8,128)}), f32[128,8,128]{2,1,0:T(8,128)S(1)}, u32[]{:S(2)}, u32[]{:S(2)}) %all-to-all-start.5) | async-done | bytes 524320 | tf_op jit(solution)/shard_map/all_to_all | solution.py:50
  291.1 3.6 %all-to-all-start.6 = ((f32[8,64,128]{2,1,0:T(8,128)}), f32[8,64,128]{2,1,0:T(8,128)S(1)}, u32[]{:S(2)}, u32[]{:S(2)}) async-start(f32[8,64,128]{2,1,0:T(8,128)} %broadcast_in_dim.41), calls=%async_computation.6 | async-start | bytes 524288 | tf_op jit(solution)/shard_map/all_to_all | solution.py:50
  297.2 6.4 %shard_map.127 = (f32[1024,64]{1,0:T(8,128)S(1)}, f32[64,64]{1,0:T(8,128)S(1)}) custom-call(f32[1024,128]{1,0:T(8,128)S(1)} %bitcast.58, f32[64,1024]{1,0:T(8,128)S(1)} %copy-done.7), custom_call_target="tpu_custom_call" | custom-call | flops 1000000000 | bytes 2097152 | tf_op jit(solution)/shard_map/pallas_call | solution.py:266
  306.1 4.5 %shard_map.128 = (f32[512,1024]{1,0:T(8,128)}, f32[512,128]{1,0:T(8,128)}, f32[512,128]{1,0:T(8,128)}) custom-call(s32[1]{0:T(128)} %bitcast.23.my_rep, f32[512,128]{1,0:T(8,128)S(1)} %bitcast.57, f32[64,64]{1,0:T(8,128)S(1)} %get-tuple-element.77.inverse, f32[1024,64]{1,0:T(8,128)S(1)} %get-tuple-element.87.factor, f32[512,1024]{1,0:T(8,128)S(1)} %bitcast_add_fusion.moved, ...), custom_call_target="tpu_custom_call" | custom-call | flops 1000000000 | bytes 8388608 | tf_op jit(solution)/shard_map/pallas_call | solution.py:207
  (102 shorter events, 48.4 us)
Async XLA Ops:
  7.2 220.8 %all-gather.3.cloned.1.call-start = ((), (), s32[]{:S(2)}) async-start(), calls=%async_computation.7 | async-start | bytes 17825792 | tf_op jit(solution)/shard_map/all_gather | solution.py:367
  15.9 8.6 %collective-permute-start = (bf16[4,512,1024]{2,1,0:T(8,128)(2,1)}, bf16[4,512,1024]{2,1,0:T(8,128)(2,1)}, u32[]{:S(2)}, u32[]{:S(2)}) collective-permute-start(bf16[4,512,1024]{2,1,0:T(8,128)(2,1)} %shard_map.119), channel_id=1, source_target_pairs={{0,1},{1,0},{2,3},{3,2},{4,5},{5,4},{6,7},{7,6},{8,9},{9,8},{10,11... | collective-permute-start | bytes 12582920 | tf_op jit(solution)/shard_map/ppermute | solution.py:33
  24.4 10.7 %collective-permute-start.2 = (bf16[4,512,1024]{2,1,0:T(8,128)(2,1)}, bf16[4,512,1024]{2,1,0:T(8,128)(2,1)S(1)}, u32[]{:S(2)}, u32[]{:S(2)}) collective-permute-start(bf16[4,512,1024]{2,1,0:T(8,128)(2,1)} %shard_map.120), channel_id=1, source_target_pairs={{0,1},{1,0},{2,3},{3,2},{4,5},{5,4},{6,7},{7,6},{8,9},{9,8},{10,11... | collective-permute-start | bytes 12582920 | tf_op jit(solution)/shard_map/ppermute | solution.py:33
  33.5 17.3 %copy-start = (f32[512,128]{1,0:T(8,128)S(1)}, f32[512,128]{1,0:T(8,128)}, u32[]{:S(2)}) copy-start(f32[512,128]{1,0:T(8,128)} %base.1) | copy-start | bytes 786436
  33.5 51.5 %collective-permute-start.1 = (bf16[2,320,1024]{2,1,0:T(8,128)(2,1)}, bf16[2,320,1024]{2,1,0:T(8,128)(2,1)}, u32[]{:S(2)}, u32[]{:S(2)}) collective-permute-start(bf16[2,320,1024]{2,1,0:T(8,128)(2,1)} %get-tuple-element.47), channel_id=1, source_target_pairs={{0,2},{1,3},{2,4},{3,5},{4,6},{5,7},{6,0},{7,1},{8,10},{9,11},{10,... | collective-permute-start | bytes 3932168 | tf_op jit(solution)/shard_map/ppermute | solution.py:33
  45.7 59.8 %collective-permute-start.3 = (bf16[2,320,1024]{2,1,0:T(8,128)(2,1)}, bf16[2,320,1024]{2,1,0:T(8,128)(2,1)}, u32[]{:S(2)}, u32[]{:S(2)}) collective-permute-start(bf16[2,320,1024]{2,1,0:T(8,128)(2,1)} %get-tuple-element.50), channel_id=1, source_target_pairs={{0,6},{1,7},{2,0},{3,1},{4,2},{5,3},{6,4},{7,5},{8,14},{9,15},{10,... | collective-permute-start | bytes 3932168 | tf_op jit(solution)/shard_map/ppermute | solution.py:33
  47.7 24.0 %collective-permute-start.4 = (bf16[2,192,1024]{2,1,0:T(8,128)(2,1)}, bf16[2,192,1024]{2,1,0:T(8,128)(2,1)S(1)}, u32[]{:S(2)}, u32[]{:S(2)}) collective-permute-start(bf16[2,192,1024]{2,1,0:T(8,128)(2,1)} %get-tuple-element.51), channel_id=1, source_target_pairs={{0,8},{1,9},{2,10},{3,11},{4,12},{5,13},{6,14},{7,15},{8,0},{9,1},... | collective-permute-start | bytes 2359304 | tf_op jit(solution)/shard_map/ppermute | solution.py:33
  50.8 54.7 %collective-permute-start.5 = (bf16[2,192,1024]{2,1,0:T(8,128)(2,1)}, bf16[2,192,1024]{2,1,0:T(8,128)(2,1)}, u32[]{:S(2)}, u32[]{:S(2)}) collective-permute-start(bf16[2,192,1024]{2,1,0:T(8,128)(2,1)} %get-tuple-element.52), channel_id=1, source_target_pairs={{0,8},{1,9},{2,10},{3,11},{4,12},{5,13},{6,14},{7,15},{8,0},{9,1},... | collective-permute-start | bytes 2359304 | tf_op jit(solution)/shard_map/ppermute | solution.py:33
  51.0 54.4 %copy-start.16 = (bf16[2,192,1024]{2,1,0:T(8,128)(2,1)S(1)}, bf16[2,192,1024]{2,1,0:T(8,128)(2,1)}, u32[]{:S(2)}) copy-start(bf16[2,192,1024]{2,1,0:T(8,128)(2,1)} %get-tuple-element.54) | copy-start | bytes 2359300
  51.0 54.4 %copy-start.17 = (bf16[2,192,1024]{2,1,0:T(8,128)(2,1)S(1)}, bf16[2,192,1024]{2,1,0:T(8,128)(2,1)}, u32[]{:S(2)}) copy-start(bf16[2,192,1024]{2,1,0:T(8,128)(2,1)} %get-tuple-element.59) | copy-start | bytes 2359300
  113.5 33.9 %all-to-all-start = ((f32[8,64,1024]{2,1,0:T(8,128)}), f32[8,64,1024]{2,1,0:T(8,128)S(1)}, u32[]{:S(2)}, u32[]{:S(2)}) async-start(f32[8,64,1024]{2,1,0:T(8,128)} %bitcast.75), calls=%async_computation | async-start | bytes 4194304 | tf_op jit(solution)/shard_map/all_to_all | solution.py:43
  117.5 187.0 %all-gather.5.cloned.1.call-start = ((), (), s32[]{:S(2)}) async-start(), calls=%async_computation.8 | async-start | bytes 2359296 | tf_op jit(solution)/shard_map/all_gather | solution.py:366
  117.5 30.1 %collective-permute-start.7 = (bf16[512,1024]{1,0:T(8,128)(2,1)}, bf16[512,1024]{1,0:T(8,128)(2,1)}, u32[]{:S(2)}, u32[]{:S(2)}) collective-permute-start(bf16[512,1024]{1,0:T(8,128)(2,1)} %pad_maximum_fusion.2), channel_id=1, source_target_pairs={{0,6},{1,7},{2,0},{3,1},{4,2},{5,3},{6,4},{7,5},{8,14},{9,15},{10,... | collective-permute-start | bytes 3145736 | tf_op jit(solution)/shard_map/ppermute | solution.py:33
  117.6 30.0 %collective-permute-start.6 = (bf16[512,1024]{1,0:T(8,128)(2,1)}, bf16[512,1024]{1,0:T(8,128)(2,1)}, u32[]{:S(2)}, u32[]{:S(2)}) collective-permute-start(bf16[512,1024]{1,0:T(8,128)(2,1)} %pad_maximum_fusion.1), channel_id=1, source_target_pairs={{0,2},{1,3},{2,4},{3,5},{4,6},{5,7},{6,0},{7,1},{8,10},{9,11},{10,... | collective-permute-start | bytes 3145736 | tf_op jit(solution)/shard_map/ppermute | solution.py:33
  148.8 5.8 %collective-permute-start.9 = (bf16[96,1024]{1,0:T(8,128)(2,1)S(1)}, bf16[96,1024]{1,0:T(8,128)(2,1)S(1)}, u32[]{:S(2)}, u32[]{:S(2)}) collective-permute-start(bf16[96,1024]{1,0:T(8,128)(2,1)S(1)} %fusion.10), channel_id=1, source_target_pairs={{0,2},{1,3},{2,4},{3,5},{4,6},{5,7},{6,0},{7,1},{8,10},{9,11},{10,... | collective-permute-start | bytes 589832 | tf_op jit(solution)/shard_map/ppermute | solution.py:33
  156.0 9.2 %collective-permute-start.10 = (bf16[96,1024]{1,0:T(8,128)(2,1)S(1)}, bf16[96,1024]{1,0:T(8,128)(2,1)S(1)}, u32[]{:S(2)}, u32[]{:S(2)}) collective-permute-start(bf16[96,1024]{1,0:T(8,128)(2,1)S(1)} %get-tuple-element.89), channel_id=1, source_target_pairs={{0,6},{1,7},{2,0},{3,1},{4,2},{5,3},{6,4},{7,5},{8,14},{9,15},{10,... | collective-permute-start | bytes 589832 | tf_op jit(solution)/shard_map/ppermute | solution.py:33
  157.7 11.6 %copy-start.21 = (bf16[320,1024]{1,0:T(8,128)(2,1)S(1)}, bf16[320,1024]{1,0:T(8,128)(2,1)}, u32[]{:S(2)}) copy-start(bf16[320,1024]{1,0:T(8,128)(2,1)} %get-tuple-element.62) | copy-start | bytes 1966084
  157.8 11.6 %collective-permute-start.8 = (bf16[320,1024]{1,0:T(8,128)(2,1)S(1)}, bf16[320,1024]{1,0:T(8,128)(2,1)S(1)}, u32[]{:S(2)}, u32[]{:S(2)}) collective-permute-start(bf16[320,1024]{1,0:T(8,128)(2,1)S(1)} %fusion.3), channel_id=1, source_target_pairs={{0,8},{1,9},{2,10},{3,11},{4,12},{5,13},{6,14},{7,15},{8,0},{9,1},... | collective-permute-start | bytes 1966088 | tf_op jit(solution)/shard_map/ppermute | solution.py:33
  171.1 22.0 %copy-start.8 = (f32[320,1024]{1,0:T(8,128)}, f32[320,1024]{1,0:T(8,128)S(1)}, u32[]{:S(2)}) copy-start(f32[320,1024]{1,0:T(8,128)S(1)} %fusion.4) | copy-start | bytes 3932164
  171.3 22.1 %copy-start.22 = (f32[1024,64]{0,1:T(8,128)S(1)}, f32[1024,64]{0,1:T(8,128)}, u32[]{:S(2)}) copy-start(f32[1024,64]{0,1:T(8,128)} %param.14) | copy-start | bytes 786436
  193.4 50.3 %copy-start.6 = (f32[64,1024]{1,0:T(8,128)}, f32[64,1024]{1,0:T(8,128)S(1)}, u32[]{:S(2)}) copy-start(f32[64,1024]{1,0:T(8,128)S(1)} %add_multiply_fusion.mean) | copy-start | bytes 786436
  223.4 20.3 %all-to-all-start.3 = ((f32[128,8,128]{2,1,0:T(8,128)}), f32[128,8,128]{2,1,0:T(8,128)S(1)}, u32[]{:S(2)}, u32[]{:S(2)}) async-start(f32[128,8,128]{2,1,0:T(8,128)} %broadcast_in_dim.38), calls=%async_computation.3 | async-start | bytes 1048576 | tf_op jit(solution)/shard_map/all_to_all | solution.py:50
  271.9 18.3 %all-to-all-start.5 = ((f32[128,8,128]{2,1,0:T(8,128)}), f32[128,8,128]{2,1,0:T(8,128)S(1)}, u32[]{:S(2)}, u32[]{:S(2)}) async-start(f32[128,8,128]{2,1,0:T(8,128)} %broadcast_in_dim.39), calls=%async_computation.5 | async-start | bytes 1048576 | tf_op jit(solution)/shard_map/all_to_all | solution.py:50
  291.1 13.4 %all-to-all-start.6 = ((f32[8,64,128]{2,1,0:T(8,128)}), f32[8,64,128]{2,1,0:T(8,128)S(1)}, u32[]{:S(2)}, u32[]{:S(2)}) async-start(f32[8,64,128]{2,1,0:T(8,128)} %broadcast_in_dim.41), calls=%async_computation.6 | async-start | bytes 524288 | tf_op jit(solution)/shard_map/all_to_all | solution.py:50
  (16 other events, 70.1 us)
Sparse Core Ops, SparseCore 0:
  10.5 161.9 all-gather.2
  193.5 52.3 all-gather.4

commit v5 on v4

--- a/solution.py
+++ b/solution.py
@@ -133,7 +133,7 @@
             num_scalar_prefetch=1, grid=(COUNT,), in_specs=in_specs, out_specs=out_specs
         ),
         out_shape=out_shape,
-        compiler_params=pltpu.CompilerParams(vmem_limit_bytes=56 << 20),
+        compiler_params=pltpu.CompilerParams(vmem_limit_bytes=60 << 20),
         cost_estimate=pl.CostEstimate(
             flops=2 * COUNT * depth * rows * width,
             bytes_accessed=2 * COUNT * (depth * rows + 2 * rows * width),
@@ -171,7 +171,7 @@
         out_specs=pl.BlockSpec((tokens, rows), lambda i: (0, i + which * steps)),
         out_shape=jax.ShapeDtypeStruct((tokens, wide), bf16),
         input_output_aliases=aliases,
-        compiler_params=pltpu.CompilerParams(vmem_limit_bytes=56 << 20),
+        compiler_params=pltpu.CompilerParams(vmem_limit_bytes=60 << 20),
         cost_estimate=pl.CostEstimate(
             flops=tokens * depth * wide,
             bytes_accessed=wide * (depth + tokens),
@@ -280,6 +280,57 @@
     return total
 
 
+def first_stage_kernel(
+    up_y0, down_y1, below, above, up_straight, down_straight, up_crossed, down_crossed,
+    sent_up, sent_down, up_up, down_down, own,
+):
+    first = up_y0.shape[0]
+    half = up_straight.shape[1] // 2
+    sent_up[:first] = add(up_y0[...], below[0]).astype(bf16)
+    sent_down[:first] = add(down_y1[...], above[0]).astype(bf16)
+    two = add(up_straight[0], down_crossed[0]).astype(bf16)
+    up = add(up_straight[1], up_crossed[0])
+    down = add(down_straight[0], down_crossed[1])
+    sent_up[first : first + half] = two[:half]
+    sent_down[first : first + half] = two[half:]
+    sent_up[first + half :] = up[half:].astype(bf16)
+    sent_down[first + half :] = down[:half].astype(bf16)
+    up_up[...] = up[:half]
+    down_down[...] = down[half:]
+    own[...] = add(down_straight[1], up_crossed[1])
+
+
+def second_stage_kernel(
+    own_y1, plain_below, above_again, below_again, up_up, down_down, sent, second_up, second_down
+):
+    first = own_y1.shape[0]
+    half = up_up.shape[0]
+    sent[...] = add(own_y1[...], plain_below[0], above_again[:first]).astype(bf16)
+    second_up[...] = add(up_up[...], below_again[first : first + half]).astype(bf16)
+    second_down[...] = add(down_down[...], above_again[first : first + half]).astype(bf16)
+
+
+def stage(kernel, shapes, planes, *operands):
+    width = operands[0].shape[-1]
+    columns = 256
+
+    def by_columns(shape, plane=None):
+        lead = (0,) * (len(shape) - 1)
+        if plane is not None:
+            shape, lead = (1,) + shape[1:], (plane,) + lead[1:]
+        return pl.BlockSpec(shape[:-1] + (columns,), lambda i: lead + (i,))
+
+    return pl.pallas_call(
+        kernel,
+        grid=(width // columns,),
+        in_specs=[by_columns(x.shape, planes.get(at)) for at, x in enumerate(operands)],
+        out_specs=[by_columns(shape) for shape, _ in shapes],
+        out_shape=[jax.ShapeDtypeStruct(*shape) for shape in shapes],
+        compiler_params=pltpu.CompilerParams(vmem_limit_bytes=60 << 20),
+        cost_estimate=pl.CostEstimate(flops=10**7, bytes_accessed=8 << 20, transcendentals=0),
+    )(*operands)
+
+
 def reduce_terms(tokens_in, cotangent, spots, early_of):
     blocks = functools.partial(term_blocks, tokens_in)
     away_up = blocks(cotangent, spots, "up")
@@ -301,27 +352,29 @@
         (below, above, up_crossed, down_crossed)
     )
     half = up_straight.shape[1] // 2
-
-    def both(straight, crossed):
-        total = add(straight, crossed)
-        return total[:half], total[half:]
-
-    two_up, two_down = both(up_straight[0], down_crossed[0])
-    up_up, up_down = both(up_straight[1], up_crossed[0])
-    down_up, down_down = both(down_straight[0], down_crossed[1])
-    sent_up = jnp.concatenate([add(up_y0, below[0]), two_up, up_down]).astype(bf16)
-    sent_down = jnp.concatenate([add(down_y1, above[0]), two_down, down_up]).astype(bf16)
+    rest, width = up_straight.shape[1:]
+    sent_up, sent_down, up_up, down_down, own_second = stage(
+        first_stage_kernel,
+        [((FIRST + rest, width), bf16)] * 2 + [((half, width), f32)] * 2 + [((rest, width), f32)],
+        {2: 0, 3: 0},
+        up_y0, down_y1, below, above, up_straight, down_straight, up_crossed, down_crossed,
+    )
     below_again, above_again = hop(sent_up, dz=1), hop(sent_down, dz=-1)
-    own_second = add(down_straight[1], up_crossed[1])
-
-    early, below_again, above_again, own_second = lax.optimization_barrier(
-        (early_of(sent_up, sent_down), below_again, above_again, own_second)
-    )
-    sent = add(own_y1, below[1], above_again[:FIRST]).astype(bf16)
-    second_up = add(up_up, below_again[FIRST : FIRST + half]).astype(bf16)
-    second_down = add(down_down, above_again[FIRST : FIRST + half]).astype(bf16)
+
+    early = early_of(sent_up, sent_down)
+    below_again, above_again, own_second = lax.optimization_barrier(
+        (below_again, above_again, own_second)
+    )
+    sent, second_up, second_down = stage(
+        second_stage_kernel,
+        [((FIRST, width), bf16)] + [((half, width), bf16)] * 2,
+        {1: 1},
+        own_y1, below, above_again, below_again, up_up, down_down,
+    )
     crossed = hop(sent, dy=1)
-    last_below, last_above = hop(second_up, dz=1), hop(second_down, dz=-1)
+    early, crossed, last_below, last_above = lax.optimization_barrier(
+        (early, crossed, hop(second_up, dz=1), hop(second_down, dz=-1))
+    )
 
     second_sum = own_second + jnp.concatenate(
         [add(last_below, above_again[FIRST + half :]), add(below_again[FIRST + half :], last_above)]
@@ -346,18 +399,18 @@
 
     lane = lax.broadcasted_iota(jnp.int32, (1, width), 1)
     mine = lane // block_width == my_rep
-    drift = feedback[0].astype(f32) - weights.astype(f32)
 
     def early_of(*behind):
+        drift = feedback[0].astype(f32) - after(weights, *behind).astype(f32)
         own_base = jnp.where(mine, jnp.tile(rep_size * base, (1, width // block_width)), 0.0)
-        return scatter_sum(after(drift + own_base, *behind), "rep", rep_size)
-
-    first_sum, second_sum, early = reduce_terms(tokens_in, cotangent, spots, early_of)
+        return scatter_sum(drift + own_base, "rep", rep_size), drift
+
+    first_sum, second_sum, (early, drift) = reduce_terms(tokens_in, cotangent, spots, early_of)
     inner_grad = jnp.concatenate([first_sum, second_sum])
     mean = (
         early + inner_rate * scatter_sum(inner_grad.astype(bf16), "rep", rep_size)
     ) / rep_size
-    moved = drift + inner_rate * inner_grad
+    moved = after(drift, mean) + inner_rate * inner_grad
 
     def product_shapes():
         return (width, 2 * rank), (rows // rep_size, 2 * rank)
@@ -370,7 +423,7 @@
         if repeat < 2:
             grad = half_of_grad(after(cotangent, packed), every_row, repeat, grad)
         summed = gather_rows(scatter_sum(packed, everything, everyone), everything, everyone)
-        summed, grad = lax.optimization_barrier((summed, grad))
+        summed, grad, moved = lax.optimization_barrier((summed, grad, moved))
         if repeat < ROUNDS - 1:
             packed, left_part = small_call(
                 functools.partial(round_kernel, False), product_shapes(), summed, mean

time: 319 us -> 311 us (0.975)
  blocking collectives: 68.6 us -> 35.5 us
  waiting for transfers between devices: 106 us -> 119 us
  Pallas kernels: 68.7 us -> 78.7 us
  other arithmetic: 20.3 us -> 10.9 us
  starting transfers between devices: 30.6 us -> 39.6 us
  local copies, waits for them, and re-layouts: 8.73 us -> 12.1 us
    all_to_all x3 -> x2, blocking collectives: 68.6 us -> 35.5 us  [scatter_sum(): got = lax.all_to_all(value, axes, 0, 0, tiled=True)]
    ppermute x11, waiting for transfers between devices: 65.2 us -> 91.2 us  [hop(): return lax.ppermute(value, 'fsdp', pairs)]
    all_to_all x1 -> x2, waiting for transfers between devices: 28.4 us -> 16.2 us  [scatter_sum(): got = lax.all_to_all(value, axes, 0, 0, tiled=True)]
    pallas_call x0 -> x2, Pallas kernels: none -> 9.27 us  [stage(): pl.pallas_call(kernel, grid=(width // columns,), in_specs=[by_columns(x.s...]
    all_to_all x1 -> x2, starting transfers between devices: 3.95 us -> 11.5 us  [scatter_sum(): got = lax.all_to_all(value, axes, 0, 0, tiled=True)]
    unnamed x48 -> x40, local copies, waits for them, and re-layouts: 4.88 us -> 8.29 us
    add x4 -> x2, other arithmetic: 6.73 us -> 3.36 us  [add(): total = total + value.astype(f32)]
  transfers between devices with their start and end apart: 17 -> 18, of which waited for: 10 -> 11; matrix products, arithmetic and copies ran while one was open for 8% -> 5% of each run, Pallas kernels for 20% -> 24%
where the time goes in v5:
time: 311 us; the launch traced here: 310 us
  waiting for transfers between devices  119 us (38%)
  Pallas kernels  78.7 us (25%)
  starting transfers between devices  39.6 us (13%)
  blocking collectives  35.5 us (11%)
  between operations  14.3 us (5%)
  local copies, waits for them, and re-layouts  12.1 us (4%)
  other arithmetic  10.9 us (4%)
    ppermute x11, waiting for transfers between devices, hop(): return lax.ppermute(value, 'fsdp', pairs)  91.2 us
    all_to_all x2, blocking collectives, scatter_sum(): got = lax.all_to_all(value, axes, 0, 0, tiled=True)  35.5 us
    pallas_call x4, Pallas kernels, term_blocks(): pl.pallas_call(kernel, grid_spec=pltpu.PrefetchScalarGridSpec(num_scalar_...  30.9 us
    pallas_call x2, Pallas kernels, half_of_grad(): pl.pallas_call(grad_kernel, grid=(steps,), in_specs=in_specs, out_specs=p...  17.7 us
    pallas_call x3, Pallas kernels, small_call(): pl.pallas_call(kernel, out_shape=[jax.ShapeDtypeStruct(shape, f32) for sh...  16.3 us
    all_to_all x2, waiting for transfers between devices, scatter_sum(): got = lax.all_to_all(value, axes, 0, 0, tiled=True)  16.2 us
    ppermute x11, starting transfers between devices, hop(): return lax.ppermute(value, 'fsdp', pairs)  15 us
    all_to_all x3, starting transfers between devices, gather_rows(): return lax.all_to_all(sent, axes, 0, 0, tiled=True)  13.1 us
  transfers between devices with their start and end apart: 18, of which 11 were waited for; matrix products, arithmetic and copies ran while one was open for 5% of the time, Pallas kernels for 24%

profile of v5, /device:TPU:1, one launch (start us, length us, event | category | flops | bytes accessed | tf_op | source)
XLA Modules:
  0.0 309.8 jit_solution(8348640620524733080)
XLA Ops:
  9.1 6.8 %shard_map.119 = bf16[4,512,1024]{2,1,0:T(8,128)(2,1)} custom-call(s32[16]{0:T(128)} %dynamic-slice_bitcast_fusion.spots, bf16[512,8192]{1,0:T(8,128)(2,1)} %bitcast.33, bf16[512,1024]{1,0:T(8,128)(2,1)} %bitcast.39), custom_call_target="tpu_custom_call" | custom-call | flops 2147483648 | bytes 10485760 | tf_op jit(solution)/shard_map/pallas_call | solution.py:130
  17.3 6.8 %shard_map.120 = bf16[4,512,1024]{2,1,0:T(8,128)(2,1)} custom-call(s32[16]{0:T(128)} %dynamic-slice_bitcast_fusion.spots, bf16[512,8192]{1,0:T(8,128)(2,1)} %bitcast.34, bf16[512,1024]{1,0:T(8,128)(2,1)} %bitcast.40), custom_call_target="tpu_custom_call" | custom-call | flops 2147483648 | bytes 10485760 | tf_op jit(solution)/shard_map/pallas_call | solution.py:130
  24.8 8.7 %shard_map.121 = (bf16[2,320,1024]{2,1,0:T(8,128)(2,1)}, bf16[320,1024]{1,0:T(8,128)(2,1)}, bf16[320,1024]{1,0:T(8,128)(2,1)}, bf16[2,192,1024]{2,1,0:T(8,128)(2,1)}, bf16[2,192,1024]{2,1,0:T(8,128)(2,1)}) custom-call(s32[16]{0:T(128)} %dynamic-slice_bitcast_fusion.spots, bf16[512,8192]{1,0:T(8,128)(2,1)} %bitcast.35, bf16[512,1024]{1,0:T(8,128)(2,1)} %bitcast.41, ...), custom_call_target="tpu_custom_call" | custom-call | flops 2147483648 | bytes 10485760 | tf_op jit(solution)/shard_map/pallas_call | solution.py:130
  35.2 8.6 %shard_map.122 = (bf16[2,320,1024]{2,1,0:T(8,128)(2,1)}, bf16[320,1024]{1,0:T(8,128)(2,1)}, bf16[320,1024]{1,0:T(8,128)(2,1)}, bf16[2,192,1024]{2,1,0:T(8,128)(2,1)}, bf16[2,192,1024]{2,1,0:T(8,128)(2,1)}) custom-call(s32[16]{0:T(128)} %dynamic-slice_bitcast_fusion.spots, bf16[512,8192]{1,0:T(8,128)(2,1)} %bitcast.36, bf16[512,1024]{1,0:T(8,128)(2,1)} %bitcast.42, ...), custom_call_target="tpu_custom_call" | custom-call | flops 2147483648 | bytes 10485760 | tf_op jit(solution)/shard_map/pallas_call | solution.py:130
  48.9 18.7 %collective-permute-done.4.up_crossed = bf16[2,192,1024]{2,1,0:T(8,128)(2,1)} collective-permute-done((bf16[2,192,1024]{2,1,0:T(8,128)(2,1)}, bf16[2,192,1024]{2,1,0:T(8,128)(2,1)}, u32[]{:S(2)}, u32[]{:S(2)}) %collective-permute-start.4) | collective-permute-done | bytes 786464 | tf_op jit(solution)/shard_map/ppermute | solution.py:33
  67.6 17.4 %collective-permute-done.2.below.plain_below = bf16[2,320,1024]{2,1,0:T(8,128)(2,1)S(1)} collective-permute-done((bf16[2,320,1024]{2,1,0:T(8,128)(2,1)}, bf16[2,320,1024]{2,1,0:T(8,128)(2,1)S(1)}, u32[]{:S(2)}, u32[]{:S(2)}) %collective-permute-start.2) | collective-permute-done | bytes 1310752 | tf_op jit(solution)/shard_map/ppermute | solution.py:33
  85.1 16.3 %collective-permute-done.5.down_crossed = bf16[2,192,1024]{2,1,0:T(8,128)(2,1)} collective-permute-done((bf16[2,192,1024]{2,1,0:T(8,128)(2,1)}, bf16[2,192,1024]{2,1,0:T(8,128)(2,1)}, u32[]{:S(2)}, u32[]{:S(2)}) %collective-permute-start.5) | collective-permute-done | bytes 786464 | tf_op jit(solution)/shard_map/ppermute | solution.py:33
  102.4 5.2 %shard_map.123 = (bf16[512,1024]{1,0:T(8,128)(2,1)}, bf16[512,1024]{1,0:T(8,128)(2,1)}, f32[96,1024]{1,0:T(8,128)}, f32[96,1024]{1,0:T(8,128)}, f32[192,1024]{1,0:T(8,128)}) custom-call(bf16[320,1024]{1,0:T(8,128)(2,1)} %get-tuple-element.61.up_y0, bf16[320,1024]{1,0:T(8,128)(2,1)} %get-tuple-element.64.down_y1, bf16[2,320,1024]{2,1,0:T(8,128)(2,1)} %copy-done.10, ...), custom_call_target="tpu_custom_call" | custom-call | flops 10000000 | bytes 8388608 | tf_op jit(solution)/shard_map/pallas_call | solution.py:323
  112.0 4.5 %all-to-all-start = ((f32[8,64,1024]{2,1,0:T(8,128)}), f32[8,64,1024]{2,1,0:T(8,128)S(1)}, u32[]{:S(2)}, u32[]{:S(2)}) async-start(f32[8,64,1024]{2,1,0:T(8,128)} %bitcast.5), calls=%async_computation | async-start | bytes 4194304 | tf_op jit(solution)/shard_map/all_to_all | solution.py:43
  119.3 25.7 %collective-permute-done.6.below_again = bf16[512,1024]{1,0:T(8,128)(2,1)S(1)} collective-permute-done((bf16[512,1024]{1,0:T(8,128)(2,1)}, bf16[512,1024]{1,0:T(8,128)(2,1)S(1)}, u32[]{:S(2)}, u32[]{:S(2)}) %collective-permute-start.6) | collective-permute-done | bytes 1048608 | tf_op jit(solution)/shard_map/ppermute | solution.py:33
  154.0 8.8 %collective-permute-done.10 = bf16[96,1024]{1,0:T(8,128)(2,1)} collective-permute-done((bf16[96,1024]{1,0:T(8,128)(2,1)}, bf16[96,1024]{1,0:T(8,128)(2,1)}, u32[]{:S(2)}, u32[]{:S(2)}) %collective-permute-start.10) | collective-permute-done | bytes 196640 | tf_op jit(solution)/shard_map/ppermute | solution.py:33
  171.6 17.5 %all_to_all.59 = bf16[8,64,1024]{2,1,0:T(8,128)(2,1)S(1)} all-to-all(bf16[8,64,1024]{2,1,0:T(8,128)(2,1)S(1)} %bitcast.48), channel_id=1, replica_groups=mesh['rep'=8,'fsdp'=16] {'rep'}, dimensions={0} | all-to-all | bytes 2097152 | tf_op jit(solution)/shard_map/all_to_all | solution.py:43
  191.4 7.0 %all-to-all-start.2 = ((f32[128,8,128]{2,1,0:T(8,128)}), f32[128,8,128]{2,1,0:T(8,128)S(1)}, u32[]{:S(2)}, u32[]{:S(2)}) async-start(f32[128,8,128]{2,1,0:T(8,128)} %bitcast.8), calls=%async_computation.2 | async-start | bytes 1048576 | tf_op jit(solution)/shard_map/all_to_all | solution.py:43
  198.4 16.2 %all-to-all-done.2 = f32[128,8,128]{2,1,0:T(8,128)S(1)} async-done(((f32[128,8,128]{2,1,0:T(8,128)}), f32[128,8,128]{2,1,0:T(8,128)S(1)}, u32[]{:S(2)}, u32[]{:S(2)}) %all-to-all-start.2) | async-done | bytes 524320 | tf_op jit(solution)/shard_map/all_to_all | solution.py:43
  215.6 5.1 %all-to-all-start.3 = ((f32[128,8,128]{2,1,0:T(8,128)}), f32[128,8,128]{2,1,0:T(8,128)S(1)}, u32[]{:S(2)}, u32[]{:S(2)}) async-start(f32[128,8,128]{2,1,0:T(8,128)} %broadcast_in_dim.38), calls=%async_computation.3 | async-start | bytes 1048576 | tf_op jit(solution)/shard_map/all_to_all | solution.py:50
  223.4 8.9 %shard_map.126.refs_0_ = bf16[512,8192]{1,0:T(8,128)(2,1)} custom-call(bf16[512,1024]{1,0:T(8,128)(2,1)} %bitcast.43, bf16[8192,1024]{1,0:T(8,128)(2,1)} %bitcast.37), custom_call_target="tpu_custom_call" | custom-call | flops 4294967296 | bytes 12582912 | tf_op jit(solution)/shard_map/pallas_call | solution.py:167
  232.3 5.7 %all-to-all-done.3 = f32[128,8,128]{2,1,0:T(8,128)S(1)} async-done(((f32[128,8,128]{2,1,0:T(8,128)}), f32[128,8,128]{2,1,0:T(8,128)S(1)}, u32[]{:S(2)}, u32[]{:S(2)}) %all-to-all-start.3) | async-done | bytes 524320 | tf_op jit(solution)/shard_map/all_to_all | solution.py:50
  238.0 8.1 %shard_map.127 = (f32[1024,128]{1,0:T(8,128)S(1)}, f32[64,128]{1,0:T(8,128)S(1)}) custom-call(f32[1024,128]{1,0:T(8,128)S(1)} %bitcast.31, f32[64,1024]{1,0:T(8,128)S(1)} %add_multiply_fusion.mean), custom_call_target="tpu_custom_call" | custom-call | flops 1000000000 | bytes 2097152 | tf_op jit(solution)/shard_map/pallas_call | solution.py:266
  246.0 18.0 %all_to_all.60 = f32[128,8,128]{2,1,0:T(8,128)S(1)} all-to-all(f32[128,8,128]{2,1,0:T(8,128)S(1)} %bitcast.32), channel_id=1, replica_groups=mesh['rep'=8,'fsdp'=16] {'rep','fsdp'}, dimensions={0} | all-to-all | bytes 1048576 | tf_op jit(solution)/shard_map/all_to_all | solution.py:43
  265.0 4.5 %all-to-all-start.5 = ((f32[128,8,128]{2,1,0:T(8,128)}), f32[128,8,128]{2,1,0:T(8,128)S(1)}, u32[]{:S(2)}, u32[]{:S(2)}) async-start(f32[128,8,128]{2,1,0:T(8,128)} %broadcast_in_dim.39), calls=%async_computation.5 | async-start | bytes 1048576 | tf_op jit(solution)/shard_map/all_to_all | solution.py:50
  269.5 8.9 %shard_map.128 = bf16[512,8192]{1,0:T(8,128)(2,1)} custom-call(bf16[512,1024]{1,0:T(8,128)(2,1)} %bitcast.44, bf16[8192,1024]{1,0:T(8,128)(2,1)} %bitcast.38, bf16[512,8192]{1,0:T(8,128)(2,1)} %shard_map.126.refs_0_), custom_call_target="tpu_custom_call", output_to_operand_aliasing={{}: (2, {})} | custom-call | flops 4294967296 | bytes 12582912 | tf_op jit(solution)/shard_map/pallas_call | solution.py:167
  278.4 4.9 %all-to-all-done.5 = f32[128,8,128]{2,1,0:T(8,128)S(1)} async-done(((f32[128,8,128]{2,1,0:T(8,128)}), f32[128,8,128]{2,1,0:T(8,128)S(1)}, u32[]{:S(2)}, u32[]{:S(2)}) %all-to-all-start.5) | async-done | bytes 524320 | tf_op jit(solution)/shard_map/all_to_all | solution.py:50
  289.6 6.4 %shard_map.129 = (f32[1024,64]{1,0:T(8,128)S(1)}, f32[64,64]{1,0:T(8,128)S(1)}) custom-call(f32[1024,128]{1,0:T(8,128)S(1)} %bitcast.30, f32[64,1024]{1,0:T(8,128)S(1)} %copy-done.7), custom_call_target="tpu_custom_call" | custom-call | flops 1000000000 | bytes 2097152 | tf_op jit(solution)/shard_map/pallas_call | solution.py:266
  298.5 4.5 %shard_map.130 = (f32[512,1024]{1,0:T(8,128)}, f32[512,128]{1,0:T(8,128)}, f32[512,128]{1,0:T(8,128)}) custom-call(s32[1]{0:T(128)} %bitcast.14.my_rep, f32[512,128]{1,0:T(8,128)S(1)} %bitcast.29, f32[64,64]{1,0:T(8,128)S(1)} %get-tuple-element.106.inverse, f32[1024,64]{1,0:T(8,128)S(1)} %get-tuple-element.117.factor, ...), custom_call_target="tpu_custom_call" | custom-call | flops 1000000000 | bytes 8388608 | tf_op jit(solution)/shard_map/pallas_call | solution.py:207
  (86 shorter events, 52.6 us)
Async XLA Ops:
  7.2 216.2 %all-gather.3.cloned.1.call-start = ((), (), s32[]{:S(2)}) async-start(), calls=%async_computation.7 | async-start | bytes 17825792 | tf_op jit(solution)/shard_map/all_gather | solution.py:420
  15.9 8.6 %collective-permute-start = (bf16[4,512,1024]{2,1,0:T(8,128)(2,1)}, bf16[4,512,1024]{2,1,0:T(8,128)(2,1)}, u32[]{:S(2)}, u32[]{:S(2)}) collective-permute-start(bf16[4,512,1024]{2,1,0:T(8,128)(2,1)} %shard_map.119), channel_id=1, source_target_pairs={{0,1},{1,0},{2,3},{3,2},{4,5},{5,4},{6,7},{7,6},{8,9},{9,8},{10,11... | collective-permute-start | bytes 12582920 | tf_op jit(solution)/shard_map/ppermute | solution.py:33
  24.4 10.7 %collective-permute-start.1 = (bf16[4,512,1024]{2,1,0:T(8,128)(2,1)}, bf16[4,512,1024]{2,1,0:T(8,128)(2,1)}, u32[]{:S(2)}, u32[]{:S(2)}) collective-permute-start(bf16[4,512,1024]{2,1,0:T(8,128)(2,1)} %shard_map.120), channel_id=1, source_target_pairs={{0,1},{1,0},{2,3},{3,2},{4,5},{5,4},{6,7},{7,6},{8,9},{9,8},{10,11... | collective-permute-start | bytes 12582920 | tf_op jit(solution)/shard_map/ppermute | solution.py:33
  33.6 51.5 %collective-permute-start.2 = (bf16[2,320,1024]{2,1,0:T(8,128)(2,1)}, bf16[2,320,1024]{2,1,0:T(8,128)(2,1)S(1)}, u32[]{:S(2)}, u32[]{:S(2)}) collective-permute-start(bf16[2,320,1024]{2,1,0:T(8,128)(2,1)} %get-tuple-element.65), channel_id=1, source_target_pairs={{0,2},{1,3},{2,4},{3,5},{4,6},{5,7},{6,0},{7,1},{8,10},{9,11},{10,... | collective-permute-start | bytes 3932168 | tf_op jit(solution)/shard_map/ppermute | solution.py:33
  43.8 57.6 %collective-permute-start.3 = (bf16[2,320,1024]{2,1,0:T(8,128)(2,1)}, bf16[2,320,1024]{2,1,0:T(8,128)(2,1)S(1)}, u32[]{:S(2)}, u32[]{:S(2)}) collective-permute-start(bf16[2,320,1024]{2,1,0:T(8,128)(2,1)} %get-tuple-element.66), channel_id=1, source_target_pairs={{0,6},{1,7},{2,0},{3,1},{4,2},{5,3},{6,4},{7,5},{8,14},{9,15},{10,... | collective-permute-start | bytes 3932168 | tf_op jit(solution)/shard_map/ppermute | solution.py:33
  45.9 21.7 %collective-permute-start.4 = (bf16[2,192,1024]{2,1,0:T(8,128)(2,1)}, bf16[2,192,1024]{2,1,0:T(8,128)(2,1)}, u32[]{:S(2)}, u32[]{:S(2)}) collective-permute-start(bf16[2,192,1024]{2,1,0:T(8,128)(2,1)} %get-tuple-element.67), channel_id=1, source_target_pairs={{0,8},{1,9},{2,10},{3,11},{4,12},{5,13},{6,14},{7,15},{8,0},{9,1},... | collective-permute-start | bytes 2359304 | tf_op jit(solution)/shard_map/ppermute | solution.py:33
  48.8 52.5 %collective-permute-start.5 = (bf16[2,192,1024]{2,1,0:T(8,128)(2,1)}, bf16[2,192,1024]{2,1,0:T(8,128)(2,1)}, u32[]{:S(2)}, u32[]{:S(2)}) collective-permute-start(bf16[2,192,1024]{2,1,0:T(8,128)(2,1)} %get-tuple-element.68), channel_id=1, source_target_pairs={{0,8},{1,9},{2,10},{3,11},{4,12},{5,13},{6,14},{7,15},{8,0},{9,1},... | collective-permute-start | bytes 2359304 | tf_op jit(solution)/shard_map/ppermute | solution.py:33
  85.1 16.3 %copy-start.10 = (bf16[2,320,1024]{2,1,0:T(8,128)(2,1)}, bf16[2,320,1024]{2,1,0:T(8,128)(2,1)S(1)}, u32[]{:S(2)}) copy-start(bf16[2,320,1024]{2,1,0:T(8,128)(2,1)S(1)} %collective-permute-done.2.below.plain_below) | copy-start | bytes 3932164
  112.0 41.8 %all-to-all-start = ((f32[8,64,1024]{2,1,0:T(8,128)}), f32[8,64,1024]{2,1,0:T(8,128)S(1)}, u32[]{:S(2)}, u32[]{:S(2)}) async-start(f32[8,64,1024]{2,1,0:T(8,128)} %bitcast.5), calls=%async_computation | async-start | bytes 4194304 | tf_op jit(solution)/shard_map/all_to_all | solution.py:43
  116.5 180.4 %all-gather.5.cloned.1.call-start = ((), (), s32[]{:S(2)}) async-start(), calls=%async_computation.8 | async-start | bytes 2359296 | tf_op jit(solution)/shard_map/all_gather | solution.py:419
  116.6 28.4 %collective-permute-start.6 = (bf16[512,1024]{1,0:T(8,128)(2,1)}, bf16[512,1024]{1,0:T(8,128)(2,1)S(1)}, u32[]{:S(2)}, u32[]{:S(2)}) collective-permute-start(bf16[512,1024]{1,0:T(8,128)(2,1)} %get-tuple-element.75), channel_id=1, source_target_pairs={{0,2},{1,3},{2,4},{3,5},{4,6},{5,7},{6,0},{7,1},{8,10},{9,11},{10,... | collective-permute-start | bytes 3145736 | tf_op jit(solution)/shard_map/ppermute | solution.py:33
  116.7 28.3 %collective-permute-start.7 = (bf16[512,1024]{1,0:T(8,128)(2,1)}, bf16[512,1024]{1,0:T(8,128)(2,1)}, u32[]{:S(2)}, u32[]{:S(2)}) collective-permute-start(bf16[512,1024]{1,0:T(8,128)(2,1)} %get-tuple-element.76), channel_id=1, source_target_pairs={{0,6},{1,7},{2,0},{3,1},{4,2},{5,3},{6,4},{7,5},{8,14},{9,15},{10,... | collective-permute-start | bytes 3145736 | tf_op jit(solution)/shard_map/ppermute | solution.py:33
  150.1 16.7 %copy-start.13 = (bf16[512,1024]{1,0:T(8,128)(2,1)S(1)}, bf16[512,1024]{1,0:T(8,128)(2,1)}, u32[]{:S(2)}) copy-start(bf16[512,1024]{1,0:T(8,128)(2,1)} %copy-done.12) | copy-start | bytes 3145732
  150.1 16.7 %collective-permute-start.8 = (bf16[320,1024]{1,0:T(8,128)(2,1)}, bf16[320,1024]{1,0:T(8,128)(2,1)}, u32[]{:S(2)}, u32[]{:S(2)}) collective-permute-start(bf16[320,1024]{1,0:T(8,128)(2,1)} %get-tuple-element.84), channel_id=1, source_target_pairs={{0,8},{1,9},{2,10},{3,11},{4,12},{5,13},{6,14},{7,15},{8,0},{9,1},... | collective-permute-start | bytes 1966088 | tf_op jit(solution)/shard_map/ppermute | solution.py:33
  152.3 10.4 %collective-permute-start.10 = (bf16[96,1024]{1,0:T(8,128)(2,1)}, bf16[96,1024]{1,0:T(8,128)(2,1)}, u32[]{:S(2)}, u32[]{:S(2)}) collective-permute-start(bf16[96,1024]{1,0:T(8,128)(2,1)} %get-tuple-element.86), channel_id=1, source_target_pairs={{0,6},{1,7},{2,0},{3,1},{4,2},{5,3},{6,4},{7,5},{8,14},{9,15},{10,... | collective-permute-start | bytes 589832 | tf_op jit(solution)/shard_map/ppermute | solution.py:33
  152.3 11.4 %collective-permute-start.9 = (bf16[96,1024]{1,0:T(8,128)(2,1)}, bf16[96,1024]{1,0:T(8,128)(2,1)}, u32[]{:S(2)}, u32[]{:S(2)}) collective-permute-start(bf16[96,1024]{1,0:T(8,128)(2,1)} %get-tuple-element.85), channel_id=1, source_target_pairs={{0,2},{1,3},{2,4},{3,5},{4,6},{5,7},{6,0},{7,1},{8,10},{9,11},{10,... | collective-permute-start | bytes 589832 | tf_op jit(solution)/shard_map/ppermute | solution.py:33
  154.0 15.6 %copy-start.15 = (bf16[2,320,1024]{2,1,0:T(8,128)(2,1)S(1)}, bf16[2,320,1024]{2,1,0:T(8,128)(2,1)}, u32[]{:S(2)}) copy-start(bf16[2,320,1024]{2,1,0:T(8,128)(2,1)} %copy-done.14) | copy-start | bytes 3932164
  171.4 17.7 %copy-start.8 = (f32[320,1024]{1,0:T(8,128)}, f32[320,1024]{1,0:T(8,128)S(1)}, u32[]{:S(2)}) copy-start(f32[320,1024]{1,0:T(8,128)S(1)} %fusion.2) | copy-start | bytes 3932164
  171.6 17.7 %copy-start.18 = (f32[1024,64]{0,1:T(8,128)S(1)}, f32[1024,64]{0,1:T(8,128)}, u32[]{:S(2)}) copy-start(f32[1024,64]{0,1:T(8,128)} %param.14) | copy-start | bytes 786436
  189.3 48.7 %copy-start.6 = (f32[64,1024]{1,0:T(8,128)}, f32[64,1024]{1,0:T(8,128)S(1)}, u32[]{:S(2)}) copy-start(f32[64,1024]{1,0:T(8,128)S(1)} %add_multiply_fusion.mean) | copy-start | bytes 786436
  191.4 23.2 %all-to-all-start.2 = ((f32[128,8,128]{2,1,0:T(8,128)}), f32[128,8,128]{2,1,0:T(8,128)S(1)}, u32[]{:S(2)}, u32[]{:S(2)}) async-start(f32[128,8,128]{2,1,0:T(8,128)} %bitcast.8), calls=%async_computation.2 | async-start | bytes 1048576 | tf_op jit(solution)/shard_map/all_to_all | solution.py:43
  215.6 22.4 %all-to-all-start.3 = ((f32[128,8,128]{2,1,0:T(8,128)}), f32[128,8,128]{2,1,0:T(8,128)S(1)}, u32[]{:S(2)}, u32[]{:S(2)}) async-start(f32[128,8,128]{2,1,0:T(8,128)} %broadcast_in_dim.38), calls=%async_computation.3 | async-start | bytes 1048576 | tf_op jit(solution)/shard_map/all_to_all | solution.py:50
  265.0 18.3 %all-to-all-start.5 = ((f32[128,8,128]{2,1,0:T(8,128)}), f32[128,8,128]{2,1,0:T(8,128)S(1)}, u32[]{:S(2)}, u32[]{:S(2)}) async-start(f32[128,8,128]{2,1,0:T(8,128)} %broadcast_in_dim.39), calls=%async_computation.5 | async-start | bytes 1048576 | tf_op jit(solution)/shard_map/all_to_all | solution.py:50
  284.2 12.7 %all-to-all-start.6 = ((f32[8,64,128]{2,1,0:T(8,128)}), f32[8,64,128]{2,1,0:T(8,128)S(1)}, u32[]{:S(2)}, u32[]{:S(2)}) async-start(f32[8,64,128]{2,1,0:T(8,128)} %broadcast_in_dim.41), calls=%async_computation.6 | async-start | bytes 524288 | tf_op jit(solution)/shard_map/all_to_all | solution.py:50
  (13 other events, 57.0 us)
Sparse Core Ops, SparseCore 0:
  10.5 162.1 all-gather.2
  189.5 48.5 all-gather.4

commit v6 on v5

--- a/solution.py
+++ b/solution.py
@@ -20,7 +20,7 @@
 bf16 = jnp.bfloat16
 
 NZ = 4
-FIRST = 320
+FIRST = 352
 PLACES = [(y, z, c) for y in range(2) for z in range(NZ) for c in range(2)]
 
 
@@ -226,26 +226,31 @@
     row = lax.broadcasted_iota(jnp.int32, (rank, rank), 0)
     lane = lax.broadcasted_iota(jnp.int32, (rank, rank), 1)
     work = jnp.concatenate([gram, (row == lane).astype(f32)], axis=1)
-    tall = lax.broadcasted_iota(jnp.int32, (rank, 1), 0)
-    scales = jnp.zeros((rank, 1), f32)
+    groups = [work[at : at + 8] for at in range(0, rank, 8)]
+    tall = lax.broadcasted_iota(jnp.int32, (8, 1), 0)
     for step in range(rank):
-        column = work[:, step : step + 1]
-        pivot = work[step : step + 1, step : step + 1]
-        scales = jnp.where(tall == step, lax.rsqrt(pivot), scales)
-        ratio = jnp.where(tall > step, column / pivot, 0.0)
-        work = work - ratio * work[step : step + 1, :]
-    return work[:, rank:] * scales
-
-
-def round_kernel(last, summed, mean, *outs):
+        at, inner = step // 8, step % 8
+        pivot_row = groups[at][inner : inner + 1]
+        scaled = pivot_row / pivot_row[:, step : step + 1]
+        for index in range(at, len(groups)):
+            column = groups[index][:, step : step + 1]
+            if index == at:
+                column = jnp.where(tall > inner, column, 0.0)
+            groups[index] = groups[index] - column * scaled
+    work = jnp.concatenate(groups)
+    pivots = jnp.sum(jnp.where(row == lane, work[:, :rank], 0.0), axis=1, keepdims=True)
+    return work[:, rank:] * lax.rsqrt(pivots)
+
+
+def round_kernel(last, summed, *refs):
     rank = summed.shape[1] // 2
     inverse = inverse_of_lower_factor(summed[:rank, rank:])
     factor = dot(summed[:, :rank], inverse, ((1,), (1,)))
     if last:
-        outs[0][...] = factor
-        outs[1][...] = inverse
+        refs[0][...] = factor
+        refs[1][...] = inverse
         return
-    product_kernel_body(mean[...], factor, *outs)
+    product_kernel_body(refs[0][...], factor, *refs[1:])
 
 
 def product_kernel_body(mean, factor, packed, left):
@@ -372,8 +377,8 @@
         own_y1, below, above_again, below_again, up_up, down_down,
     )
     crossed = hop(sent, dy=1)
-    early, crossed, last_below, last_above = lax.optimization_barrier(
-        (early, crossed, hop(second_up, dz=1), hop(second_down, dz=-1))
+    crossed, last_below, last_above = lax.optimization_barrier(
+        (crossed, hop(second_up, dz=1), hop(second_down, dz=-1))
     )
 
     second_sum = own_second + jnp.concatenate(
@@ -430,7 +435,7 @@
             )
     left = gather_rows(after(left_part, summed), "rep", rep_size)
     factor, inverse = small_call(
-        functools.partial(round_kernel, True), ((width, rank), (rank, rank)), summed, mean
+        functools.partial(round_kernel, True), ((width, rank), (rank, rank)), summed
     )
     feedback_out, base_out, momentum_out = final_outputs(
         my_rep, left, inverse, factor, moved, full_base, base, momentum

time: 311 us -> 307 us (0.987)
  blocking collectives: 35.5 us -> 18.8 us
  waiting for transfers between devices: 119 us -> 129 us
  starting transfers between devices: 39.6 us -> 43.4 us
    all_to_all x2 -> x1, blocking collectives: 35.5 us -> 18.8 us  [scatter_sum(): got = lax.all_to_all(value, axes, 0, 0, tiled=True)]
    all_to_all x2 -> x3, waiting for transfers between devices: 16.2 us -> 31.7 us  [scatter_sum(): got = lax.all_to_all(value, axes, 0, 0, tiled=True)]
    all_to_all x2 -> x3, starting transfers between devices: 11.5 us -> 16.8 us  [scatter_sum(): got = lax.all_to_all(value, axes, 0, 0, tiled=True)]
    ppermute x11, waiting for transfers between devices: 91.2 us -> 87.2 us  [hop(): return lax.ppermute(value, 'fsdp', pairs)]
  transfers between devices with their start and end apart: 18 -> 19, of which waited for: 11 -> 12; matrix products, arithmetic and copies ran while one was open for 5% -> 5% of each run, Pallas kernels for 24% -> 24%
where the time goes in v6:
time: 307 us; the launch traced here: 306 us
  waiting for transfers between devices  129 us (42%)
  Pallas kernels  77.9 us (25%)
  starting transfers between devices  43.4 us (14%)
  blocking collectives  18.8 us (6%)
  between operations  14.3 us (5%)
  local copies, waits for them, and re-layouts  12.2 us (4%)
  other arithmetic  10.3 us (3%)
    ppermute x11, waiting for transfers between devices, hop(): return lax.ppermute(value, 'fsdp', pairs)  87.2 us
    all_to_all x3, waiting for transfers between devices, scatter_sum(): got = lax.all_to_all(value, axes, 0, 0, tiled=True)  31.7 us
    pallas_call x4, Pallas kernels, term_blocks(): pl.pallas_call(kernel, grid_spec=pltpu.PrefetchScalarGridSpec(num_scalar_...  30.9 us
    all_to_all x1, blocking collectives, scatter_sum(): got = lax.all_to_all(value, axes, 0, 0, tiled=True)  18.8 us
    pallas_call x2, Pallas kernels, half_of_grad(): pl.pallas_call(grad_kernel, grid=(steps,), in_specs=in_specs, out_specs=p...  17.8 us
    all_to_all x3, starting transfers between devices, scatter_sum(): got = lax.all_to_all(value, axes, 0, 0, tiled=True)  16.8 us
    pallas_call x3, Pallas kernels, small_call(): pl.pallas_call(kernel, out_shape=[jax.ShapeDtypeStruct(shape, f32) for sh...  15.7 us
    all_to_all x3, starting transfers between devices, gather_rows(): return lax.all_to_all(sent, axes, 0, 0, tiled=True)  13.7 us
  transfers between devices with their start and end apart: 19, of which 12 were waited for; matrix products, arithmetic and copies ran while one was open for 5% of the time, Pallas kernels for 24%

profile of v6, /device:TPU:1, one launch (start us, length us, event | category | flops | bytes accessed | tf_op | source)
XLA Modules:
  0.0 305.8 jit_solution(12232634656367872764)
XLA Ops:
  9.1 6.8 %shard_map.119 = bf16[4,512,1024]{2,1,0:T(8,128)(2,1)} custom-call(s32[16]{0:T(128)} %dynamic-slice_bitcast_fusion.spots, bf16[512,8192]{1,0:T(8,128)(2,1)} %bitcast.33, bf16[512,1024]{1,0:T(8,128)(2,1)} %bitcast.39), custom_call_target="tpu_custom_call" | custom-call | flops 2147483648 | bytes 10485760 | tf_op jit(solution)/shard_map/pallas_call | solution.py:130
  17.3 6.8 %shard_map.120 = bf16[4,512,1024]{2,1,0:T(8,128)(2,1)} custom-call(s32[16]{0:T(128)} %dynamic-slice_bitcast_fusion.spots, bf16[512,8192]{1,0:T(8,128)(2,1)} %bitcast.34, bf16[512,1024]{1,0:T(8,128)(2,1)} %bitcast.40), custom_call_target="tpu_custom_call" | custom-call | flops 2147483648 | bytes 10485760 | tf_op jit(solution)/shard_map/pallas_call | solution.py:130
  24.8 8.8 %shard_map.121 = (bf16[2,352,1024]{2,1,0:T(8,128)(2,1)}, bf16[352,1024]{1,0:T(8,128)(2,1)}, bf16[352,1024]{1,0:T(8,128)(2,1)}, bf16[2,160,1024]{2,1,0:T(8,128)(2,1)}, bf16[2,160,1024]{2,1,0:T(8,128)(2,1)}) custom-call(s32[16]{0:T(128)} %dynamic-slice_bitcast_fusion.spots, bf16[512,8192]{1,0:T(8,128)(2,1)} %bitcast.35, bf16[512,1024]{1,0:T(8,128)(2,1)} %bitcast.41, ...), custom_call_target="tpu_custom_call" | custom-call | flops 2147483648 | bytes 10485760 | tf_op jit(solution)/shard_map/pallas_call | solution.py:130
  35.2 8.5 %shard_map.122 = (bf16[2,352,1024]{2,1,0:T(8,128)(2,1)}, bf16[352,1024]{1,0:T(8,128)(2,1)}, bf16[352,1024]{1,0:T(8,128)(2,1)}, bf16[2,160,1024]{2,1,0:T(8,128)(2,1)}, bf16[2,160,1024]{2,1,0:T(8,128)(2,1)}) custom-call(s32[16]{0:T(128)} %dynamic-slice_bitcast_fusion.spots, bf16[512,8192]{1,0:T(8,128)(2,1)} %bitcast.36, bf16[512,1024]{1,0:T(8,128)(2,1)} %bitcast.42, ...), custom_call_target="tpu_custom_call" | custom-call | flops 2147483648 | bytes 10485760 | tf_op jit(solution)/shard_map/pallas_call | solution.py:130
  48.7 14.6 %collective-permute-done.4.up_crossed = bf16[2,160,1024]{2,1,0:T(8,128)(2,1)S(1)} collective-permute-done((bf16[2,160,1024]{2,1,0:T(8,128)(2,1)}, bf16[2,160,1024]{2,1,0:T(8,128)(2,1)S(1)}, u32[]{:S(2)}, u32[]{:S(2)}) %collective-permute-start.4) | collective-permute-done | bytes 655392 | tf_op jit(solution)/shard_map/ppermute | solution.py:33
  63.3 27.3 %collective-permute-done.2.below.plain_below = bf16[2,352,1024]{2,1,0:T(8,128)(2,1)S(1)} collective-permute-done((bf16[2,352,1024]{2,1,0:T(8,128)(2,1)}, bf16[2,352,1024]{2,1,0:T(8,128)(2,1)S(1)}, u32[]{:S(2)}, u32[]{:S(2)}) %collective-permute-start.2) | collective-permute-done | bytes 1441824 | tf_op jit(solution)/shard_map/ppermute | solution.py:33
  95.8 5.0 %shard_map.123 = (bf16[512,1024]{1,0:T(8,128)(2,1)}, bf16[512,1024]{1,0:T(8,128)(2,1)}, f32[80,1024]{1,0:T(8,128)}, f32[80,1024]{1,0:T(8,128)}, f32[160,1024]{1,0:T(8,128)}) custom-call(bf16[352,1024]{1,0:T(8,128)(2,1)} %get-tuple-element.59.up_y0, bf16[352,1024]{1,0:T(8,128)(2,1)} %get-tuple-element.62.down_y1, bf16[2,352,1024]{2,1,0:T(8,128)(2,1)} %copy-done.8, ...), custom_call_target="tpu_custom_call" | custom-call | flops 10000000 | bytes 8388608 | tf_op jit(solution)/shard_map/pallas_call | solution.py:328
  107.6 5.2 %all-to-all-start = ((f32[8,64,1024]{2,1,0:T(8,128)}), f32[8,64,1024]{2,1,0:T(8,128)S(1)}, u32[]{:S(2)}, u32[]{:S(2)}) async-start(f32[8,64,1024]{2,1,0:T(8,128)} %bitcast.5), calls=%async_computation | async-start | bytes 4194304 | tf_op jit(solution)/shard_map/all_to_all | solution.py:43
  112.8 18.6 %collective-permute-done.6.below_again = bf16[512,1024]{1,0:T(8,128)(2,1)S(1)} collective-permute-done((bf16[512,1024]{1,0:T(8,128)(2,1)}, bf16[512,1024]{1,0:T(8,128)(2,1)S(1)}, u32[]{:S(2)}, u32[]{:S(2)}) %collective-permute-start.6) | collective-permute-done | bytes 1048608 | tf_op jit(solution)/shard_map/ppermute | solution.py:33
  143.5 17.1 %collective-permute-done.8 = bf16[352,1024]{1,0:T(8,128)(2,1)S(1)} collective-permute-done((bf16[352,1024]{1,0:T(8,128)(2,1)}, bf16[352,1024]{1,0:T(8,128)(2,1)S(1)}, u32[]{:S(2)}, u32[]{:S(2)}) %collective-permute-start.8) | collective-permute-done | bytes 720928 | tf_op jit(solution)/shard_map/ppermute | solution.py:33
  166.2 5.5 %all-to-all-start.1 = ((bf16[8,64,1024]{2,1,0:T(8,128)(2,1)}), bf16[8,64,1024]{2,1,0:T(8,128)(2,1)S(1)}, u32[]{:S(2)}, u32[]{:S(2)}) async-start(bf16[8,64,1024]{2,1,0:T(8,128)(2,1)} %bitcast.7), calls=%async_computation.1 | async-start | bytes 2097152 | tf_op jit(solution)/shard_map/all_to_all | solution.py:43
  171.9 15.7 %all-to-all-done.1 = bf16[8,64,1024]{2,1,0:T(8,128)(2,1)S(1)} async-done(((bf16[8,64,1024]{2,1,0:T(8,128)(2,1)}), bf16[8,64,1024]{2,1,0:T(8,128)(2,1)S(1)}, u32[]{:S(2)}, u32[]{:S(2)}) %all-to-all-start.1) | async-done | bytes 1048608 | tf_op jit(solution)/shard_map/all_to_all | solution.py:43
  189.8 6.1 %all-to-all-start.2 = ((f32[128,8,128]{2,1,0:T(8,128)}), f32[128,8,128]{2,1,0:T(8,128)S(1)}, u32[]{:S(2)}, u32[]{:S(2)}) async-start(f32[128,8,128]{2,1,0:T(8,128)} %bitcast.8), calls=%async_computation.2 | async-start | bytes 1048576 | tf_op jit(solution)/shard_map/all_to_all | solution.py:43
  195.9 16.0 %all-to-all-done.2 = f32[128,8,128]{2,1,0:T(8,128)S(1)} async-done(((f32[128,8,128]{2,1,0:T(8,128)}), f32[128,8,128]{2,1,0:T(8,128)S(1)}, u32[]{:S(2)}, u32[]{:S(2)}) %all-to-all-start.2) | async-done | bytes 524320 | tf_op jit(solution)/shard_map/all_to_all | solution.py:43
  212.9 5.8 %all-to-all-start.3 = ((f32[128,8,128]{2,1,0:T(8,128)}), f32[128,8,128]{2,1,0:T(8,128)S(1)}, u32[]{:S(2)}, u32[]{:S(2)}) async-start(f32[128,8,128]{2,1,0:T(8,128)} %broadcast_in_dim.38), calls=%async_computation.3 | async-start | bytes 1048576 | tf_op jit(solution)/shard_map/all_to_all | solution.py:50
  221.4 8.9 %shard_map.126.refs_0_ = bf16[512,8192]{1,0:T(8,128)(2,1)} custom-call(bf16[512,1024]{1,0:T(8,128)(2,1)} %bitcast.43, bf16[8192,1024]{1,0:T(8,128)(2,1)} %bitcast.37), custom_call_target="tpu_custom_call" | custom-call | flops 4294967296 | bytes 12582912 | tf_op jit(solution)/shard_map/pallas_call | solution.py:167
  230.3 4.5 %all-to-all-done.3 = f32[128,8,128]{2,1,0:T(8,128)S(1)} async-done(((f32[128,8,128]{2,1,0:T(8,128)}), f32[128,8,128]{2,1,0:T(8,128)S(1)}, u32[]{:S(2)}, u32[]{:S(2)}) %all-to-all-start.3) | async-done | bytes 524320 | tf_op jit(solution)/shard_map/all_to_all | solution.py:50
  234.8 7.8 %shard_map.127 = (f32[1024,128]{1,0:T(8,128)S(1)}, f32[64,128]{1,0:T(8,128)S(1)}) custom-call(f32[1024,128]{1,0:T(8,128)S(1)} %bitcast.31, f32[64,1024]{1,0:T(8,128)S(1)} %add_multiply_fusion.mean.refs_0_), custom_call_target="tpu_custom_call" | custom-call | flops 1000000000 | bytes 2097152 | tf_op jit(solution)/shard_map/pallas_call | solution.py:271
  242.6 18.8 %all_to_all.59 = f32[128,8,128]{2,1,0:T(8,128)S(1)} all-to-all(f32[128,8,128]{2,1,0:T(8,128)S(1)} %bitcast.32), channel_id=1, replica_groups=mesh['rep'=8,'fsdp'=16] {'rep','fsdp'}, dimensions={0} | all-to-all | bytes 1048576 | tf_op jit(solution)/shard_map/all_to_all | solution.py:43
  262.3 4.5 %all-to-all-start.5 = ((f32[128,8,128]{2,1,0:T(8,128)}), f32[128,8,128]{2,1,0:T(8,128)S(1)}, u32[]{:S(2)}, u32[]{:S(2)}) async-start(f32[128,8,128]{2,1,0:T(8,128)} %broadcast_in_dim.39), calls=%async_computation.5 | async-start | bytes 1048576 | tf_op jit(solution)/shard_map/all_to_all | solution.py:50
  266.9 8.9 %shard_map.128 = bf16[512,8192]{1,0:T(8,128)(2,1)} custom-call(bf16[512,1024]{1,0:T(8,128)(2,1)} %bitcast.44, bf16[8192,1024]{1,0:T(8,128)(2,1)} %bitcast.38, bf16[512,8192]{1,0:T(8,128)(2,1)} %shard_map.126.refs_0_), custom_call_target="tpu_custom_call", output_to_operand_aliasing={{}: (2, {})} | custom-call | flops 4294967296 | bytes 12582912 | tf_op jit(solution)/shard_map/pallas_call | solution.py:167
  275.7 4.9 %all-to-all-done.5 = f32[128,8,128]{2,1,0:T(8,128)S(1)} async-done(((f32[128,8,128]{2,1,0:T(8,128)}), f32[128,8,128]{2,1,0:T(8,128)S(1)}, u32[]{:S(2)}, u32[]{:S(2)}) %all-to-all-start.5) | async-done | bytes 524320 | tf_op jit(solution)/shard_map/all_to_all | solution.py:50
  285.9 6.1 %shard_map.129 = (f32[1024,64]{1,0:T(8,128)S(1)}, f32[64,64]{1,0:T(8,128)S(1)}) custom-call(f32[1024,128]{1,0:T(8,128)S(1)} %bitcast.30), custom_call_target="tpu_custom_call" | custom-call | flops 1000000000 | bytes 2097152 | tf_op jit(solution)/shard_map/pallas_call | solution.py:271
  294.5 4.5 %shard_map.130 = (f32[512,1024]{1,0:T(8,128)}, f32[512,128]{1,0:T(8,128)}, f32[512,128]{1,0:T(8,128)}) custom-call(s32[1]{0:T(128)} %bitcast.14.my_rep, f32[512,128]{1,0:T(8,128)S(1)} %bitcast.29, f32[64,64]{1,0:T(8,128)S(1)} %get-tuple-element.102.inverse, f32[1024,64]{1,0:T(8,128)S(1)} %get-tuple-element.113.factor, ...), custom_call_target="tpu_custom_call" | custom-call | flops 1000000000 | bytes 8388608 | tf_op jit(solution)/shard_map/pallas_call | solution.py:207
  (87 shorter events, 54.9 us)
Async XLA Ops:
  7.2 214.2 %all-gather.3.cloned.1.call-start = ((), (), s32[]{:S(2)}) async-start(), calls=%async_computation.7 | async-start | bytes 17825792 | tf_op jit(solution)/shard_map/all_gather | solution.py:425
  15.9 8.6 %collective-permute-start = (bf16[4,512,1024]{2,1,0:T(8,128)(2,1)}, bf16[4,512,1024]{2,1,0:T(8,128)(2,1)}, u32[]{:S(2)}, u32[]{:S(2)}) collective-permute-start(bf16[4,512,1024]{2,1,0:T(8,128)(2,1)} %shard_map.119), channel_id=1, source_target_pairs={{0,1},{1,0},{2,3},{3,2},{4,5},{5,4},{6,7},{7,6},{8,9},{9,8},{10,11... | collective-permute-start | bytes 12582920 | tf_op jit(solution)/shard_map/ppermute | solution.py:33
  24.4 10.8 %collective-permute-start.1 = (bf16[4,512,1024]{2,1,0:T(8,128)(2,1)}, bf16[4,512,1024]{2,1,0:T(8,128)(2,1)}, u32[]{:S(2)}, u32[]{:S(2)}) collective-permute-start(bf16[4,512,1024]{2,1,0:T(8,128)(2,1)} %shard_map.120), channel_id=1, source_target_pairs={{0,1},{1,0},{2,3},{3,2},{4,5},{5,4},{6,7},{7,6},{8,9},{9,8},{10,11... | collective-permute-start | bytes 12582920 | tf_op jit(solution)/shard_map/ppermute | solution.py:33
  33.6 57.1 %collective-permute-start.2 = (bf16[2,352,1024]{2,1,0:T(8,128)(2,1)}, bf16[2,352,1024]{2,1,0:T(8,128)(2,1)S(1)}, u32[]{:S(2)}, u32[]{:S(2)}) collective-permute-start(bf16[2,352,1024]{2,1,0:T(8,128)(2,1)} %get-tuple-element.63), channel_id=1, source_target_pairs={{0,2},{1,3},{2,4},{3,5},{4,6},{5,7},{6,0},{7,1},{8,10},{9,11},{10,... | collective-permute-start | bytes 4325384 | tf_op jit(solution)/shard_map/ppermute | solution.py:33
  43.8 50.8 %collective-permute-start.3 = (bf16[2,352,1024]{2,1,0:T(8,128)(2,1)}, bf16[2,352,1024]{2,1,0:T(8,128)(2,1)S(1)}, u32[]{:S(2)}, u32[]{:S(2)}) collective-permute-start(bf16[2,352,1024]{2,1,0:T(8,128)(2,1)} %get-tuple-element.64), channel_id=1, source_target_pairs={{0,6},{1,7},{2,0},{3,1},{4,2},{5,3},{6,4},{7,5},{8,14},{9,15},{10,... | collective-permute-start | bytes 4325384 | tf_op jit(solution)/shard_map/ppermute | solution.py:33
  45.8 17.6 %collective-permute-start.4 = (bf16[2,160,1024]{2,1,0:T(8,128)(2,1)}, bf16[2,160,1024]{2,1,0:T(8,128)(2,1)S(1)}, u32[]{:S(2)}, u32[]{:S(2)}) collective-permute-start(bf16[2,160,1024]{2,1,0:T(8,128)(2,1)} %get-tuple-element.65), channel_id=1, source_target_pairs={{0,8},{1,9},{2,10},{3,11},{4,12},{5,13},{6,14},{7,15},{8,0},{9,1},... | collective-permute-start | bytes 1966088 | tf_op jit(solution)/shard_map/ppermute | solution.py:33
  48.7 42.0 %collective-permute-start.5 = (bf16[2,160,1024]{2,1,0:T(8,128)(2,1)}, bf16[2,160,1024]{2,1,0:T(8,128)(2,1)S(1)}, u32[]{:S(2)}, u32[]{:S(2)}) collective-permute-start(bf16[2,160,1024]{2,1,0:T(8,128)(2,1)} %get-tuple-element.66), channel_id=1, source_target_pairs={{0,8},{1,9},{2,10},{3,11},{4,12},{5,13},{6,14},{7,15},{8,0},{9,1},... | collective-permute-start | bytes 1966088 | tf_op jit(solution)/shard_map/ppermute | solution.py:33
  63.3 31.3 %copy-start.16 = (bf16[2,160,1024]{2,1,0:T(8,128)(2,1)}, bf16[2,160,1024]{2,1,0:T(8,128)(2,1)S(1)}, u32[]{:S(2)}) copy-start(bf16[2,160,1024]{2,1,0:T(8,128)(2,1)S(1)} %collective-permute-done.4.up_crossed) | copy-start | bytes 1966084
  100.8 30.7 %collective-permute-start.6 = (bf16[512,1024]{1,0:T(8,128)(2,1)}, bf16[512,1024]{1,0:T(8,128)(2,1)S(1)}, u32[]{:S(2)}, u32[]{:S(2)}) collective-permute-start(bf16[512,1024]{1,0:T(8,128)(2,1)} %get-tuple-element.73), channel_id=1, source_target_pairs={{0,2},{1,3},{2,4},{3,5},{4,6},{5,7},{6,0},{7,1},{8,10},{9,11},{10,... | collective-permute-start | bytes 3145736 | tf_op jit(solution)/shard_map/ppermute | solution.py:33
  102.1 29.4 %collective-permute-start.7 = (bf16[512,1024]{1,0:T(8,128)(2,1)}, bf16[512,1024]{1,0:T(8,128)(2,1)}, u32[]{:S(2)}, u32[]{:S(2)}) collective-permute-start(bf16[512,1024]{1,0:T(8,128)(2,1)} %get-tuple-element.74), channel_id=1, source_target_pairs={{0,6},{1,7},{2,0},{3,1},{4,2},{5,3},{6,4},{7,5},{8,14},{9,15},{10,... | collective-permute-start | bytes 3145736 | tf_op jit(solution)/shard_map/ppermute | solution.py:33
  107.6 58.6 %all-to-all-start = ((f32[8,64,1024]{2,1,0:T(8,128)}), f32[8,64,1024]{2,1,0:T(8,128)S(1)}, u32[]{:S(2)}, u32[]{:S(2)}) async-start(f32[8,64,1024]{2,1,0:T(8,128)} %bitcast.5), calls=%async_computation | async-start | bytes 4194304 | tf_op jit(solution)/shard_map/all_to_all | solution.py:43
  136.6 26.5 %copy-start.11 = (bf16[512,1024]{1,0:T(8,128)(2,1)S(1)}, bf16[512,1024]{1,0:T(8,128)(2,1)}, u32[]{:S(2)}) copy-start(bf16[512,1024]{1,0:T(8,128)(2,1)} %copy-done.10) | copy-start | bytes 3145732
  136.6 26.5 %copy-start.13 = (bf16[2,352,1024]{2,1,0:T(8,128)(2,1)S(1)}, bf16[2,352,1024]{2,1,0:T(8,128)(2,1)}, u32[]{:S(2)}) copy-start(bf16[2,352,1024]{2,1,0:T(8,128)(2,1)} %copy-done.12) | copy-start | bytes 4325380
  136.6 26.5 %copy-start.15 = (bf16[352,1024]{1,0:T(8,128)(2,1)S(1)}, bf16[352,1024]{1,0:T(8,128)(2,1)}, u32[]{:S(2)}) copy-start(bf16[352,1024]{1,0:T(8,128)(2,1)} %get-tuple-element.76) | copy-start | bytes 2162692
  136.6 24.0 %collective-permute-start.8 = (bf16[352,1024]{1,0:T(8,128)(2,1)}, bf16[352,1024]{1,0:T(8,128)(2,1)S(1)}, u32[]{:S(2)}, u32[]{:S(2)}) collective-permute-start(bf16[352,1024]{1,0:T(8,128)(2,1)} %get-tuple-element.83), channel_id=1, source_target_pairs={{0,8},{1,9},{2,10},{3,11},{4,12},{5,13},{6,14},{7,15},{8,0},{9,1},... | collective-permute-start | bytes 2162696 | tf_op jit(solution)/shard_map/ppermute | solution.py:33
  136.7 4.8 %collective-permute-start.10 = (bf16[80,1024]{1,0:T(8,128)(2,1)}, bf16[80,1024]{1,0:T(8,128)(2,1)S(1)}, u32[]{:S(2)}, u32[]{:S(2)}) collective-permute-start(bf16[80,1024]{1,0:T(8,128)(2,1)} %get-tuple-element.85), channel_id=1, source_target_pairs={{0,6},{1,7},{2,0},{3,1},{4,2},{5,3},{6,4},{7,5},{8,14},{9,15},{10,... | collective-permute-start | bytes 491528 | tf_op jit(solution)/shard_map/ppermute | solution.py:33
  137.5 6.0 %collective-permute-start.9 = (bf16[80,1024]{1,0:T(8,128)(2,1)}, bf16[80,1024]{1,0:T(8,128)(2,1)S(1)}, u32[]{:S(2)}, u32[]{:S(2)}) collective-permute-start(bf16[80,1024]{1,0:T(8,128)(2,1)} %get-tuple-element.84), channel_id=1, source_target_pairs={{0,2},{1,3},{2,4},{3,5},{4,6},{5,7},{6,0},{7,1},{8,10},{9,11},{10,... | collective-permute-start | bytes 491528 | tf_op jit(solution)/shard_map/ppermute | solution.py:33
  166.2 21.4 %all-to-all-start.1 = ((bf16[8,64,1024]{2,1,0:T(8,128)(2,1)}), bf16[8,64,1024]{2,1,0:T(8,128)(2,1)S(1)}, u32[]{:S(2)}, u32[]{:S(2)}) async-start(bf16[8,64,1024]{2,1,0:T(8,128)(2,1)} %bitcast.7), calls=%async_computation.1 | async-start | bytes 2097152 | tf_op jit(solution)/shard_map/all_to_all | solution.py:43
  171.7 121.2 %all-gather.5.cloned.1.call-start = ((), (), s32[]{:S(2)}) async-start(), calls=%async_computation.8 | async-start | bytes 2359296 | tf_op jit(solution)/shard_map/all_gather | solution.py:424
  171.9 15.9 %copy-start.18 = (f32[1024,64]{0,1:T(8,128)S(1)}, f32[1024,64]{0,1:T(8,128)}, u32[]{:S(2)}) copy-start(f32[1024,64]{0,1:T(8,128)} %param.14) | copy-start | bytes 786436
  189.8 22.1 %all-to-all-start.2 = ((f32[128,8,128]{2,1,0:T(8,128)}), f32[128,8,128]{2,1,0:T(8,128)S(1)}, u32[]{:S(2)}, u32[]{:S(2)}) async-start(f32[128,8,128]{2,1,0:T(8,128)} %bitcast.8), calls=%async_computation.2 | async-start | bytes 1048576 | tf_op jit(solution)/shard_map/all_to_all | solution.py:43
  212.9 21.9 %all-to-all-start.3 = ((f32[128,8,128]{2,1,0:T(8,128)}), f32[128,8,128]{2,1,0:T(8,128)S(1)}, u32[]{:S(2)}, u32[]{:S(2)}) async-start(f32[128,8,128]{2,1,0:T(8,128)} %broadcast_in_dim.38), calls=%async_computation.3 | async-start | bytes 1048576 | tf_op jit(solution)/shard_map/all_to_all | solution.py:50
  262.3 18.3 %all-to-all-start.5 = ((f32[128,8,128]{2,1,0:T(8,128)}), f32[128,8,128]{2,1,0:T(8,128)S(1)}, u32[]{:S(2)}, u32[]{:S(2)}) async-start(f32[128,8,128]{2,1,0:T(8,128)} %broadcast_in_dim.39), calls=%async_computation.5 | async-start | bytes 1048576 | tf_op jit(solution)/shard_map/all_to_all | solution.py:50
  281.5 11.5 %all-to-all-start.6 = ((f32[8,64,128]{2,1,0:T(8,128)}), f32[8,64,128]{2,1,0:T(8,128)S(1)}, u32[]{:S(2)}, u32[]{:S(2)}) async-start(f32[8,64,128]{2,1,0:T(8,128)} %broadcast_in_dim.41), calls=%async_computation.6 | async-start | bytes 524288 | tf_op jit(solution)/shard_map/all_to_all | solution.py:50
  (14 other events, 41.4 us)
Sparse Core Ops, SparseCore 0:
  10.5 153.8 all-gather.2
  187.9 52.3 all-gather.4
